TPU v7x, 32 devices: a whole 2x2x4 slice. The times are simulated.
32 devices in a mesh: wide: 8 (over z, y), narrow: 4 (over x, core).
Axes of the slice: x: 2, y: 2, z: 4, core: 2. Of those that a mesh axis runs over, the one named last changes fastest.
Arguments:
- trace_guess: float32 [8, 4, 16, 128, 128], P('wide', 'narrow'), may hold values from -6 to 6
- trace_rhs: float32 [8, 4, 16, 128, 128], P('wide', 'narrow'), may hold values from -6 to 6
- block_inverse: bfloat16 [8, 4, 16, 128, 128], P('wide', 'narrow')
- coupling: bfloat16 [8, 4, 16, 2, 128, 128], P('wide', 'narrow'), may hold values from -0.1875 to 0.1875
- block_neighbours: int32 [8, 4, 16, 2], P('wide', 'narrow'), may hold values from 0 to 23
- block_send: int32 [8, 4, 4, 2], P('wide', 'narrow'), may hold values from 0 to 15
- cell_faces: int32 [8, 4, 6, 2048], P('wide', 'narrow'), may hold values from 0 to 3071
- face_coeff: float32 [8, 4, 6, 2048], P('wide', 'narrow'), may hold values from 0.2 to 2
- cell_source: float32 [8, 4, 2048], P('wide', 'narrow'), may hold values from -6 to 6
- cell_neighbours: int32 [8, 4, 6, 2048], P('wide', 'narrow'), may hold values from 0 to 3071, as said below
- upwind_flags: int32 [8, 4, 6, 2048], P('wide', 'narrow'), may hold values 0 or 1
- cell_send: int32 [8, 4, 4, 256], P('wide', 'narrow'), may hold values from 0 to 2047
- saturation: float32 [8, 4, 4, 2048], P('wide', 'narrow'), may hold values from -3 to 3
- step_ratio: float32 [8, 4, 2048], P('wide', 'narrow'), may hold values from 0.05 to 0.2
Outputs:
- traces: float32 [8, 4, 16, 128, 128], P('wide', 'narrow')
- saturation_next: float32 [8, 4, 4, 2048], P('wide', 'narrow')
Inputs may be any that keep to these rules, and one draw needn't show every extreme that they name: `cell_neighbours`: faces 0 to 3 (f) index either an own cell (below 2048) or a cell of their own side's range, 2048 + f * 256 to 2048 + (f + 1) * 256 - 1; faces 4 and 5 index own cells only.
All inputs are finite; a program needn't handle non-finite values. No bound on the sum of `upwind_flags` on one device may be relied on, other than what follows from the above.
Results may differ from a plain program's by a relative error of at most 0.003.
Values may be sent and summed in bfloat16 or wider, within the bound.
No kernel may reach another device: no remote copies, remote signals or barrier semaphores. Data moves between devices by JAX's collectives and lax.ppermute only.
A program may use at most 64 MiB of HBM per device.

v0:
```python
import jax
import jax.numpy as jnp
from jax import lax
from jax.sharding import PartitionSpec as P

lane_width = 128


def with_halo(block, sides, width):
    for axis, dim in sides:
        count = lax.axis_size(axis)
        forward = [(i, i + 1) for i in range(count - 1)]
        backward = [(target, source) for source, target in forward]
        low = lax.ppermute(
            lax.slice_in_dim(block, block.shape[dim] - width, None, axis=dim), axis, forward
        )
        high = lax.ppermute(lax.slice_in_dim(block, 0, width, axis=dim), axis, backward)
        block = jnp.concatenate([low, block, high], axis=dim)
    return block


def pick_blocks(table, index):
    count = table.shape[0]
    flat = table.reshape(count, -1)
    chooser = index.reshape(-1, 1) == lax.broadcasted_iota(jnp.int32, (1, count), 1)
    chosen = jnp.dot(chooser.astype(jnp.bfloat16), flat, preferred_element_type=jnp.float32).astype(
        jnp.bfloat16
    )
    return chosen.reshape(index.shape + table.shape[1:])


def lookup(values, index):
    modes, length = values.shape
    padded_len = -(-length // lane_width) * lane_width
    groups = padded_len // lane_width
    table = values.reshape(modes, groups, lane_width)
    high_part = index // lane_width
    low_part = index - high_part * lane_width
    high_hot = (high_part[:, None] == lax.broadcasted_iota(jnp.int32, (1, groups), 1)).astype(
        jnp.float32
    )
    low_hot = (low_part[:, None] == lax.broadcasted_iota(jnp.int32, (1, lane_width), 1)).astype(
        jnp.float32
    )
    lanes = jnp.einsum(
        "nh,mhl->mnl",
        high_hot,
        table,
        precision=lax.Precision.HIGHEST,
        preferred_element_type=jnp.float32,
    )
    return jnp.sum(lanes * low_hot[None], -1)


def trade_blocks(pieces):
    along_wide = with_halo(pieces[0:2], (("wide", 0),), 1)
    along_narrow = with_halo(pieces[2:4], (("narrow", 0),), 1)
    return jnp.concatenate(
        [along_wide[0:1], along_wide[3:4], along_narrow[0:1], along_narrow[3:4]], 0
    )


def trade_cells(pieces):
    along_wide = with_halo(pieces[0:2], (("wide", 0),), 1)
    along_narrow = with_halo(pieces[2:4], (("narrow", 0),), 1)
    return jnp.concatenate(
        [along_wide[0:1], along_wide[3:4], along_narrow[0:1], along_narrow[3:4]], 0
    )


def smooth(extended, inverse, couple, links, rhs):
    near = pick_blocks(extended, links)
    coupled = jnp.einsum("bkij,bkrj->bri", couple, near, preferred_element_type=jnp.float32)
    resid = (rhs - coupled).astype(jnp.bfloat16)
    return jnp.einsum("bij,brj->bri", inverse, resid, preferred_element_type=jnp.float32)


def per_device(
    trace_guess,
    trace_rhs,
    block_inverse,
    coupling,
    block_neighbours,
    block_send,
    cell_faces,
    face_coeff,
    cell_source,
    cell_neighbours,
    upwind_flags,
    cell_send,
    saturation,
    step_ratio,
):
    guess = trace_guess[0, 0]
    rhs = trace_rhs[0, 0]
    inverse = block_inverse[0, 0]
    couple = coupling[0, 0]
    links = block_neighbours[0, 0]
    sends = block_send[0, 0].reshape(-1)
    blocks, columns, faces = guess.shape
    current = guess.astype(jnp.bfloat16)
    outgoing = pick_blocks(current, sends)
    fresh = guess
    for sweep in range(2):
        arrived = trade_blocks(outgoing.reshape((4, -1) + outgoing.shape[1:]))
        extended = jnp.concatenate([current, arrived.reshape((-1,) + current.shape[1:])], 0)
        fresh = smooth(extended, inverse, couple, links, rhs)
        current = fresh.astype(jnp.bfloat16)
        edge = pick_blocks(current, sends)
        outgoing = edge if sweep == 0 else edge[:, 0:1, :]
    arrived = trade_blocks(outgoing.reshape(4, -1, 1, faces))
    face_values = (
        jnp.concatenate([current[:, 0, :], arrived.reshape(-1, faces)], 0)
        .reshape(1, -1)
        .astype(jnp.float32)
    )
    face_index = cell_faces[0, 0]
    face_trace = jnp.concatenate([lookup(face_values, face_index[face]) for face in range(6)], 0)
    coeff = face_coeff[0, 0]
    total = jnp.sum(coeff, 0)
    pressure = (cell_source[0, 0] + jnp.sum(coeff * face_trace, 0)) / total
    flux = coeff * (pressure[None, :] - face_trace)
    modes_now = saturation[0, 0]
    outbound = cell_send[0, 0]
    neighbours = cell_neighbours[0, 0]
    flags = upwind_flags[0, 0]
    ratio = step_ratio[0, 0]
    sent_modes = lookup(modes_now, outbound.reshape(-1)).reshape(4, 4, -1)
    flows = []
    pieces = jnp.transpose(sent_modes, (1, 0, 2))
    arrived_cells = trade_cells(pieces)
    ext_modes = jnp.concatenate(
        [modes_now, jnp.transpose(arrived_cells, (1, 0, 2)).reshape(4, -1)], 1
    )
    for face in range(6):
        axis_mode = face // 2 + 1
        sign = -1.0 if face % 2 == 0 else 1.0
        picked_modes = lookup(ext_modes, neighbours[face])
        across = picked_modes[0] - sign * picked_modes[axis_mode]
        own = modes_now[0] + sign * modes_now[axis_mode]
        flows.append(flux[face] * jnp.where(flags[face] == 1, own, across))
    flow = jnp.stack(flows, 0)
    result = [modes_now[0] - ratio * jnp.sum(flow, 0)]
    for axis_mode in range(1, 4):
        low, high = (2 * axis_mode - 2, 2 * axis_mode - 1)
        volume = 0.5 * (flux[high] - flux[low]) * modes_now[0]
        result.append(modes_now[axis_mode] + 3.0 * ratio * (volume - (flow[high] - flow[low])))
    return (fresh[None, None], jnp.stack(result, 0)[None, None])


def solution(mesh):
    placed = (
        P("wide", "narrow", None, None, None),
        P("wide", "narrow", None, None, None),
        P("wide", "narrow", None, None, None),
        P("wide", "narrow", None, None, None, None),
        P("wide", "narrow", None, None),
        P("wide", "narrow", None, None),
        P("wide", "narrow", None, None),
        P("wide", "narrow", None, None),
        P("wide", "narrow", None),
        P("wide", "narrow", None, None),
        P("wide", "narrow", None, None),
        P("wide", "narrow", None, None),
        P("wide", "narrow", None, None),
        P("wide", "narrow", None),
    )
    return jax.shard_map(
        per_device,
        mesh=mesh,
        in_specs=placed,
        out_specs=(P("wide", "narrow", None, None, None), P("wide", "narrow", None, None)),
        check_vma=False,
    )
```

profile of v0, /device:TPU:10, one launch (start us, length us, event | category | flops | bytes accessed | tf_op | source)
XLA Modules:
  0.0 103.8 jit_solution(8268694978029076781)
XLA Ops:
  1.6 1.3 %convert_element_type.115 = bf16[1,1,16,128,128]{4,3,2,1,0:T(8,128)(2,1)S(1)} convert(f32[1,1,16,128,128]{4,3,2,1,0:T(8,128)} %param.14) | non-fusion elementwise | flops 262144 | bytes 1572864 | tf_op jit(solution)/shard_map/convert_element_type | solution.py:101
  3.6 3.4 %collective-permute-start = (bf16[1,2,128,128]{3,2,1,0:T(8,128)(2,1)S(1)}, bf16[1,2,128,128]{3,2,1,0:T(8,128)(2,1)S(1)}, u32[]{:S(2)}, u32[]{:S(2)}) collective-permute-start(bf16[1,2,128,128]{3,2,1,0:T(8,128)(2,1)S(1)} %copy.108), channel_id=1, source_target_pairs={{0,4},{4,8},{8,12},{12,16},{16,20},{20,24},{24,28},{1,5},{5,9},{9,... | collective-permute-start | bytes 196616 | tf_op jit(solution)/shard_map/ppermute | solution.py:14
  7.1 1.1 %multiply_reduce_fusion = f32[1024,4]{0,1:T(4,128)S(1)} fusion(f32[1024,128]{0,1:T(8,128)S(1)} %fusion.54, f32[1,4,16,128]{3,1,2,0:T(4,128)S(1)} %bitcast.422, s32[1024]{0:T(1024)S(1)} %get-tuple-element.64), kind=kOutput, calls=%fused_computation.29 | convolution fusion | flops 101724160 | bytes 577536 | tf_op jit(solution)/shard_map/nh,mhl->mnl/dot_general | solution.py:45
  8.9 3.4 %collective-permute-start.12 = (f32[1,4,256]{2,0,1:T(1,128)}, f32[1,4,256]{2,0,1:T(1,128)}, u32[]{:S(2)}, u32[]{:S(2)}) collective-permute-start(f32[1,4,256]{2,0,1:T(1,128)} %get-tuple-element.36), channel_id=1, source_target_pairs={{0,4},{4,8},{8,12},{12,16},{16,20},{20,24},{24,28},{1,5},{5,9},{9,... | collective-permute-start | bytes 12296 | tf_op jit(solution)/shard_map/ppermute | solution.py:14
  12.3 3.3 %collective-permute-start.13 = (f32[1,4,256]{2,0,1:T(1,128)}, f32[1,4,256]{2,0,1:T(1,128)}, u32[]{:S(2)}, u32[]{:S(2)}) collective-permute-start(f32[1,4,256]{2,0,1:T(1,128)} %get-tuple-element.39), channel_id=1, source_target_pairs={{4,0},{8,4},{12,8},{16,12},{20,16},{24,20},{28,24},{5,1},{9,5},{13... | collective-permute-start | bytes 12296 | tf_op jit(solution)/shard_map/ppermute | solution.py:17
  15.6 1.9 %collective-permute-start.14 = (f32[1,4,256]{2,0,1:T(1,128)}, f32[1,4,256]{2,0,1:T(1,128)}, u32[]{:S(2)}, u32[]{:S(2)}) collective-permute-start(f32[1,4,256]{2,0,1:T(1,128)} %get-tuple-element.38), channel_id=1, source_target_pairs={{0,1},{1,2},{2,3},{4,5},{5,6},{6,7},{8,9},{9,10},{10,11},{12,13},{... | collective-permute-start | bytes 12296 | tf_op jit(solution)/shard_map/ppermute | solution.py:14
  17.5 3.6 %collective-permute-start.15 = (f32[1,4,256]{2,0,1:T(1,128)}, f32[1,4,256]{2,0,1:T(1,128)}, u32[]{:S(2)}, u32[]{:S(2)}) collective-permute-start(f32[1,4,256]{2,0,1:T(1,128)} %get-tuple-element.37), channel_id=1, source_target_pairs={{1,0},{2,1},{3,2},{5,4},{6,5},{7,6},{9,8},{10,9},{11,10},{13,12},{... | collective-permute-start | bytes 12296 | tf_op jit(solution)/shard_map/ppermute | solution.py:17
  25.6 1.1 %fusion.36 = f32[2048,128]{0,1:T(8,128)} fusion(s32[2048]{0:T(1024)S(1)} %get-tuple-element.43), kind=kLoop, calls=%fused_computation.73 | loop fusion | flops 524288 | bytes 1056768 | tf_op jit(solution)/shard_map/convert_element_type | solution.py:42
  27.3 1.1 %fusion.35 = f32[2048,128]{0,1:T(8,128)} fusion(s32[2048]{0:T(1024)S(1)} %get-tuple-element.45), kind=kLoop, calls=%fused_computation.72 | loop fusion | flops 524288 | bytes 1056768 | tf_op jit(solution)/shard_map/convert_element_type | solution.py:42
  29.0 1.1 %fusion.34 = f32[2048,128]{0,1:T(8,128)} fusion(s32[2048]{0:T(1024)S(1)} %get-tuple-element.47), kind=kLoop, calls=%fused_computation.71 | loop fusion | flops 524288 | bytes 1056768 | tf_op jit(solution)/shard_map/convert_element_type | solution.py:42
  32.4 1.1 %fusion.32 = f32[2048,128]{0,1:T(8,128)} fusion(s32[2048]{0:T(1024)S(1)} %get-tuple-element.63), kind=kLoop, calls=%fused_computation.69 | loop fusion | flops 524288 | bytes 1056768 | tf_op jit(solution)/shard_map/convert_element_type | solution.py:42
  35.5 3.0 %collective-permute-start.1 = (bf16[1,2,128,128]{3,2,1,0:T(8,128)(2,1)S(1)}, bf16[1,2,128,128]{3,2,1,0:T(8,128)(2,1)S(1)}, u32[]{:S(2)}, u32[]{:S(2)}) collective-permute-start(bf16[1,2,128,128]{3,2,1,0:T(8,128)(2,1)S(1)} %copy.107), channel_id=1, source_target_pairs={{4,0},{8,4},{12,8},{16,12},{20,16},{24,20},{28,24},{5,1},{9,5},{13... | collective-permute-start | bytes 196616 | tf_op jit(solution)/shard_map/ppermute | solution.py:17
  38.5 1.9 %collective-permute-start.2 = (bf16[1,2,128,128]{3,2,1,0:T(8,128)(2,1)S(1)}, bf16[1,2,128,128]{3,2,1,0:T(8,128)(2,1)S(1)}, u32[]{:S(2)}, u32[]{:S(2)}) collective-permute-start(bf16[1,2,128,128]{3,2,1,0:T(8,128)(2,1)S(1)} %copy.106), channel_id=1, source_target_pairs={{0,1},{1,2},{2,3},{4,5},{5,6},{6,7},{8,9},{9,10},{10,11},{12,13},{... | collective-permute-start | bytes 196616 | tf_op jit(solution)/shard_map/ppermute | solution.py:14
  40.4 3.8 %collective-permute-start.3 = (bf16[1,2,128,128]{3,2,1,0:T(8,128)(2,1)S(1)}, bf16[1,2,128,128]{3,2,1,0:T(8,128)(2,1)S(1)}, u32[]{:S(2)}, u32[]{:S(2)}) collective-permute-start(bf16[1,2,128,128]{3,2,1,0:T(8,128)(2,1)S(1)} %copy.105), channel_id=1, source_target_pairs={{1,0},{2,1},{3,2},{5,4},{6,5},{7,6},{9,8},{10,9},{11,10},{13,12},{... | collective-permute-start | bytes 196616 | tf_op jit(solution)/shard_map/ppermute | solution.py:17
  45.0 3.4 %fusion = f32[4,2048]{1,0:T(4,128)} fusion(f32[2048,128]{0,1:T(8,128)S(1)} %fusion.37, s32[2048]{0:T(1024)} %get-tuple-element.40, f32[1,4,24,128]{3,1,2,0:T(4,128)S(1)} %maximum_bitcast_fusion), kind=kOutput, calls=%fused_computation.6 | convolution fusion | flops 304128000 | bytes 1138688 | tf_op jit(solution)/shard_map/nh,mhl->mnl/dot_general | solution.py:45
  48.4 2.7 %fusion.1 = f32[4,2048]{1,0:T(4,128)} fusion(f32[2048,128]{0,1:T(8,128)S(1)} %copy-done.4, s32[2048]{0:T(1024)S(1)} %copy-done.33, f32[1,4,24,128]{3,1,2,0:T(4,128)S(1)} %maximum_bitcast_fusion), kind=kOutput, calls=%fused_computation.8 | convolution fusion | flops 304128000 | bytes 1138688 | tf_op jit(solution)/shard_map/nh,mhl->mnl/dot_general | solution.py:45
  51.1 2.7 %fusion.2 = f32[4,2048]{1,0:T(4,128)} fusion(f32[2048,128]{0,1:T(8,128)S(1)} %copy-done.5, s32[2048]{0:T(1024)S(1)} %copy-done.34, f32[1,4,24,128]{3,1,2,0:T(4,128)S(1)} %maximum_bitcast_fusion), kind=kOutput, calls=%fused_computation.10 | convolution fusion | flops 304128000 | bytes 1138688 | tf_op jit(solution)/shard_map/nh,mhl->mnl/dot_general | solution.py:45
  53.8 2.7 %fusion.3 = f32[4,2048]{1,0:T(4,128)} fusion(f32[2048,128]{0,1:T(8,128)S(1)} %copy-done.6, s32[2048]{0:T(1024)S(1)} %copy-done.35, f32[1,4,24,128]{3,1,2,0:T(4,128)S(1)} %maximum_bitcast_fusion), kind=kOutput, calls=%fused_computation.12 | convolution fusion | flops 304128000 | bytes 1138688 | tf_op jit(solution)/shard_map/nh,mhl->mnl/dot_general | solution.py:45
  57.2 1.2 %copy.33 = bf16[4,8,128,128]{3,2,1,0:T(8,128)(2,1)} copy(bf16[4,8,128,128]{3,1,2,0:T(8,128)(2,1)S(1)} %fusion.12) | data formatting | bytes 2097152
  59.0 2.0 %convolution_convert_fusion.5 = bf16[16,128,128]{2,1,0:T(8,128)(2,1)S(1)} fusion(bf16[16,2,128,128]{3,2,1,0:T(8,128)(2,1)} %bitcast.413, bf16[1,1,16,2,128,128]{5,4,3,2,1,0:T(8,128)(2,1)S(1)} %copy-done, f32[1,1,16,128,128]{4,3,2,1,0:T(8,128)S(1)} %copy-done.1, bf16[1,1,16,128,128]{4,3,2,1,0:T(8,128)(2,1)S(1)} %copy-done.2), kind=kOutput, calls=%fused_computation.38 | convolution fusion | flops 202113024 | bytes 4194304 | tf_op jit(solution)/shard_map/bij,brj->bri/dot_general | solution.py:75
  61.6 2.9 %collective-permute-start.4 = (bf16[1,2,128,128]{3,2,1,0:T(8,128)(2,1)S(1)}, bf16[1,2,128,128]{3,2,1,0:T(8,128)(2,1)S(1)}, u32[]{:S(2)}, u32[]{:S(2)}) collective-permute-start(bf16[1,2,128,128]{3,2,1,0:T(8,128)(2,1)S(1)} %copy.104), channel_id=1, source_target_pairs={{0,4},{4,8},{8,12},{12,16},{16,20},{20,24},{24,28},{1,5},{5,9},{9,... | collective-permute-start | bytes 196616 | tf_op jit(solution)/shard_map/ppermute | solution.py:14
  64.5 3.9 %collective-permute-start.5 = (bf16[1,2,128,128]{3,2,1,0:T(8,128)(2,1)S(1)}, bf16[1,2,128,128]{3,2,1,0:T(8,128)(2,1)S(1)}, u32[]{:S(2)}, u32[]{:S(2)}) collective-permute-start(bf16[1,2,128,128]{3,2,1,0:T(8,128)(2,1)S(1)} %copy.103), channel_id=1, source_target_pairs={{4,0},{8,4},{12,8},{16,12},{20,16},{24,20},{28,24},{5,1},{9,5},{13... | collective-permute-start | bytes 196616 | tf_op jit(solution)/shard_map/ppermute | solution.py:17
  68.4 1.9 %collective-permute-start.6 = (bf16[1,2,128,128]{3,2,1,0:T(8,128)(2,1)S(1)}, bf16[1,2,128,128]{3,2,1,0:T(8,128)(2,1)S(1)}, u32[]{:S(2)}, u32[]{:S(2)}) collective-permute-start(bf16[1,2,128,128]{3,2,1,0:T(8,128)(2,1)S(1)} %copy.102), channel_id=1, source_target_pairs={{0,1},{1,2},{2,3},{4,5},{5,6},{6,7},{8,9},{9,10},{10,11},{12,13},{... | collective-permute-start | bytes 196616 | tf_op jit(solution)/shard_map/ppermute | solution.py:14
  70.4 3.9 %collective-permute-start.7 = (bf16[1,2,128,128]{3,2,1,0:T(8,128)(2,1)S(1)}, bf16[1,2,128,128]{3,2,1,0:T(8,128)(2,1)S(1)}, u32[]{:S(2)}, u32[]{:S(2)}) collective-permute-start(bf16[1,2,128,128]{3,2,1,0:T(8,128)(2,1)S(1)} %copy.101), channel_id=1, source_target_pairs={{1,0},{2,1},{3,2},{5,4},{6,5},{7,6},{9,8},{10,9},{11,10},{13,12},{... | collective-permute-start | bytes 196616 | tf_op jit(solution)/shard_map/ppermute | solution.py:17
  74.3 2.1 %fusion.4 = f32[4,2048]{1,0:T(4,128)S(1)} fusion(f32[2048,128]{0,1:T(8,128)S(1)} %copy-done.3, s32[2048]{0:T(1024)S(1)} %copy-done.32, f32[1,4,24,128]{3,1,2,0:T(4,128)S(1)} %copy-done.13), kind=kOutput, calls=%fused_computation.14 | convolution fusion | flops 304128000 | bytes 1138688 | tf_op jit(solution)/shard_map/nh,mhl->mnl/dot_general | solution.py:45
  77.7 2.9 %fusion.152 = (bf16[16,128,128]{2,1,0:T(8,128)(2,1)}, f32[16,128,128]{2,1,0:T(8,128)}) fusion(bf16[1,1,16,128,128]{4,3,2,1,0:T(8,128)(2,1)} %param.16, bf16[16,2,128,128]{3,2,1,0:T(8,128)(2,1)S(1)} %bitcast.412, bf16[1,1,16,2,128,128]{5,4,3,2,1,0:T(8,128)(2,1)S(1)} %copy-done, f32[1,1,16,128,128]{4,3,2,1,0:T(8,128)S(1)} %copy-done.1), kind=kOutput, calls=%fused_computation.325 | convolution fusion | flops 202113024 | bytes 5242880 | tf_op jit(solution)/shard_map/bij,brj->bri/dot_general | solution.py:75
  80.7 1.4 %fusion.25 = bf16[8,128,128]{2,0,1:T(8,128)(2,1)S(1)} fusion(bf16[2,8,128,128]{3,2,1,0:T(8,128)(2,1)} %bitcast.414, s32[8]{0:T(128)S(1)} %copy-done.38), kind=kOutput, calls=%fused_computation.46 | convolution fusion | flops 4325504 | bytes 786464 | tf_op jit(solution)/shard_map/dot_general | solution.py:26
  82.2 1.9 %collective-permute-start.10 = (bf16[1,2,1,128]{3,1,2,0:T(2,128)(2,1)S(1)}, bf16[1,2,1,128]{3,1,2,0:T(2,128)(2,1)S(1)}, u32[]{:S(2)}, u32[]{:S(2)}) collective-permute-start(bf16[1,2,1,128]{3,1,2,0:T(2,128)(2,1)S(1)} %get-tuple-element.11), channel_id=1, source_target_pairs={{0,1},{1,2},{2,3},{4,5},{5,6},{6,7},{8,9},{9,10},{10,11},{12,13},{... | collective-permute-start | bytes 1544 | tf_op jit(solution)/shard_map/ppermute | solution.py:14
  84.1 3.6 %collective-permute-start.11 = (bf16[1,2,1,128]{3,1,2,0:T(2,128)(2,1)S(1)}, bf16[1,2,1,128]{3,1,2,0:T(2,128)(2,1)S(1)}, u32[]{:S(2)}, u32[]{:S(2)}) collective-permute-start(bf16[1,2,1,128]{3,1,2,0:T(2,128)(2,1)S(1)} %get-tuple-element.10), channel_id=1, source_target_pairs={{1,0},{2,1},{3,2},{5,4},{6,5},{7,6},{9,8},{10,9},{11,10},{13,12},{... | collective-permute-start | bytes 1544 | tf_op jit(solution)/shard_map/ppermute | solution.py:17
  87.7 2.0 %collective-permute-start.8 = (bf16[1,2,1,128]{3,1,2,0:T(2,128)(2,1)S(1)}, bf16[1,2,1,128]{3,1,2,0:T(2,128)(2,1)S(1)}, u32[]{:S(2)}, u32[]{:S(2)}) collective-permute-start(bf16[1,2,1,128]{3,1,2,0:T(2,128)(2,1)S(1)} %get-tuple-element.9), channel_id=1, source_target_pairs={{0,4},{4,8},{8,12},{12,16},{16,20},{20,24},{24,28},{1,5},{5,9},{9,... | collective-permute-start | bytes 1544 | tf_op jit(solution)/shard_map/ppermute | solution.py:14
  89.7 4.8 %collective-permute-start.9 = (bf16[1,2,1,128]{3,1,2,0:T(2,128)(2,1)S(1)}, bf16[1,2,1,128]{3,1,2,0:T(2,128)(2,1)S(1)}, u32[]{:S(2)}, u32[]{:S(2)}) collective-permute-start(bf16[1,2,1,128]{3,1,2,0:T(2,128)(2,1)S(1)} %get-tuple-element.12), channel_id=1, source_target_pairs={{4,0},{8,4},{12,8},{16,12},{20,16},{24,20},{28,24},{5,1},{9,5},{13... | collective-permute-start | bytes 1544 | tf_op jit(solution)/shard_map/ppermute | solution.py:17
  94.5 3.2 %fusion.5 = f32[4,2048]{1,0:T(4,128)S(1)} fusion(f32[2048,128]{0,1:T(8,128)} %fusion.32, s32[2048]{0:T(1024)S(1)} %copy-done.31, f32[1,4,24,128]{3,1,2,0:T(4,128)S(1)} %copy-done.13), kind=kOutput, calls=%fused_computation.16 | convolution fusion | flops 304128000 | bytes 1138688 | tf_op jit(solution)/shard_map/nh,mhl->mnl/dot_general | solution.py:45
  (167 shorter events, 21.7 us)
Async XLA Ops:
  0.6 57.8 %copy-start = (bf16[1,1,16,2,128,128]{5,4,3,2,1,0:T(8,128)(2,1)S(1)}, bf16[1,1,16,2,128,128]{5,4,3,2,1,0:T(8,128)(2,1)}, u32[]{:S(2)}) copy-start(bf16[1,1,16,2,128,128]{5,4,3,2,1,0:T(8,128)(2,1)} %param.17) | copy-start | bytes 3145732
  2.9 4.1 %copy-start.41 = (s32[1,1,4,256]{3,2,1,0:T(4,128)S(1)}, s32[1,1,4,256]{3,2,1,0:T(4,128)}, u32[]{:S(2)}) copy-start(s32[1,1,4,256]{3,2,1,0:T(4,128)} %param.25) | copy-start | bytes 12292
  2.9 4.2 %copy-start.8 = (f32[1,1,4,2048]{3,2,1,0:T(4,128)S(1)}, f32[1,1,4,2048]{3,2,1,0:T(4,128)}, u32[]{:S(2)}) copy-start(f32[1,1,4,2048]{3,2,1,0:T(4,128)} %param.26) | copy-start | bytes 98308
  3.3 17.9 %copy-start.10 = (s32[1,1,6,2048]{3,1,2,0:T(1,128)S(1)}, s32[1,1,6,2048]{3,1,2,0:T(1,128)}, u32[]{:S(2)}) copy-start(s32[1,1,6,2048]{3,1,2,0:T(1,128)} %param.20) | copy-start | bytes 147460
  3.6 20.8 %copy-start.11 = (s32[1,1,6,2048]{3,1,2,0:T(1,128)S(1)}, s32[1,1,6,2048]{3,1,2,0:T(1,128)}, u32[]{:S(2)}) copy-start(s32[1,1,6,2048]{3,1,2,0:T(1,128)} %param.23) | copy-start | bytes 147460
  3.6 52.9 %collective-permute-start = (bf16[1,2,128,128]{3,2,1,0:T(8,128)(2,1)S(1)}, bf16[1,2,128,128]{3,2,1,0:T(8,128)(2,1)S(1)}, u32[]{:S(2)}, u32[]{:S(2)}) collective-permute-start(bf16[1,2,128,128]{3,2,1,0:T(8,128)(2,1)S(1)} %copy.108), channel_id=1, source_target_pairs={{0,4},{4,8},{8,12},{12,16},{16,20},{20,24},{24,28},{1,5},{5,9},{9,... | collective-permute-start | bytes 196616 | tf_op jit(solution)/shard_map/ppermute | solution.py:14
  8.9 26.6 %collective-permute-start.12 = (f32[1,4,256]{2,0,1:T(1,128)}, f32[1,4,256]{2,0,1:T(1,128)}, u32[]{:S(2)}, u32[]{:S(2)}) collective-permute-start(f32[1,4,256]{2,0,1:T(1,128)} %get-tuple-element.36), channel_id=1, source_target_pairs={{0,4},{4,8},{8,12},{12,16},{16,20},{20,24},{24,28},{1,5},{5,9},{9,... | collective-permute-start | bytes 12296 | tf_op jit(solution)/shard_map/ppermute | solution.py:14
  12.3 26.2 %collective-permute-start.13 = (f32[1,4,256]{2,0,1:T(1,128)}, f32[1,4,256]{2,0,1:T(1,128)}, u32[]{:S(2)}, u32[]{:S(2)}) collective-permute-start(f32[1,4,256]{2,0,1:T(1,128)} %get-tuple-element.39), channel_id=1, source_target_pairs={{4,0},{8,4},{12,8},{16,12},{20,16},{24,20},{28,24},{5,1},{9,5},{13... | collective-permute-start | bytes 12296 | tf_op jit(solution)/shard_map/ppermute | solution.py:17
  15.6 24.8 %collective-permute-start.14 = (f32[1,4,256]{2,0,1:T(1,128)}, f32[1,4,256]{2,0,1:T(1,128)}, u32[]{:S(2)}, u32[]{:S(2)}) collective-permute-start(f32[1,4,256]{2,0,1:T(1,128)} %get-tuple-element.38), channel_id=1, source_target_pairs={{0,1},{1,2},{2,3},{4,5},{5,6},{6,7},{8,9},{9,10},{10,11},{12,13},{... | collective-permute-start | bytes 12296 | tf_op jit(solution)/shard_map/ppermute | solution.py:14
  17.5 26.7 %collective-permute-start.15 = (f32[1,4,256]{2,0,1:T(1,128)}, f32[1,4,256]{2,0,1:T(1,128)}, u32[]{:S(2)}, u32[]{:S(2)}) collective-permute-start(f32[1,4,256]{2,0,1:T(1,128)} %get-tuple-element.37), channel_id=1, source_target_pairs={{1,0},{2,1},{3,2},{5,4},{6,5},{7,6},{9,8},{10,9},{11,10},{13,12},{... | collective-permute-start | bytes 12296 | tf_op jit(solution)/shard_map/ppermute | solution.py:17
  32.4 3.0 %copy-start.7 = (f32[1,1,6,2048]{3,1,2,0:T(1,128)S(1)}, f32[1,1,6,2048]{3,1,2,0:T(1,128)}, u32[]{:S(2)}) copy-start(f32[1,1,6,2048]{3,1,2,0:T(1,128)} %param.21) | copy-start | bytes 147460
  35.4 21.3 %copy-start.39 = (s32[32]{0:T(128)}, s32[32]{0:T(128)S(1)}, u32[]{:S(2)}) copy-start(s32[32]{0:T(128)S(1)} %eq.543) | copy-start | bytes 388
  35.5 21.0 %collective-permute-start.1 = (bf16[1,2,128,128]{3,2,1,0:T(8,128)(2,1)S(1)}, bf16[1,2,128,128]{3,2,1,0:T(8,128)(2,1)S(1)}, u32[]{:S(2)}, u32[]{:S(2)}) collective-permute-start(bf16[1,2,128,128]{3,2,1,0:T(8,128)(2,1)S(1)} %copy.107), channel_id=1, source_target_pairs={{4,0},{8,4},{12,8},{16,12},{20,16},{24,20},{28,24},{5,1},{9,5},{13... | collective-permute-start | bytes 196616 | tf_op jit(solution)/shard_map/ppermute | solution.py:17
  38.5 18.0 %collective-permute-start.2 = (bf16[1,2,128,128]{3,2,1,0:T(8,128)(2,1)S(1)}, bf16[1,2,128,128]{3,2,1,0:T(8,128)(2,1)S(1)}, u32[]{:S(2)}, u32[]{:S(2)}) collective-permute-start(bf16[1,2,128,128]{3,2,1,0:T(8,128)(2,1)S(1)} %copy.106), channel_id=1, source_target_pairs={{0,1},{1,2},{2,3},{4,5},{5,6},{6,7},{8,9},{9,10},{10,11},{12,13},{... | collective-permute-start | bytes 196616 | tf_op jit(solution)/shard_map/ppermute | solution.py:14
  40.4 16.1 %collective-permute-start.3 = (bf16[1,2,128,128]{3,2,1,0:T(8,128)(2,1)S(1)}, bf16[1,2,128,128]{3,2,1,0:T(8,128)(2,1)S(1)}, u32[]{:S(2)}, u32[]{:S(2)}) collective-permute-start(bf16[1,2,128,128]{3,2,1,0:T(8,128)(2,1)S(1)} %copy.105), channel_id=1, source_target_pairs={{1,0},{2,1},{3,2},{5,4},{6,5},{7,6},{9,8},{10,9},{11,10},{13,12},{... | collective-permute-start | bytes 196616 | tf_op jit(solution)/shard_map/ppermute | solution.py:17
  45.0 8.8 %copy-start.12 = (f32[1,4,24,128]{3,1,2,0:T(4,128)}, f32[1,4,24,128]{3,1,2,0:T(4,128)S(1)}, u32[]{:S(2)}) copy-start(f32[1,4,24,128]{3,1,2,0:T(4,128)S(1)} %maximum_bitcast_fusion) | copy-start | bytes 147460
  45.0 3.4 %copy-start.4 = (f32[2048,128]{0,1:T(8,128)S(1)}, f32[2048,128]{0,1:T(8,128)}, u32[]{:S(2)}) copy-start(f32[2048,128]{0,1:T(8,128)} %fusion.36) | copy-start | bytes 3145732
  45.0 3.4 %copy-start.33 = (s32[2048]{0:T(1024)S(1)}, s32[2048]{0:T(1024)}, u32[]{:S(2)}) copy-start(s32[2048]{0:T(1024)} %get-tuple-element.42) | copy-start | bytes 24580
  61.0 13.3 %copy-start.3 = (f32[2048,128]{0,1:T(8,128)S(1)}, f32[2048,128]{0,1:T(8,128)}, u32[]{:S(2)}) copy-start(f32[2048,128]{0,1:T(8,128)} %fusion.33) | copy-start | bytes 3145732
  61.0 13.3 %copy-start.13 = (f32[1,4,24,128]{3,1,2,0:T(4,128)S(1)}, f32[1,4,24,128]{3,1,2,0:T(4,128)}, u32[]{:S(2)}) copy-start(f32[1,4,24,128]{3,1,2,0:T(4,128)} %copy-done.12) | copy-start | bytes 147460
  61.0 13.3 %copy-start.32 = (s32[2048]{0:T(1024)S(1)}, s32[2048]{0:T(1024)}, u32[]{:S(2)}) copy-start(s32[2048]{0:T(1024)} %get-tuple-element.48) | copy-start | bytes 24580
  61.6 15.1 %collective-permute-start.4 = (bf16[1,2,128,128]{3,2,1,0:T(8,128)(2,1)S(1)}, bf16[1,2,128,128]{3,2,1,0:T(8,128)(2,1)S(1)}, u32[]{:S(2)}, u32[]{:S(2)}) collective-permute-start(bf16[1,2,128,128]{3,2,1,0:T(8,128)(2,1)S(1)} %copy.104), channel_id=1, source_target_pairs={{0,4},{4,8},{8,12},{12,16},{16,20},{20,24},{24,28},{1,5},{5,9},{9,... | collective-permute-start | bytes 196616 | tf_op jit(solution)/shard_map/ppermute | solution.py:14
  64.5 12.2 %collective-permute-start.5 = (bf16[1,2,128,128]{3,2,1,0:T(8,128)(2,1)S(1)}, bf16[1,2,128,128]{3,2,1,0:T(8,128)(2,1)S(1)}, u32[]{:S(2)}, u32[]{:S(2)}) collective-permute-start(bf16[1,2,128,128]{3,2,1,0:T(8,128)(2,1)S(1)} %copy.103), channel_id=1, source_target_pairs={{4,0},{8,4},{12,8},{16,12},{20,16},{24,20},{28,24},{5,1},{9,5},{13... | collective-permute-start | bytes 196616 | tf_op jit(solution)/shard_map/ppermute | solution.py:17
  68.4 8.3 %collective-permute-start.6 = (bf16[1,2,128,128]{3,2,1,0:T(8,128)(2,1)S(1)}, bf16[1,2,128,128]{3,2,1,0:T(8,128)(2,1)S(1)}, u32[]{:S(2)}, u32[]{:S(2)}) collective-permute-start(bf16[1,2,128,128]{3,2,1,0:T(8,128)(2,1)S(1)} %copy.102), channel_id=1, source_target_pairs={{0,1},{1,2},{2,3},{4,5},{5,6},{6,7},{8,9},{9,10},{10,11},{12,13},{... | collective-permute-start | bytes 196616 | tf_op jit(solution)/shard_map/ppermute | solution.py:14
  70.4 6.4 %collective-permute-start.7 = (bf16[1,2,128,128]{3,2,1,0:T(8,128)(2,1)S(1)}, bf16[1,2,128,128]{3,2,1,0:T(8,128)(2,1)S(1)}, u32[]{:S(2)}, u32[]{:S(2)}) collective-permute-start(bf16[1,2,128,128]{3,2,1,0:T(8,128)(2,1)S(1)} %copy.101), channel_id=1, source_target_pairs={{1,0},{2,1},{3,2},{5,4},{6,5},{7,6},{9,8},{10,9},{11,10},{13,12},{... | collective-permute-start | bytes 196616 | tf_op jit(solution)/shard_map/ppermute | solution.py:17
  77.7 16.8 %copy-start.31 = (s32[2048]{0:T(1024)S(1)}, s32[2048]{0:T(1024)}, u32[]{:S(2)}) copy-start(s32[2048]{0:T(1024)} %get-tuple-element.62) | copy-start | bytes 24580
  82.1 16.5 %copy-start.19 = (s32[2048]{0:T(1024)S(1)}, s32[2048]{0:T(1024)}, u32[]{:S(2)}) copy-start(s32[2048]{0:T(1024)} %get-tuple-element.50) | copy-start | bytes 24580
  82.1 16.5 %copy-start.20 = (s32[2048]{0:T(1024)S(1)}, s32[2048]{0:T(1024)}, u32[]{:S(2)}) copy-start(s32[2048]{0:T(1024)} %get-tuple-element.51) | copy-start | bytes 24580
  82.2 16.4 %collective-permute-start.10 = (bf16[1,2,1,128]{3,1,2,0:T(2,128)(2,1)S(1)}, bf16[1,2,1,128]{3,1,2,0:T(2,128)(2,1)S(1)}, u32[]{:S(2)}, u32[]{:S(2)}) collective-permute-start(bf16[1,2,1,128]{3,1,2,0:T(2,128)(2,1)S(1)} %get-tuple-element.11), channel_id=1, source_target_pairs={{0,1},{1,2},{2,3},{4,5},{5,6},{6,7},{8,9},{9,10},{10,11},{12,13},{... | collective-permute-start | bytes 1544 | tf_op jit(solution)/shard_map/ppermute | solution.py:14
  84.1 14.4 %collective-permute-start.11 = (bf16[1,2,1,128]{3,1,2,0:T(2,128)(2,1)S(1)}, bf16[1,2,1,128]{3,1,2,0:T(2,128)(2,1)S(1)}, u32[]{:S(2)}, u32[]{:S(2)}) collective-permute-start(bf16[1,2,1,128]{3,1,2,0:T(2,128)(2,1)S(1)} %get-tuple-element.10), channel_id=1, source_target_pairs={{1,0},{2,1},{3,2},{5,4},{6,5},{7,6},{9,8},{10,9},{11,10},{13,12},{... | collective-permute-start | bytes 1544 | tf_op jit(solution)/shard_map/ppermute | solution.py:17
  87.7 10.8 %collective-permute-start.8 = (bf16[1,2,1,128]{3,1,2,0:T(2,128)(2,1)S(1)}, bf16[1,2,1,128]{3,1,2,0:T(2,128)(2,1)S(1)}, u32[]{:S(2)}, u32[]{:S(2)}) collective-permute-start(bf16[1,2,1,128]{3,1,2,0:T(2,128)(2,1)S(1)} %get-tuple-element.9), channel_id=1, source_target_pairs={{0,4},{4,8},{8,12},{12,16},{16,20},{20,24},{24,28},{1,5},{5,9},{9,... | collective-permute-start | bytes 1544 | tf_op jit(solution)/shard_map/ppermute | solution.py:14
  89.7 8.8 %collective-permute-start.9 = (bf16[1,2,1,128]{3,1,2,0:T(2,128)(2,1)S(1)}, bf16[1,2,1,128]{3,1,2,0:T(2,128)(2,1)S(1)}, u32[]{:S(2)}, u32[]{:S(2)}) collective-permute-start(bf16[1,2,1,128]{3,1,2,0:T(2,128)(2,1)S(1)} %get-tuple-element.12), channel_id=1, source_target_pairs={{4,0},{8,4},{12,8},{16,12},{20,16},{24,20},{28,24},{5,1},{9,5},{13... | collective-permute-start | bytes 1544 | tf_op jit(solution)/shard_map/ppermute | solution.py:17
  (26 other events, 37.9 us)
where the time goes:
time: 105 us; the launch traced here: 104 us
  starting transfers between devices  49.3 us (47%)
  matrix products  29.6 us (28%)
  other arithmetic  16.1 us (15%)
  local copies, waits for them, and re-layouts  6.99 us (7%)
  between operations  1.76 us (2%)
    ppermute x8, starting transfers between devices, with_halo(): lax.ppermute(lax.slice_in_dim(block, 0, width, axis=dim), axis, backward)  29.9 us
    dot_general x13, matrix products, lookup(): jnp.einsum('nh,mhl->mnl', high_hot, table, precision=lax.Precision.HIGHES...  21.5 us
    ppermute x8, starting transfers between devices, with_halo(): lax.ppermute(lax.slice_in_dim(block, block.shape[dim] - width, None, axis...  19.4 us
    convert_element_type x7, other arithmetic, lookup(): (low_part[:, None] == lax.broadcasted_iota(jnp.int32, (1, lane_width), 1)...  5.61 us
    unnamed x105, local copies, waits for them, and re-layouts  5.31 us
    dot_general x2, matrix products, smooth(): jnp.einsum('bij,brj->bri', inverse, resid, preferred_element_type=jnp.flo...  4.94 us
    sub x6, other arithmetic, lookup(): low_part = index - high_part * lane_width  3.71 us
    select_n x7, other arithmetic, lookup(): high_part = index // lane_width  3.64 us
  transfers between devices with their start and end apart: 16, of which 0 were waited for; matrix products, arithmetic and copies ran while one was open for 33% of the time, Pallas kernels for 0%

commit v1 on v0

v1 whole, which is shorter than its diff:
```python
import functools

import jax
import jax.numpy as jnp
from jax import lax
from jax.experimental import pallas as pl
from jax.experimental.pallas import tpu as pltpu
from jax.sharding import PartitionSpec as P

lane_width = 128
tail_rows = 16
vmem_bytes = 48 * 1024 * 1024
axes = ("wide", "narrow")


def pairings(wide, narrow):
    def number(i, j):
        return i * narrow + j

    def close(pairs, partner_of):
        taken = {d for pair in pairs for d in pair}
        for i in range(wide):
            for j in range(narrow):
                partner = partner_of(i, j)
                if number(i, j) in taken:
                    continue
                if 0 <= partner[0] < wide and 0 <= partner[1] < narrow:
                    if number(*partner) not in taken:
                        pairs.append((number(i, j), number(*partner)))
                        taken |= {number(i, j), number(*partner)}
        moves = [(a, b) for a, b in pairs] + [(b, a) for a, b in pairs if a != b]
        sources = {a for a, _ in moves}
        return moves + [(d, d) for d in range(wide * narrow) if d not in sources]

    plans = []
    for first in (0, 1):
        pairs = [
            (number(i, j), number(i + 1, j))
            for i in range(first, wide - 1, 2)
            for j in range(narrow)
        ]
        plans.append(close(pairs, lambda i, j: (i, j ^ 1)))
    for first in (0, 1):
        pairs = [
            (number(i, j), number(i, j + 1))
            for i in range(wide)
            for j in range(first, narrow - 1, 2)
        ]
        plans.append(close(pairs, lambda i, j: (i, narrow - 1 - j)))
    return plans


def trade(pieces, plans):
    return [lax.ppermute(piece, axes, plan) for piece, plan in zip(pieces, plans)]


def sides_of(wide, narrow):
    found = []
    for base, axis, count in ((0, "wide", wide), (2, "narrow", narrow)):
        here = lax.axis_index(axis)
        for first in (0, 1):
            partner = ((here + first) ^ 1) - first
            side = base + jnp.where(partner > here, 1, 0)
            found.append((side, (partner >= 0) & (partner < count)))
    return found


def spread(row):
    return jnp.broadcast_to(row, (8, lane_width))


def take_lanes(row, low):
    return jnp.take_along_axis(row, low, axis=1, mode="promise_in_bounds")


def pack_kernel(mesh_dims, sends, guess, cell_list, sat, out0, out1, out2, out3, picked):
    places = sides_of(*mesh_dims)
    blocks_sent = sends.shape[0]
    size = guess.shape[1]
    groups = sat.shape[0] // 4
    lists = cell_list.shape[0]
    halves = lists // 4
    index = cell_list[...]
    high = index >> 7
    low = index & (lane_width - 1)
    found = jnp.zeros(index.shape, jnp.float32)
    for group in range(groups):
        modes = sat[pl.ds(group * 4, 4), :]
        mean, along_x, along_y = modes[0:1], modes[1:2], modes[2:3]
        four = jnp.concatenate([mean - along_x, mean + along_x, mean - along_y, mean + along_y], 0)
        rows = jnp.concatenate([four] * halves, 0)
        found = jnp.where(high == group, take_lanes(rows, low), found)
    picked[...] = found
    for (side, _), out in zip(places, (out0, out1, out2, out3)):
        for block in range(blocks_sent):
            out[pl.ds(block * size, size), :] = guess[sends[block, side]].astype(jnp.bfloat16)
        values = [picked[pl.ds(half * 4 + side, 1), :] for half in range(halves)]
        coarse = [value.astype(jnp.bfloat16).astype(jnp.float32) for value in values]
        fine = [value - rounded for value, rounded in zip(values, coarse)]
        blank = jnp.zeros((tail_rows - 2 * halves, lane_width), jnp.float32)
        out[pl.ds(blocks_sent * size, tail_rows), :] = jnp.concatenate(
            coarse + fine + [blank], 0
        ).astype(jnp.bfloat16)


def product(left, right):
    return lax.dot_general(
        left, right, (((1,), (1,)), ((), ())), preferred_element_type=jnp.float32
    )


def land(extended, places, arrived, own_count, blocks_sent, size):
    for (side, exists), came in zip(places, arrived):
        for block in range(blocks_sent):
            value = came[pl.ds(block * size, size), :]
            value = jnp.where(exists, value, jnp.zeros_like(value))
            extended[own_count + side * blocks_sent + block] = value


def first_sweep_kernel(
    mesh_dims, links, sends, guess, in0, in1, in2, in3, couple, inverse, rhs,
    smoothed, out0, out1, out2, out3, extended,
):
    places = sides_of(*mesh_dims)
    blocks, size = guess.shape[0], guess.shape[1]
    blocks_sent = sends.shape[0]
    for block in range(blocks):
        extended[block] = guess[block].astype(jnp.bfloat16)
    land(extended, places, (in0, in1, in2, in3), blocks, blocks_sent, size)
    for block in range(blocks):
        near = jnp.concatenate([extended[links[0, block]], extended[links[1, block]]], 1)
        matrix = jnp.concatenate([couple[block, 0], couple[block, 1]], 1)
        resid = (rhs[block] - product(near, matrix)).astype(jnp.bfloat16)
        smoothed[block] = product(resid, inverse[block]).astype(jnp.bfloat16)
    for (side, _), out in zip(places, (out0, out1, out2, out3)):
        for block in range(blocks_sent):
            out[pl.ds(block * size, size), :] = smoothed[sends[block, side]]


def first_column_kernel(
    mesh_dims, links, sends, current, in0, in1, in2, in3, couple, inverse, rhs,
    column, out0, out1, out2, out3, extended,
):
    places = sides_of(*mesh_dims)
    blocks = current.shape[0]
    size = current.shape[1]
    blocks_sent = sends.shape[0]
    for block in range(blocks):
        extended[block] = current[block, 0:tail_rows, :]
    for (side, exists), came in zip(places, (in0, in1, in2, in3)):
        for block in range(blocks_sent):
            value = came[pl.ds(block * size, tail_rows), :]
            value = jnp.where(exists, value, jnp.zeros_like(value))
            extended[blocks + side * blocks_sent + block] = value
    for block in range(blocks):
        near = jnp.concatenate([extended[links[0, block]], extended[links[1, block]]], 1)
        matrix = jnp.concatenate([couple[block, 0], couple[block, 1]], 1)
        resid = (rhs[block, 0:tail_rows, :] - product(near, matrix)).astype(jnp.bfloat16)
        fresh = product(resid, inverse[block])[0:1, :]
        column[pl.ds(block, 1), :] = fresh.astype(jnp.bfloat16).astype(jnp.float32)
    for (side, _), out in zip(places, (out0, out1, out2, out3)):
        rows = [column[pl.ds(sends[block, side], 1), :] for block in range(blocks_sent)]
        blank = jnp.zeros((tail_rows - blocks_sent, lane_width), jnp.float32)
        out[...] = jnp.concatenate(rows + [blank], 0).astype(jnp.bfloat16)


def second_sweep_kernel(
    mesh_dims, links, current, in0, in1, in2, in3, couple, inverse, rhs, fresh, extended,
):
    places = sides_of(*mesh_dims)
    blocks, size = current.shape[0], current.shape[1]
    blocks_sent = in0.shape[0] // size
    for block in range(blocks):
        extended[block] = current[block]
    land(extended, places, (in0, in1, in2, in3), blocks, blocks_sent, size)
    for block in range(blocks):
        near = jnp.concatenate([extended[links[0, block]], extended[links[1, block]]], 1)
        matrix = jnp.concatenate([couple[block, 0], couple[block, 1]], 1)
        resid = (rhs[block] - product(near, matrix)).astype(jnp.bfloat16)
        fresh[block] = product(resid, inverse[block])


def cells_kernel(
    mesh_dims, blocks_sent, halves, column, in0, in1, in2, in3, tail0, tail1, tail2, tail3,
    cell_faces, coeff, source, neighbours, flags, sat, ratio, out, faces, across_rows,
):
    places = sides_of(*mesh_dims)
    own_rows = column.shape[0]
    face_rows = own_rows + 4 * blocks_sent
    groups = sat.shape[0] // 4
    faces[pl.ds(0, own_rows), :] = column[...]
    for (side, exists), came in zip(places, (in0, in1, in2, in3)):
        value = came[...].astype(jnp.float32)[0:blocks_sent]
        value = jnp.where(exists, value, jnp.zeros_like(value))
        for block in range(blocks_sent):
            faces[pl.ds(own_rows + side * blocks_sent + block, 1), :] = value[block : block + 1]
    modes = [sat[pl.ds(mode, groups, stride=4), :] for mode in range(4)]
    stride = across_rows.shape[0] // 6
    for (side, exists), came in zip(places, (tail0, tail1, tail2, tail3)):
        value = came[...].astype(jnp.float32)
        value = value[0:halves] + value[halves : 2 * halves]
        value = jnp.where(exists, value, jnp.zeros_like(value))
        for half in range(halves):
            across_rows[pl.ds(side * stride + groups + half, 1), :] = value[half : half + 1]
    for face in range(6):
        mode = modes[face // 2 + 1]
        across_rows[pl.ds(face * stride, groups), :] = (
            modes[0] + mode if face % 2 == 0 else modes[0] - mode
        )
    weights = [coeff[pl.ds(face * groups, groups), :] for face in range(6)]
    traces = []
    across = []
    for face in range(6):
        parts = []
        for start in range(0, groups, 8):
            index = cell_faces[pl.ds(face * groups + start, 8), :]
            high, low = index >> 7, index & (lane_width - 1)
            value = jnp.zeros((8, lane_width), jnp.float32)
            for row in range(face_rows):
                got = take_lanes(spread(faces[pl.ds(row, 1), :]), low)
                value = jnp.where(high == row, got, value)
            parts.append(value)
        traces.append(jnp.concatenate(parts, 0))
        parts = []
        for start in range(0, groups, 8):
            index = neighbours[pl.ds(face * groups + start, 8), :]
            high, low = index >> 7, index & (lane_width - 1)
            if 0 < face < 4:
                high = jnp.where(high >= groups, high - face * halves, high)
            value = jnp.zeros((8, lane_width), jnp.float32)
            for row in range(groups + halves if face < 4 else groups):
                got = take_lanes(spread(across_rows[pl.ds(face * stride + row, 1), :]), low)
                value = jnp.where(high == row, got, value)
            parts.append(value)
        across.append(jnp.concatenate(parts, 0))
    total = weights[0]
    gained = source[...] + weights[0] * traces[0]
    for face in range(1, 6):
        total = total + weights[face]
        gained = gained + weights[face] * traces[face]
    pressure = gained / total
    flux = [weights[face] * (pressure - traces[face]) for face in range(6)]
    flow = []
    for face in range(6):
        mode = modes[face // 2 + 1]
        own = modes[0] - mode if face % 2 == 0 else modes[0] + mode
        upwind = flags[pl.ds(face * groups, groups), :] == 1
        flow.append(flux[face] * jnp.where(upwind, own, across[face]))
    step = ratio[...]
    out[pl.ds(0, groups, stride=4), :] = modes[0] - step * (
        flow[0] + flow[1] + flow[2] + flow[3] + flow[4] + flow[5]
    )
    for mode in range(1, 4):
        lo, hi = 2 * mode - 2, 2 * mode - 1
        volume = 0.5 * (flux[hi] - flux[lo]) * modes[0]
        out[pl.ds(mode, groups, stride=4), :] = modes[mode] + 3.0 * step * (
            volume - (flow[hi] - flow[lo])
        )


def call(kernel, outs, specs, scratch=(), flops=0, traffic=0):
    return pl.pallas_call(
        kernel,
        out_shape=outs,
        in_specs=specs,
        out_specs=jax.tree.map(lambda _: pl.BlockSpec(memory_space=pltpu.VMEM), outs),
        scratch_shapes=list(scratch),
        compiler_params=pltpu.CompilerParams(vmem_limit_bytes=vmem_bytes),
        cost_estimate=pl.CostEstimate(flops=flops, bytes_accessed=traffic, transcendentals=0),
    )


scalars = pl.BlockSpec(memory_space=pltpu.SMEM)
whole = pl.BlockSpec(memory_space=pltpu.VMEM)


def by_cells(array):
    return array.reshape(-1, lane_width)


def by_groups(array):
    rows = array.shape[0]
    return jnp.swapaxes(array.reshape(rows, -1, lane_width), 0, 1).reshape(-1, lane_width)


def per_device(
    mesh_dims,
    plans,
    trace_guess,
    trace_rhs,
    block_inverse,
    coupling,
    block_neighbours,
    block_send,
    cell_faces,
    face_coeff,
    cell_source,
    cell_neighbours,
    upwind_flags,
    cell_send,
    saturation,
    step_ratio,
):
    guess = trace_guess[0, 0]
    rhs = trace_rhs[0, 0]
    inverse = block_inverse[0, 0]
    couple = coupling[0, 0]
    links = block_neighbours[0, 0].T
    sends = block_send[0, 0].T
    blocks, columns, size = guess.shape
    blocks_sent = sends.shape[0]
    halo_rows = blocks_sent * columns
    extended_blocks = blocks + 4 * blocks_sent
    sat = by_groups(saturation[0, 0])
    cell_list = by_groups(cell_send[0, 0])
    halves = cell_list.shape[0] // 4
    groups = sat.shape[0] // 4
    half, single = jnp.bfloat16, jnp.float32

    packed = call(
        functools.partial(pack_kernel, mesh_dims),
        [jax.ShapeDtypeStruct((halo_rows + tail_rows, size), half)] * 4,
        [scalars, whole, whole, whole],
        [pltpu.VMEM((4 * halves, lane_width), single)],
    )(sends, guess, cell_list, sat)
    arrived = trade(packed, plans)

    sweep_flops = 6 * blocks * columns * size * size
    smoothed, *packed = call(
        functools.partial(first_sweep_kernel, mesh_dims),
        [jax.ShapeDtypeStruct(guess.shape, half)]
        + [jax.ShapeDtypeStruct((halo_rows, size), half)] * 4,
        [scalars, scalars] + [whole] * 8,
        [pltpu.VMEM((extended_blocks, columns, size), half)],
        sweep_flops,
    )(links, sends, guess, *arrived, couple, inverse, rhs)
    swept = trade(packed, plans)

    column, *packed = call(
        functools.partial(first_column_kernel, mesh_dims),
        [jax.ShapeDtypeStruct((blocks, size), single)]
        + [jax.ShapeDtypeStruct((tail_rows, size), half)] * 4,
        [scalars, scalars] + [whole] * 8,
        [pltpu.VMEM((extended_blocks, tail_rows, size), half)],
        sweep_flops // 8,
    )(links, sends, smoothed, *swept, couple, inverse, rhs)
    edges = trade(packed, plans)

    traces = call(
        functools.partial(second_sweep_kernel, mesh_dims),
        jax.ShapeDtypeStruct(guess.shape, single),
        [scalars] + [whole] * 8,
        [pltpu.VMEM((extended_blocks, columns, size), half)],
        sweep_flops,
    )(links, smoothed, *swept, couple, inverse, rhs)

    tails = [piece[halo_rows:] for piece in arrived]
    face_rows = -(-extended_blocks // 8) * 8
    cell_rows = -(-(groups + halves) // 8) * 8
    following = call(
        functools.partial(cells_kernel, mesh_dims, blocks_sent, halves),
        jax.ShapeDtypeStruct(sat.shape, single),
        [whole] * 16,
        [
            pltpu.VMEM((face_rows, lane_width), single),
            pltpu.VMEM((6 * cell_rows, lane_width), single),
        ],
    )(
        column,
        *edges,
        *tails,
        by_cells(cell_faces[0, 0]),
        by_cells(face_coeff[0, 0]),
        by_cells(cell_source[0]),
        by_cells(cell_neighbours[0, 0]),
        by_cells(upwind_flags[0, 0]),
        sat,
        by_cells(step_ratio[0]),
    )
    saturation_next = jnp.swapaxes(following.reshape(groups, 4, lane_width), 0, 1).reshape(4, -1)
    return traces[None, None], saturation_next[None, None]


def solution(mesh):
    mesh_dims = (mesh.shape["wide"], mesh.shape["narrow"])

    def spec(rank):
        return P("wide", "narrow", *([None] * (rank - 2)))

    placed = tuple(spec(rank) for rank in (5, 5, 5, 6, 4, 4, 4, 4, 3, 4, 4, 4, 4, 3))
    return jax.shard_map(
        functools.partial(per_device, mesh_dims, pairings(*mesh_dims)),
        mesh=mesh,
        in_specs=placed,
        out_specs=(spec(5), spec(4)),
        check_vma=False,
    )
```

time: 105 us -> 34.1 us (0.32)
  the two profiles are of different devices: /device:TPU:10 before, /device:TPU:5 now
where the time goes in v1:
time: 34.1 us; the launch traced here: 33.7 us
  starting transfers between devices  13.4 us (39%)
  Pallas kernels  7.17 us (21%)
  local copies, waits for them, and re-layouts  7.02 us (21%)
  waiting for transfers between devices  5.29 us (16%)
  between operations  0.8 us (2%)
    ppermute x12, starting transfers between devices, trade(): lax.ppermute(piece, axes, plan)  13.4 us
    unnamed x34, local copies, waits for them, and re-layouts  7.01 us
    ppermute x12, waiting for transfers between devices, trade(): lax.ppermute(piece, axes, plan)  5.29 us
    pallas_call x1, Pallas kernels, per_device(): call(functools.partial(second_sweep_kernel, mesh_dims), jax.ShapeDtypeStr...  2.39 us
    pallas_call x1, Pallas kernels, per_device(): call(functools.partial(first_sweep_kernel, mesh_dims), [jax.ShapeDtypeStr...  1.47 us
    pallas_call x1, Pallas kernels, per_device(): call(functools.partial(first_column_kernel, mesh_dims), [jax.ShapeDtypeSt...  1.34 us
    pallas_call x1, Pallas kernels, per_device(): call(functools.partial(cells_kernel, mesh_dims, blocks_sent, halves), jax...  1.3 us
  transfers between devices with their start and end apart: 12, of which 3 were waited for; matrix products, arithmetic and copies ran while one was open for 0% of the time, Pallas kernels for 7%

profile of v1, /device:TPU:5, one launch (start us, length us, event | category | flops | bytes accessed | tf_op | source)
XLA Modules:
  0.0 33.7 jit_solution(16324188160741155083)
XLA Ops:
  0.7 1.3 %copy-done.5 = f32[1,1,16,128,128]{4,3,2,1,0:T(8,128)S(1)} copy-done((f32[1,1,16,128,128]{4,3,2,1,0:T(8,128)S(1)}, f32[1,1,16,128,128]{4,3,2,1,0:T(8,128)}, u32[]{:S(2)}) %copy-start.5) | copy-done | bytes 1048600
  2.0 0.8 %copy-done.6 = f32[1,1,4,2048]{3,2,1,0:T(4,128)S(1)} copy-done((f32[1,1,4,2048]{3,2,1,0:T(4,128)S(1)}, f32[1,1,4,2048]{3,2,1,0:T(4,128)}, u32[]{:S(2)}) %copy-start.6) | copy-done | bytes 32792
  2.7 0.7 %copy-done.12 = s32[1,1,4,2]{2,3,1,0:T(2,128)S(1)} copy-done((s32[1,1,4,2]{2,3,1,0:T(2,128)S(1)}, s32[1,1,4,2]{2,3,1,0:T(2,128)}, u32[]{:S(2)}) %copy-start.12) | copy-done | bytes 56
  3.4 0.7 %copy-done.16 = s32[1,1,4,256]{3,2,1,0:T(4,128)S(1)} copy-done((s32[1,1,4,256]{3,2,1,0:T(4,128)S(1)}, s32[1,1,4,256]{3,2,1,0:T(4,128)}, u32[]{:S(2)}) %copy-start.16) | copy-done | bytes 4120
  4.1 0.7 %shard_map.149 = (bf16[272,128]{1,0:T(8,128)(2,1)S(1)}, bf16[272,128]{1,0:T(8,128)(2,1)S(1)}, bf16[272,128]{1,0:T(8,128)(2,1)S(1)}, bf16[272,128]{1,0:T(8,128)(2,1)S(1)}) custom-call(s32[2,4]{1,0:T(2,128)S(1)} %bitcast.49, f32[16,128,128]{2,1,0:T(8,128)S(1)} %bitcast.41, s32[8,128]{1,0:T(8,128)S(1)} %bitcast.57, f32[64,128]{1,0:T(8,128)S(1)} %bitcast.43), custom_call_target="tpu_custom_call" | custom-call | tf_op jit(solution)/shard_map/pallas_call | solution.py:320
  4.7 0.1 collective-permute-start
  4.8 2.5 %collective-permute-start.1 = (bf16[272,128]{1,0:T(8,128)(2,1)S(1)}, bf16[272,128]{1,0:T(8,128)(2,1)S(1)}, u32[]{:S(2)}, u32[]{:S(2)}) collective-permute-start(bf16[272,128]{1,0:T(8,128)(2,1)S(1)} %get-tuple-element.17), channel_id=1, source_target_pairs={{4,8},{5,9},{6,10},{7,11},{12,16},{13,17},{14,18},{15,19},{20,24},... | collective-permute-start | bytes 208904 | tf_op jit(solution)/shard_map/ppermute | solution.py:54
  7.3 1.2 %collective-permute-start.2 = (bf16[272,128]{1,0:T(8,128)(2,1)S(1)}, bf16[272,128]{1,0:T(8,128)(2,1)S(1)}, u32[]{:S(2)}, u32[]{:S(2)}) collective-permute-start(bf16[272,128]{1,0:T(8,128)(2,1)S(1)} %get-tuple-element.18), channel_id=1, source_target_pairs={{0,1},{2,3},{4,5},{6,7},{8,9},{10,11},{12,13},{14,15},{16,17},{18,... | collective-permute-start | bytes 208904 | tf_op jit(solution)/shard_map/ppermute | solution.py:54
  8.5 1.1 %collective-permute-start.3 = (bf16[272,128]{1,0:T(8,128)(2,1)S(1)}, bf16[272,128]{1,0:T(8,128)(2,1)S(1)}, u32[]{:S(2)}, u32[]{:S(2)}) collective-permute-start(bf16[272,128]{1,0:T(8,128)(2,1)S(1)} %get-tuple-element.19), channel_id=1, source_target_pairs={{1,2},{5,6},{9,10},{13,14},{17,18},{21,22},{25,26},{29,30},{0,3},{... | collective-permute-start | bytes 208904 | tf_op jit(solution)/shard_map/ppermute | solution.py:54
  9.6 0.0 collective-permute-done.in0
  9.6 0.0 collective-permute-done.1.in1
  9.6 2.7 %collective-permute-done.3.in3 = bf16[272,128]{1,0:T(8,128)(2,1)S(1)} collective-permute-done((bf16[272,128]{1,0:T(8,128)(2,1)S(1)}, bf16[272,128]{1,0:T(8,128)(2,1)S(1)}, u32[]{:S(2)}, u32[]{:S(2)}) %collective-permute-start.3) | collective-permute-done | bytes 69664 | tf_op jit(solution)/shard_map/ppermute | solution.py:54
  12.3 0.7 %copy-done.13 = s32[1,1,16,2]{2,3,1,0:T(2,128)S(1)} copy-done((s32[1,1,16,2]{2,3,1,0:T(2,128)S(1)}, s32[1,1,16,2]{2,3,1,0:T(2,128)}, u32[]{:S(2)}) %copy-start.13) | copy-done | bytes 152
  13.0 1.2 %copy-done.1 = f32[1,1,16,128,128]{4,3,2,1,0:T(8,128)S(1)} copy-done((f32[1,1,16,128,128]{4,3,2,1,0:T(8,128)S(1)}, f32[1,1,16,128,128]{4,3,2,1,0:T(8,128)}, u32[]{:S(2)}) %copy-start.1) | copy-done | bytes 1048600
  14.2 1.0 %copy-done.3 = bf16[1,1,16,128,128]{4,3,2,1,0:T(8,128)(2,1)S(1)} copy-done((bf16[1,1,16,128,128]{4,3,2,1,0:T(8,128)(2,1)S(1)}, bf16[1,1,16,128,128]{4,3,2,1,0:T(8,128)(2,1)}, u32[]{:S(2)}) %copy-start.3) | copy-done | bytes 524312
  15.3 1.5 %shard_map.150 = (bf16[16,128,128]{2,1,0:T(8,128)(2,1)S(1)}, bf16[256,128]{1,0:T(8,128)(2,1)S(1)}, bf16[256,128]{1,0:T(8,128)(2,1)S(1)}, bf16[256,128]{1,0:T(8,128)(2,1)S(1)}, bf16[256,128]{1,0:T(8,128)(2,1)S(1)}) custom-call(s32[2,16]{1,0:T(2,128)S(1)} %bitcast.52, s32[2,4]{1,0:T(2,128)S(1)} %bitcast.50, f32[16,128,128]{2,1,0:T(8,128)S(1)} %bitcast.42, ...), custom_call_target="tpu_custom_call" | custom-call | flops 201326592 | tf_op jit(solution)/shard_map/pallas_call | solution.py:329
  16.8 0.1 collective-permute-start.4
  16.8 2.5 %collective-permute-start.5 = (bf16[256,128]{1,0:T(8,128)(2,1)S(1)}, bf16[256,128]{1,0:T(8,128)(2,1)S(1)}, u32[]{:S(2)}, u32[]{:S(2)}) collective-permute-start(bf16[256,128]{1,0:T(8,128)(2,1)S(1)} %get-tuple-element.22), channel_id=1, source_target_pairs={{4,8},{5,9},{6,10},{7,11},{12,16},{13,17},{14,18},{15,19},{20,24},... | collective-permute-start | bytes 196616 | tf_op jit(solution)/shard_map/ppermute | solution.py:54
  19.3 0.6 %collective-permute-start.6 = (bf16[256,128]{1,0:T(8,128)(2,1)S(1)}, bf16[256,128]{1,0:T(8,128)(2,1)S(1)}, u32[]{:S(2)}, u32[]{:S(2)}) collective-permute-start(bf16[256,128]{1,0:T(8,128)(2,1)S(1)} %get-tuple-element.23), channel_id=1, source_target_pairs={{0,1},{2,3},{4,5},{6,7},{8,9},{10,11},{12,13},{14,15},{16,17},{18,... | collective-permute-start | bytes 196616 | tf_op jit(solution)/shard_map/ppermute | solution.py:54
  19.9 1.1 %collective-permute-start.7 = (bf16[256,128]{1,0:T(8,128)(2,1)S(1)}, bf16[256,128]{1,0:T(8,128)(2,1)S(1)}, u32[]{:S(2)}, u32[]{:S(2)}) collective-permute-start(bf16[256,128]{1,0:T(8,128)(2,1)S(1)} %get-tuple-element.24), channel_id=1, source_target_pairs={{1,2},{5,6},{9,10},{13,14},{17,18},{21,22},{25,26},{29,30},{0,3},{... | collective-permute-start | bytes 196616 | tf_op jit(solution)/shard_map/ppermute | solution.py:54
  21.0 0.0 collective-permute-done.4.in0
  21.0 0.5 %collective-permute-done.5.in1 = bf16[256,128]{1,0:T(8,128)(2,1)S(1)} collective-permute-done((bf16[256,128]{1,0:T(8,128)(2,1)S(1)}, bf16[256,128]{1,0:T(8,128)(2,1)S(1)}, u32[]{:S(2)}, u32[]{:S(2)}) %collective-permute-start.5) | collective-permute-done | bytes 65568 | tf_op jit(solution)/shard_map/ppermute | solution.py:54
  21.6 2.0 %collective-permute-done.7.in3 = bf16[256,128]{1,0:T(8,128)(2,1)S(1)} collective-permute-done((bf16[256,128]{1,0:T(8,128)(2,1)S(1)}, bf16[256,128]{1,0:T(8,128)(2,1)S(1)}, u32[]{:S(2)}, u32[]{:S(2)}) %collective-permute-start.7) | collective-permute-done | bytes 65568 | tf_op jit(solution)/shard_map/ppermute | solution.py:54
  23.6 1.3 %shard_map.152 = (f32[16,128]{1,0:T(8,128)S(1)}, bf16[16,128]{1,0:T(8,128)(2,1)S(1)}, bf16[16,128]{1,0:T(8,128)(2,1)S(1)}, bf16[16,128]{1,0:T(8,128)(2,1)S(1)}, bf16[16,128]{1,0:T(8,128)(2,1)S(1)}) custom-call(s32[2,16]{1,0:T(2,128)S(1)} %bitcast.53, s32[2,4]{1,0:T(2,128)S(1)} %bitcast.51, bf16[16,128,128]{2,1,0:T(8,128)(2,1)S(1)} %get-tuple-element.20.current, ...), custom_call_target="tpu_custom_call" | custom-call | flops 25165824 | tf_op jit(solution)/shard_map/pallas_call | solution.py:339
  25.0 0.1 collective-permute-start.8
  25.0 2.5 %collective-permute-start.9 = (bf16[16,128]{1,0:T(8,128)(2,1)S(1)}, bf16[16,128]{1,0:T(8,128)(2,1)S(1)}, u32[]{:S(2)}, u32[]{:S(2)}) collective-permute-start(bf16[16,128]{1,0:T(8,128)(2,1)S(1)} %get-tuple-element.27), channel_id=1, source_target_pairs={{4,8},{5,9},{6,10},{7,11},{12,16},{13,17},{14,18},{15,19},{20,24},... | collective-permute-start | bytes 12296 | tf_op jit(solution)/shard_map/ppermute | solution.py:54
  27.5 0.6 %collective-permute-start.10 = (bf16[16,128]{1,0:T(8,128)(2,1)S(1)}, bf16[16,128]{1,0:T(8,128)(2,1)S(1)}, u32[]{:S(2)}, u32[]{:S(2)}) collective-permute-start(bf16[16,128]{1,0:T(8,128)(2,1)S(1)} %get-tuple-element.28), channel_id=1, source_target_pairs={{0,1},{2,3},{4,5},{6,7},{8,9},{10,11},{12,13},{14,15},{16,17},{18,... | collective-permute-start | bytes 12296 | tf_op jit(solution)/shard_map/ppermute | solution.py:54
  28.1 1.2 %collective-permute-start.11 = (bf16[16,128]{1,0:T(8,128)(2,1)S(1)}, bf16[16,128]{1,0:T(8,128)(2,1)S(1)}, u32[]{:S(2)}, u32[]{:S(2)}) collective-permute-start(bf16[16,128]{1,0:T(8,128)(2,1)S(1)} %get-tuple-element.29), channel_id=1, source_target_pairs={{1,2},{5,6},{9,10},{13,14},{17,18},{21,22},{25,26},{29,30},{0,3},{... | collective-permute-start | bytes 12296 | tf_op jit(solution)/shard_map/ppermute | solution.py:54
  29.3 2.4 %shard_map.151 = f32[16,128,128]{2,1,0:T(8,128)} custom-call(s32[2,16]{1,0:T(2,128)S(1)} %bitcast.54, bf16[16,128,128]{2,1,0:T(8,128)(2,1)S(1)} %get-tuple-element.20.current, bf16[256,128]{1,0:T(8,128)(2,1)S(1)} %collective-permute-done.4.in0, bf16[256,128]{1,0:T(8,128)(2,1)S(1)} %collective-permute-done.5.in1, ...), custom_call_target="tpu_custom_call" | custom-call | flops 201326592 | tf_op jit(solution)/shard_map/pallas_call | solution.py:349
  31.7 0.0 collective-permute-done.8.in0
  31.8 0.6 %copy-done.14 = f32[1,1,2048]{2,1,0:T(1,128)S(1)} copy-done((f32[1,1,2048]{2,1,0:T(1,128)S(1)}, f32[1,1,2048]{2,1,0:T(1,128)}, u32[]{:S(2)}) %copy-start.14) | copy-done | bytes 8216
  32.4 1.3 %shard_map.153 = f32[64,128]{1,0:T(8,128)} custom-call(f32[16,128]{1,0:T(8,128)S(1)} %get-tuple-element.25.column, bf16[16,128]{1,0:T(8,128)(2,1)S(1)} %collective-permute-done.8.in0, bf16[16,128]{1,0:T(8,128)(2,1)S(1)} %collective-permute-done.9.in1, bf16[16,128]{1,0:T(8,128)(2,1)S(1)} %collective-permute-done.10.in2, ...), custom_call_target="tpu_custom_call" | custom-call | tf_op jit(solution)/shard_map/pallas_call | solution.py:360
  (35 shorter events, 0.1 us)
Async XLA Ops:
  0.6 11.7 %copy-start = (bf16[1,1,16,2,128,128]{5,4,3,2,1,0:T(8,128)(2,1)S(1)}, bf16[1,1,16,2,128,128]{5,4,3,2,1,0:T(8,128)(2,1)}, u32[]{:S(2)}) copy-start(bf16[1,1,16,2,128,128]{5,4,3,2,1,0:T(8,128)(2,1)} %param.17) | copy-start | bytes 3145732
  0.6 1.3 %copy-start.5 = (f32[1,1,16,128,128]{4,3,2,1,0:T(8,128)S(1)}, f32[1,1,16,128,128]{4,3,2,1,0:T(8,128)}, u32[]{:S(2)}) copy-start(f32[1,1,16,128,128]{4,3,2,1,0:T(8,128)} %param.14) | copy-start | bytes 3145732
  2.0 0.8 %copy-start.6 = (f32[1,1,4,2048]{3,2,1,0:T(4,128)S(1)}, f32[1,1,4,2048]{3,2,1,0:T(4,128)}, u32[]{:S(2)}) copy-start(f32[1,1,4,2048]{3,2,1,0:T(4,128)} %param.26) | copy-start | bytes 98308
  2.7 0.7 %copy-start.12 = (s32[1,1,4,2]{2,3,1,0:T(2,128)S(1)}, s32[1,1,4,2]{2,3,1,0:T(2,128)}, u32[]{:S(2)}) copy-start(s32[1,1,4,2]{2,3,1,0:T(2,128)} %param.19) | copy-start | bytes 100
  3.4 0.7 %copy-start.16 = (s32[1,1,4,256]{3,2,1,0:T(4,128)S(1)}, s32[1,1,4,256]{3,2,1,0:T(4,128)}, u32[]{:S(2)}) copy-start(s32[1,1,4,256]{3,2,1,0:T(4,128)} %param.25) | copy-start | bytes 12292
  4.7 4.9 %collective-permute-start = (bf16[272,128]{1,0:T(8,128)(2,1)S(1)}, bf16[272,128]{1,0:T(8,128)(2,1)S(1)}, u32[]{:S(2)}, u32[]{:S(2)}) collective-permute-start(bf16[272,128]{1,0:T(8,128)(2,1)S(1)} %get-tuple-element.16), channel_id=1, source_target_pairs={{0,4},{1,5},{2,6},{3,7},{8,12},{9,13},{10,14},{11,15},{16,20},{17,... | collective-permute-start | bytes 208904 | tf_op jit(solution)/shard_map/ppermute | solution.py:54
  4.8 4.8 %collective-permute-start.1 = (bf16[272,128]{1,0:T(8,128)(2,1)S(1)}, bf16[272,128]{1,0:T(8,128)(2,1)S(1)}, u32[]{:S(2)}, u32[]{:S(2)}) collective-permute-start(bf16[272,128]{1,0:T(8,128)(2,1)S(1)} %get-tuple-element.17), channel_id=1, source_target_pairs={{4,8},{5,9},{6,10},{7,11},{12,16},{13,17},{14,18},{15,19},{20,24},... | collective-permute-start | bytes 208904 | tf_op jit(solution)/shard_map/ppermute | solution.py:54
  7.3 2.3 %collective-permute-start.2 = (bf16[272,128]{1,0:T(8,128)(2,1)S(1)}, bf16[272,128]{1,0:T(8,128)(2,1)S(1)}, u32[]{:S(2)}, u32[]{:S(2)}) collective-permute-start(bf16[272,128]{1,0:T(8,128)(2,1)S(1)} %get-tuple-element.18), channel_id=1, source_target_pairs={{0,1},{2,3},{4,5},{6,7},{8,9},{10,11},{12,13},{14,15},{16,17},{18,... | collective-permute-start | bytes 208904 | tf_op jit(solution)/shard_map/ppermute | solution.py:54
  8.5 3.8 %collective-permute-start.3 = (bf16[272,128]{1,0:T(8,128)(2,1)S(1)}, bf16[272,128]{1,0:T(8,128)(2,1)S(1)}, u32[]{:S(2)}, u32[]{:S(2)}) collective-permute-start(bf16[272,128]{1,0:T(8,128)(2,1)S(1)} %get-tuple-element.19), channel_id=1, source_target_pairs={{1,2},{5,6},{9,10},{13,14},{17,18},{21,22},{25,26},{29,30},{0,3},{... | collective-permute-start | bytes 208904 | tf_op jit(solution)/shard_map/ppermute | solution.py:54
  12.3 0.7 %copy-start.13 = (s32[1,1,16,2]{2,3,1,0:T(2,128)S(1)}, s32[1,1,16,2]{2,3,1,0:T(2,128)}, u32[]{:S(2)}) copy-start(s32[1,1,16,2]{2,3,1,0:T(2,128)} %param.18) | copy-start | bytes 388
  13.0 1.2 %copy-start.1 = (f32[1,1,16,128,128]{4,3,2,1,0:T(8,128)S(1)}, f32[1,1,16,128,128]{4,3,2,1,0:T(8,128)}, u32[]{:S(2)}) copy-start(f32[1,1,16,128,128]{4,3,2,1,0:T(8,128)} %param.15) | copy-start | bytes 3145732
  14.2 1.0 %copy-start.3 = (bf16[1,1,16,128,128]{4,3,2,1,0:T(8,128)(2,1)S(1)}, bf16[1,1,16,128,128]{4,3,2,1,0:T(8,128)(2,1)}, u32[]{:S(2)}) copy-start(bf16[1,1,16,128,128]{4,3,2,1,0:T(8,128)(2,1)} %param.16) | copy-start | bytes 1572868
  15.3 8.3 %copy-start.2 = (f32[1,1,16,128,128]{4,3,2,1,0:T(8,128)S(1)}, f32[1,1,16,128,128]{4,3,2,1,0:T(8,128)}, u32[]{:S(2)}) copy-start(f32[1,1,16,128,128]{4,3,2,1,0:T(8,128)} %param.15) | copy-start | bytes 3145732
  15.3 8.3 %copy-start.4 = (bf16[1,1,16,128,128]{4,3,2,1,0:T(8,128)(2,1)S(1)}, bf16[1,1,16,128,128]{4,3,2,1,0:T(8,128)(2,1)}, u32[]{:S(2)}) copy-start(bf16[1,1,16,128,128]{4,3,2,1,0:T(8,128)(2,1)} %param.16) | copy-start | bytes 1572868
  16.8 4.3 %collective-permute-start.4 = (bf16[256,128]{1,0:T(8,128)(2,1)S(1)}, bf16[256,128]{1,0:T(8,128)(2,1)S(1)}, u32[]{:S(2)}, u32[]{:S(2)}) collective-permute-start(bf16[256,128]{1,0:T(8,128)(2,1)S(1)} %get-tuple-element.21), channel_id=1, source_target_pairs={{0,4},{1,5},{2,6},{3,7},{8,12},{9,13},{10,14},{11,15},{16,20},{17,... | collective-permute-start | bytes 196616 | tf_op jit(solution)/shard_map/ppermute | solution.py:54
  16.8 4.7 %collective-permute-start.5 = (bf16[256,128]{1,0:T(8,128)(2,1)S(1)}, bf16[256,128]{1,0:T(8,128)(2,1)S(1)}, u32[]{:S(2)}, u32[]{:S(2)}) collective-permute-start(bf16[256,128]{1,0:T(8,128)(2,1)S(1)} %get-tuple-element.22), channel_id=1, source_target_pairs={{4,8},{5,9},{6,10},{7,11},{12,16},{13,17},{14,18},{15,19},{20,24},... | collective-permute-start | bytes 196616 | tf_op jit(solution)/shard_map/ppermute | solution.py:54
  19.3 2.3 %collective-permute-start.6 = (bf16[256,128]{1,0:T(8,128)(2,1)S(1)}, bf16[256,128]{1,0:T(8,128)(2,1)S(1)}, u32[]{:S(2)}, u32[]{:S(2)}) collective-permute-start(bf16[256,128]{1,0:T(8,128)(2,1)S(1)} %get-tuple-element.23), channel_id=1, source_target_pairs={{0,1},{2,3},{4,5},{6,7},{8,9},{10,11},{12,13},{14,15},{16,17},{18,... | collective-permute-start | bytes 196616 | tf_op jit(solution)/shard_map/ppermute | solution.py:54
  19.9 3.7 %collective-permute-start.7 = (bf16[256,128]{1,0:T(8,128)(2,1)S(1)}, bf16[256,128]{1,0:T(8,128)(2,1)S(1)}, u32[]{:S(2)}, u32[]{:S(2)}) collective-permute-start(bf16[256,128]{1,0:T(8,128)(2,1)S(1)} %get-tuple-element.24), channel_id=1, source_target_pairs={{1,2},{5,6},{9,10},{13,14},{17,18},{21,22},{25,26},{29,30},{0,3},{... | collective-permute-start | bytes 196616 | tf_op jit(solution)/shard_map/ppermute | solution.py:54
  25.0 6.7 %collective-permute-start.8 = (bf16[16,128]{1,0:T(8,128)(2,1)S(1)}, bf16[16,128]{1,0:T(8,128)(2,1)S(1)}, u32[]{:S(2)}, u32[]{:S(2)}) collective-permute-start(bf16[16,128]{1,0:T(8,128)(2,1)S(1)} %get-tuple-element.26), channel_id=1, source_target_pairs={{0,4},{1,5},{2,6},{3,7},{8,12},{9,13},{10,14},{11,15},{16,20},{17,... | collective-permute-start | bytes 12296 | tf_op jit(solution)/shard_map/ppermute | solution.py:54
  25.0 6.7 %collective-permute-start.9 = (bf16[16,128]{1,0:T(8,128)(2,1)S(1)}, bf16[16,128]{1,0:T(8,128)(2,1)S(1)}, u32[]{:S(2)}, u32[]{:S(2)}) collective-permute-start(bf16[16,128]{1,0:T(8,128)(2,1)S(1)} %get-tuple-element.27), channel_id=1, source_target_pairs={{4,8},{5,9},{6,10},{7,11},{12,16},{13,17},{14,18},{15,19},{20,24},... | collective-permute-start | bytes 12296 | tf_op jit(solution)/shard_map/ppermute | solution.py:54
  27.5 4.2 %collective-permute-start.10 = (bf16[16,128]{1,0:T(8,128)(2,1)S(1)}, bf16[16,128]{1,0:T(8,128)(2,1)S(1)}, u32[]{:S(2)}, u32[]{:S(2)}) collective-permute-start(bf16[16,128]{1,0:T(8,128)(2,1)S(1)} %get-tuple-element.28), channel_id=1, source_target_pairs={{0,1},{2,3},{4,5},{6,7},{8,9},{10,11},{12,13},{14,15},{16,17},{18,... | collective-permute-start | bytes 12296 | tf_op jit(solution)/shard_map/ppermute | solution.py:54
  28.1 3.6 %copy-start.8 = (s32[1,1,6,2048]{3,1,2,0:T(1,128)S(1)}, s32[1,1,6,2048]{3,1,2,0:T(1,128)}, u32[]{:S(2)}) copy-start(s32[1,1,6,2048]{3,1,2,0:T(1,128)} %param.20) | copy-start | bytes 147460
  28.1 3.6 %copy-start.9 = (f32[1,1,6,2048]{3,1,2,0:T(1,128)S(1)}, f32[1,1,6,2048]{3,1,2,0:T(1,128)}, u32[]{:S(2)}) copy-start(f32[1,1,6,2048]{3,1,2,0:T(1,128)} %param.21) | copy-start | bytes 147460
  28.1 3.6 %copy-start.10 = (s32[1,1,6,2048]{3,1,2,0:T(1,128)S(1)}, s32[1,1,6,2048]{3,1,2,0:T(1,128)}, u32[]{:S(2)}) copy-start(s32[1,1,6,2048]{3,1,2,0:T(1,128)} %param.23) | copy-start | bytes 147460
  28.1 3.6 %copy-start.11 = (s32[1,1,6,2048]{3,1,2,0:T(1,128)S(1)}, s32[1,1,6,2048]{3,1,2,0:T(1,128)}, u32[]{:S(2)}) copy-start(s32[1,1,6,2048]{3,1,2,0:T(1,128)} %param.24) | copy-start | bytes 147460
  28.1 3.6 %collective-permute-start.11 = (bf16[16,128]{1,0:T(8,128)(2,1)S(1)}, bf16[16,128]{1,0:T(8,128)(2,1)S(1)}, u32[]{:S(2)}, u32[]{:S(2)}) collective-permute-start(bf16[16,128]{1,0:T(8,128)(2,1)S(1)} %get-tuple-element.29), channel_id=1, source_target_pairs={{1,2},{5,6},{9,10},{13,14},{17,18},{21,22},{25,26},{29,30},{0,3},{... | collective-permute-start | bytes 12296 | tf_op jit(solution)/shard_map/ppermute | solution.py:54
  29.3 2.5 %copy-start.7 = (f32[1,1,4,2048]{3,2,1,0:T(4,128)S(1)}, f32[1,1,4,2048]{3,2,1,0:T(4,128)}, u32[]{:S(2)}) copy-start(f32[1,1,4,2048]{3,2,1,0:T(4,128)} %param.26) | copy-start | bytes 98308
  29.3 2.5 %copy-start.15 = (f32[1,1,2048]{2,1,0:T(1,128)S(1)}, f32[1,1,2048]{2,1,0:T(1,128)}, u32[]{:S(2)}) copy-start(f32[1,1,2048]{2,1,0:T(1,128)} %param.27) | copy-start | bytes 24580
  31.7 0.7 %copy-start.14 = (f32[1,1,2048]{2,1,0:T(1,128)S(1)}, f32[1,1,2048]{2,1,0:T(1,128)}, u32[]{:S(2)}) copy-start(f32[1,1,2048]{2,1,0:T(1,128)} %param.22) | copy-start | bytes 24580

commit v2 on v1

v2 whole, which is shorter than its diff:
```python
import functools

import jax
import jax.numpy as jnp
from jax import lax
from jax.experimental import pallas as pl
from jax.experimental.pallas import tpu as pltpu
from jax.sharding import PartitionSpec as P

lane_width = 128
tail_rows = 16
vmem_bytes = 24 * 1024 * 1024
axes = ("wide", "narrow")


def pairings(wide, narrow):
    def number(i, j):
        return i * narrow + j

    def close(pairs, partner_of):
        taken = {d for pair in pairs for d in pair}
        for i in range(wide):
            for j in range(narrow):
                partner = partner_of(i, j)
                if number(i, j) in taken:
                    continue
                if 0 <= partner[0] < wide and 0 <= partner[1] < narrow:
                    if number(*partner) not in taken:
                        pairs.append((number(i, j), number(*partner)))
                        taken |= {number(i, j), number(*partner)}
        moves = [(a, b) for a, b in pairs] + [(b, a) for a, b in pairs if a != b]
        sources = {a for a, _ in moves}
        return moves + [(d, d) for d in range(wide * narrow) if d not in sources]

    plans = []
    for first in (0, 1):
        pairs = [
            (number(i, j), number(i + 1, j))
            for i in range(first, wide - 1, 2)
            for j in range(narrow)
        ]
        plans.append(close(pairs, lambda i, j: (i, j ^ 1)))
    for first in (0, 1):
        pairs = [
            (number(i, j), number(i, j + 1))
            for i in range(wide)
            for j in range(first, narrow - 1, 2)
        ]
        plans.append(close(pairs, lambda i, j: (i, narrow - 1 - j)))
    return plans


def trade(pieces, plans):
    return [lax.ppermute(piece, axes, plan) for piece, plan in zip(pieces, plans)]


def sides_of(wide, narrow):
    found = []
    for base, axis, count in ((0, "wide", wide), (2, "narrow", narrow)):
        here = lax.axis_index(axis)
        for first in (0, 1):
            partner = ((here + first) ^ 1) - first
            side = base + jnp.where(partner > here, 1, 0)
            found.append((side, (partner >= 0) & (partner < count)))
    return found


def spread(row):
    return jnp.broadcast_to(row, (8, lane_width))


def take_lanes(row, low):
    return jnp.take_along_axis(row, low, axis=1, mode="promise_in_bounds")


def pack_kernel(
    mesh_dims, sends_far, guess_far, list_far, sat_far,
    out0, out1, out2, out3, rounded,
    sends, guess, cell_list, sat, picked, arrivals,
):
    places = sides_of(*mesh_dims)
    blocks, size = guess.shape[0], guess.shape[1]
    copies = [
        pltpu.make_async_copy(far, near, arrivals.at[slot])
        for slot, (far, near) in enumerate(
            ((list_far, cell_list), (sat_far, sat), (sends_far, sends))
        )
    ]
    loads = [
        pltpu.make_async_copy(guess_far.at[block], guess.at[block], arrivals.at[3 + block])
        for block in range(blocks)
    ]
    for copy in copies + loads:
        copy.start()
    copies[0].wait()
    copies[1].wait()
    blocks_sent = sends.shape[0]
    groups = sat.shape[0] // 4
    lists = cell_list.shape[0]
    halves = lists // 4
    index = cell_list[...]
    high = index >> 7
    low = index & (lane_width - 1)
    found = jnp.zeros(index.shape, jnp.float32)
    for group in range(groups):
        modes = sat[pl.ds(group * 4, 4), :]
        mean, along_x, along_y = modes[0:1], modes[1:2], modes[2:3]
        four = jnp.concatenate([mean - along_x, mean + along_x, mean - along_y, mean + along_y], 0)
        rows = jnp.concatenate([four] * halves, 0)
        found = jnp.where(high == group, take_lanes(rows, low), found)
    picked[...] = found
    for (side, _), out in zip(places, (out0, out1, out2, out3)):
        values = [picked[pl.ds(half * 4 + side, 1), :] for half in range(halves)]
        coarse = [value.astype(jnp.bfloat16).astype(jnp.float32) for value in values]
        fine = [value - rounded_value for value, rounded_value in zip(values, coarse)]
        blank = jnp.zeros((tail_rows - 2 * halves, lane_width), jnp.float32)
        out[pl.ds(blocks_sent * size, tail_rows), :] = jnp.concatenate(
            coarse + fine + [blank], 0
        ).astype(jnp.bfloat16)
    for block in range(blocks):
        loads[block].wait()
        rounded[block] = guess[block].astype(jnp.bfloat16)
    copies[2].wait()
    for (side, _), out in zip(places, (out0, out1, out2, out3)):
        for block in range(blocks_sent):
            out[pl.ds(block * size, size), :] = rounded[sends[block, side]]


def fetch_kernel(count, *refs):
    fars, nears, arrivals = refs[1 : 1 + count], refs[1 + count : 1 + 2 * count], refs[-1]
    copies = [
        pltpu.make_async_copy(far, near, arrivals.at[slot])
        for slot, (far, near) in enumerate(zip(fars, nears))
    ]
    for copy in copies:
        copy.start()
    for copy in copies:
        copy.wait()


def product(left, right):
    return lax.dot_general(
        left, right, (((1,), (1,)), ((), ())), preferred_element_type=jnp.float32
    )


def relax(extended, links, couple, inverse, rhs, block):
    near = jnp.concatenate([extended[links[0, block]], extended[links[1, block]]], 1)
    matrix = jnp.concatenate([couple[block, 0], couple[block, 1]], 1)
    resid = (rhs[block, 0 : near.shape[0], :] - product(near, matrix)).astype(jnp.bfloat16)
    return product(resid, inverse[block])


def extend(extended, own, places, arrived, blocks_sent, size):
    rows = extended.shape[1]
    own_count = own.shape[0]
    for block in range(own_count):
        extended[block] = own[block, 0:rows, :]
    for (side, exists), came in zip(places, arrived):
        for block in range(blocks_sent):
            value = came[pl.ds(block * size, rows), :]
            value = jnp.where(exists, value, jnp.zeros_like(value))
            extended[own_count + side * blocks_sent + block] = value


def first_edge_kernel(
    mesh_dims, links, sends, own, in0, in1, in2, in3, couple, inverse, rhs,
    extended, out0, out1, out2, out3,
):
    places = sides_of(*mesh_dims)
    size = own.shape[1]
    blocks_sent = sends.shape[0]
    extend(extended, own, places, (in0, in1, in2, in3), blocks_sent, size)
    for (side, _), out in zip(places, (out0, out1, out2, out3)):
        for block in range(blocks_sent):
            fresh = relax(extended, links, couple, inverse, rhs, sends[block, side])
            out[pl.ds(block * size, size), :] = fresh.astype(jnp.bfloat16)


def look_up(table, first_row, rows, high, low):
    value = jnp.zeros((8, lane_width), jnp.float32)
    for row in range(rows):
        got = take_lanes(spread(table[pl.ds(first_row + row, 1), :]), low)
        value = jnp.where(high == row, got, value)
    return value


def first_sweep_kernel(
    mesh_dims, halves, links, extended, couple, inverse, rhs,
    sat, neighbours, tail0, tail1, tail2, tail3,
    smoothed, across, across_rows,
):
    places = sides_of(*mesh_dims)
    groups = sat.shape[0] // 4
    stride = across_rows.shape[0] // 6
    modes = [sat[pl.ds(mode, groups, stride=4), :] for mode in range(4)]
    for (side, exists), came in zip(places, (tail0, tail1, tail2, tail3)):
        value = came[...].astype(jnp.float32)
        value = value[0:halves] + value[halves : 2 * halves]
        value = jnp.where(exists, value, jnp.zeros_like(value))
        for half in range(halves):
            across_rows[pl.ds(side * stride + groups + half, 1), :] = value[half : half + 1]
    for face in range(6):
        mode = modes[face // 2 + 1]
        across_rows[pl.ds(face * stride, groups), :] = (
            modes[0] + mode if face % 2 == 0 else modes[0] - mode
        )
    for block in range(smoothed.shape[0]):
        smoothed[block] = relax(extended, links, couple, inverse, rhs, block).astype(jnp.bfloat16)
    for face in range(6):
        for start in range(0, groups, 8):
            index = neighbours[pl.ds(face * groups + start, 8), :]
            high, low = index >> 7, index & (lane_width - 1)
            if 0 < face < 4:
                high = jnp.where(high >= groups, high - face * halves, high)
            rows = groups + halves if face < 4 else groups
            across[pl.ds(face * groups + start, 8), :] = look_up(
                across_rows, face * stride, rows, high, low
            )


def second_edge_kernel(
    mesh_dims, links, sends, own, in0, in1, in2, in3, couple, inverse, rhs,
    out0, out1, out2, out3, extended,
):
    places = sides_of(*mesh_dims)
    size = own.shape[1]
    blocks_sent = sends.shape[0]
    extend(extended, own, places, (in0, in1, in2, in3), blocks_sent, size)
    for (side, _), out in zip(places, (out0, out1, out2, out3)):
        rows = [
            relax(extended, links, couple, inverse, rhs, sends[block, side])[0:1, :]
            for block in range(blocks_sent)
        ]
        blank = jnp.zeros((tail_rows - blocks_sent, lane_width), jnp.float32)
        out[...] = jnp.concatenate(rows + [blank], 0).astype(jnp.bfloat16)


def second_sweep_kernel(
    mesh_dims, links, own, in0, in1, in2, in3, couple, inverse, rhs,
    traces, column, extended, fresh, departures,
):
    places = sides_of(*mesh_dims)
    blocks, size = own.shape[0], own.shape[1]
    blocks_sent = in0.shape[0] // size
    extend(extended, own, places, (in0, in1, in2, in3), blocks_sent, size)
    stores = []
    for block in range(blocks):
        value = relax(extended, links, couple, inverse, rhs, block)
        fresh[block] = value
        stores.append(
            pltpu.make_async_copy(fresh.at[block], traces.at[block], departures.at[block])
        )
        stores[block].start()
        column[pl.ds(block, 1), :] = value[0:1].astype(jnp.bfloat16).astype(jnp.float32)
    for store in stores:
        store.wait()


def cells_kernel(
    mesh_dims, blocks_sent, column, in0, in1, in2, in3, across,
    cell_faces, coeff, source, flags, sat, ratio, out, faces,
):
    places = sides_of(*mesh_dims)
    own_rows = column.shape[0]
    face_rows = own_rows + 4 * blocks_sent
    groups = sat.shape[0] // 4
    faces[pl.ds(0, own_rows), :] = column[...]
    for (side, exists), came in zip(places, (in0, in1, in2, in3)):
        value = came[...].astype(jnp.float32)[0:blocks_sent]
        value = jnp.where(exists, value, jnp.zeros_like(value))
        for block in range(blocks_sent):
            faces[pl.ds(own_rows + side * blocks_sent + block, 1), :] = value[block : block + 1]
    modes = [sat[pl.ds(mode, groups, stride=4), :] for mode in range(4)]
    weights = [coeff[pl.ds(face * groups, groups), :] for face in range(6)]
    traces = []
    for face in range(6):
        parts = []
        for start in range(0, groups, 8):
            index = cell_faces[pl.ds(face * groups + start, 8), :]
            parts.append(look_up(faces, 0, face_rows, index >> 7, index & (lane_width - 1)))
        traces.append(jnp.concatenate(parts, 0))
    total = weights[0]
    gained = source[...] + weights[0] * traces[0]
    for face in range(1, 6):
        total = total + weights[face]
        gained = gained + weights[face] * traces[face]
    pressure = gained / total
    flux = [weights[face] * (pressure - traces[face]) for face in range(6)]
    flow = []
    for face in range(6):
        mode = modes[face // 2 + 1]
        own = modes[0] - mode if face % 2 == 0 else modes[0] + mode
        rows = pl.ds(face * groups, groups)
        flow.append(flux[face] * jnp.where(flags[rows, :] == 1, own, across[rows, :]))
    step = ratio[...]
    out[pl.ds(0, groups, stride=4), :] = modes[0] - step * (
        flow[0] + flow[1] + flow[2] + flow[3] + flow[4] + flow[5]
    )
    for mode in range(1, 4):
        lo, hi = 2 * mode - 2, 2 * mode - 1
        volume = 0.5 * (flux[hi] - flux[lo]) * modes[0]
        out[pl.ds(mode, groups, stride=4), :] = modes[mode] + 3.0 * step * (
            volume - (flow[hi] - flow[lo])
        )


scalars = pl.BlockSpec(memory_space=pltpu.SMEM)
whole = pl.BlockSpec(memory_space=pltpu.VMEM)
far = pl.BlockSpec(memory_space=pl.ANY)


def call(kernel, outs, specs, scratch=(), flops=0, traffic=0, out_specs=None):
    return pl.pallas_call(
        kernel,
        out_shape=outs,
        in_specs=specs,
        out_specs=[whole] * len(outs) if out_specs is None else out_specs,
        scratch_shapes=list(scratch),
        compiler_params=pltpu.CompilerParams(vmem_limit_bytes=vmem_bytes),
        cost_estimate=pl.CostEstimate(flops=flops, bytes_accessed=traffic, transcendentals=0),
    )


def keep_far(array):
    return pltpu.with_memory_space_constraint(array, pltpu.HBM)


def by_cells(array):
    return array.reshape(-1, lane_width)


def by_groups(array):
    rows = array.shape[0]
    return jnp.swapaxes(array.reshape(rows, -1, lane_width), 0, 1).reshape(-1, lane_width)


def per_device(
    mesh_dims,
    plans,
    trace_guess,
    trace_rhs,
    block_inverse,
    coupling,
    block_neighbours,
    block_send,
    cell_faces,
    face_coeff,
    cell_source,
    cell_neighbours,
    upwind_flags,
    cell_send,
    saturation,
    step_ratio,
):
    guess = trace_guess[0, 0]
    rhs = trace_rhs[0, 0]
    inverse = block_inverse[0, 0]
    couple = coupling[0, 0]
    links = block_neighbours[0, 0].T
    sends = block_send[0, 0].T
    blocks, columns, size = guess.shape
    blocks_sent = sends.shape[0]
    halo_rows = blocks_sent * columns
    extended_blocks = blocks + 4 * blocks_sent
    sat = by_groups(saturation[0, 0])
    cell_list = by_groups(cell_send[0, 0])
    halves = cell_list.shape[0] // 4
    groups = sat.shape[0] // 4
    half, single = jnp.bfloat16, jnp.float32

    def like(array):
        return jax.ShapeDtypeStruct(array.shape, array.dtype)

    *packed, own = call(
        functools.partial(pack_kernel, mesh_dims),
        [jax.ShapeDtypeStruct((halo_rows + tail_rows, size), half)] * 4
        + [jax.ShapeDtypeStruct(guess.shape, half)],
        [far] * 4,
        [
            pltpu.SMEM(sends.shape, jnp.int32),
            pltpu.VMEM(guess.shape, single),
            pltpu.VMEM(cell_list.shape, jnp.int32),
            pltpu.VMEM(sat.shape, single),
            pltpu.VMEM((4 * halves, lane_width), single),
            pltpu.SemaphoreType.DMA((3 + blocks,)),
        ],
    )(*map(keep_far, (sends, guess, cell_list, sat)))
    arrived = trade(packed, plans)

    remote = [
        couple,
        inverse,
        rhs,
        by_cells(cell_faces[0, 0]),
        by_cells(face_coeff[0, 0]),
        by_cells(cell_source[0]),
        by_cells(cell_neighbours[0, 0]),
        by_cells(upwind_flags[0, 0]),
        sat,
        by_cells(step_ratio[0]),
        links,
        sends,
    ]
    (
        couple,
        inverse,
        rhs,
        cell_faces,
        coeff,
        source,
        neighbours,
        flags,
        sat,
        ratio,
        links,
        sends,
    ) = call(
        functools.partial(fetch_kernel, len(remote)),
        [like(array) for array in remote],
        [far] * (1 + len(remote)),
        [pltpu.SemaphoreType.DMA((len(remote),))],
        traffic=4 * guess.size,
    )(own, *map(keep_far, remote))

    sweep_flops = 6 * blocks * columns * size * size
    extended, *packed = call(
        functools.partial(first_edge_kernel, mesh_dims),
        [jax.ShapeDtypeStruct((extended_blocks, columns, size), half)]
        + [jax.ShapeDtypeStruct((halo_rows, size), half)] * 4,
        [scalars, scalars] + [whole] * 8,
        flops=sweep_flops // 2,
    )(links, sends, own, *arrived, couple, inverse, rhs)
    swept = trade(packed, plans)

    tails = [piece[halo_rows:] for piece in arrived]
    cell_rows = -(-(groups + halves) // 8) * 8
    smoothed, across = call(
        functools.partial(first_sweep_kernel, mesh_dims, halves),
        [like(own), jax.ShapeDtypeStruct(neighbours.shape, single)],
        [scalars] + [whole] * 10,
        [pltpu.VMEM((6 * cell_rows, lane_width), single)],
        sweep_flops,
    )(links, extended, couple, inverse, rhs, sat, neighbours, *tails)

    edges = trade(
        call(
            functools.partial(second_edge_kernel, mesh_dims),
            [jax.ShapeDtypeStruct((tail_rows, size), half)] * 4,
            [scalars, scalars] + [whole] * 8,
            [pltpu.VMEM((extended_blocks, tail_rows, size), half)],
            sweep_flops // 16,
        )(links, sends, smoothed, *swept, couple, inverse, rhs),
        plans,
    )

    traces, column = call(
        functools.partial(second_sweep_kernel, mesh_dims),
        [jax.ShapeDtypeStruct(guess.shape, single), jax.ShapeDtypeStruct((blocks, size), single)],
        [scalars] + [whole] * 8,
        [
            pltpu.VMEM((extended_blocks, columns, size), half),
            pltpu.VMEM(guess.shape, single),
            pltpu.SemaphoreType.DMA((blocks,)),
        ],
        sweep_flops,
        out_specs=[far, whole],
    )(links, smoothed, *swept, couple, inverse, rhs)

    face_rows = -(-extended_blocks // 8) * 8
    (following,) = call(
        functools.partial(cells_kernel, mesh_dims, blocks_sent),
        [like(sat)],
        [whole] * 12,
        [pltpu.VMEM((face_rows, lane_width), single)],
    )(column, *edges, across, cell_faces, coeff, source, flags, sat, ratio)
    saturation_next = jnp.swapaxes(following.reshape(groups, 4, lane_width), 0, 1).reshape(4, -1)
    return traces[None, None], saturation_next[None, None]


def solution(mesh):
    mesh_dims = (mesh.shape["wide"], mesh.shape["narrow"])

    def spec(rank):
        return P("wide", "narrow", *([None] * (rank - 2)))

    placed = tuple(spec(rank) for rank in (5, 5, 5, 6, 4, 4, 4, 4, 3, 4, 4, 4, 4, 3))
    return jax.shard_map(
        functools.partial(per_device, mesh_dims, pairings(*mesh_dims)),
        mesh=mesh,
        in_specs=placed,
        out_specs=(spec(5), spec(4)),
        check_vma=False,
    )
```

time: 34.1 us -> 27.1 us (0.79)
  the two profiles are of different devices: /device:TPU:5 before, /device:TPU:8 now
where the time goes in v2:
time: 27.1 us; the launch traced here: 26.9 us
  starting transfers between devices  10.2 us (38%)
  Pallas kernels  10.1 us (37%)
  waiting for transfers between devices  5.83 us (22%)
  between operations  0.72 us (3%)
    ppermute x12, starting transfers between devices, trade(): lax.ppermute(piece, axes, plan)  10.2 us
    ppermute x12, waiting for transfers between devices, trade(): lax.ppermute(piece, axes, plan)  5.83 us
    pallas_call x1, Pallas kernels, per_device(): call(functools.partial(second_sweep_kernel, mesh_dims), [jax.ShapeDtypeSt...  2.2 us
    pallas_call x1, Pallas kernels, per_device(): call(functools.partial(fetch_kernel, len(remote)), [like(array) for array...  1.82 us
    pallas_call x1, Pallas kernels, per_device(): call(functools.partial(pack_kernel, mesh_dims), [jax.ShapeDtypeStruct((ha...  1.47 us
    pallas_call x1, Pallas kernels, per_device(): call(functools.partial(first_sweep_kernel, mesh_dims, halves), [like(own)...  1.37 us
    pallas_call x1, Pallas kernels, per_device(): call(functools.partial(first_edge_kernel, mesh_dims), [jax.ShapeDtypeStru...  1.16 us
    pallas_call x1, Pallas kernels, per_device(): call(functools.partial(cells_kernel, mesh_dims, blocks_sent), [like(sat)]...  1.05 us
  transfers between devices with their start and end apart: 12, of which 4 were waited for; matrix products, arithmetic and copies ran while one was open for 0% of the time, Pallas kernels for 20%

profile of v2, /device:TPU:8, one launch (start us, length us, event | category | flops | bytes accessed | tf_op | source)
XLA Modules:
  0.0 26.9 jit_solution(18336902344816954304)
XLA Ops:
  0.6 1.5 %shard_map.149 = (bf16[272,128]{1,0:T(8,128)(2,1)S(1)}, bf16[272,128]{1,0:T(8,128)(2,1)S(1)}, bf16[272,128]{1,0:T(8,128)(2,1)S(1)}, bf16[272,128]{1,0:T(8,128)(2,1)S(1)}, bf16[16,128,128]{2,1,0:T(8,128)(2,1)S(1)}) custom-call(s32[2,4]{1,0:T(2,128)} %bitcast.46, f32[16,128,128]{2,1,0:T(8,128)} %bitcast.34, s32[8,128]{1,0:T(8,128)} %bitcast.45, f32[64,128]{1,0:T(8,128)} %bitcast.36), custom_call_target="tpu_custom_call" | custom-call | tf_op jit(solution)/shard_map/pallas_call | solution.py:375
  2.1 1.6 %collective-permute-start = (bf16[272,128]{1,0:T(8,128)(2,1)S(1)}, bf16[272,128]{1,0:T(8,128)(2,1)S(1)}, u32[]{:S(2)}, u32[]{:S(2)}) collective-permute-start(bf16[272,128]{1,0:T(8,128)(2,1)S(1)} %get-tuple-element.35), channel_id=1, source_target_pairs={{0,4},{1,5},{2,6},{3,7},{8,12},{9,13},{10,14},{11,15},{16,20},{17,... | collective-permute-start | bytes 208904 | tf_op jit(solution)/shard_map/ppermute | solution.py:54
  3.7 0.0 collective-permute-start.1
  3.7 0.0 collective-permute-start.2
  3.7 2.0 %collective-permute-start.3 = (bf16[272,128]{1,0:T(8,128)(2,1)S(1)}, bf16[272,128]{1,0:T(8,128)(2,1)S(1)}, u32[]{:S(2)}, u32[]{:S(2)}) collective-permute-start(bf16[272,128]{1,0:T(8,128)(2,1)S(1)} %get-tuple-element.38), channel_id=1, source_target_pairs={{1,2},{5,6},{9,10},{13,14},{17,18},{21,22},{25,26},{29,30},{0,3},{... | collective-permute-start | bytes 208904 | tf_op jit(solution)/shard_map/ppermute | solution.py:54
  5.7 1.8 %shard_map.150 = (bf16[16,2,128,128]{3,2,1,0:T(8,128)(2,1)S(1)}, bf16[16,128,128]{2,1,0:T(8,128)(2,1)S(1)}, f32[16,128,128]{2,1,0:T(8,128)S(1)}, s32[96,128]{1,0...) custom-call(bf16[16,128,128]{2,1,0:T(8,128)(2,1)S(1)} %get-tuple-ele, ...), custom_call_target="tpu_custom_call" | custom-call | bytes 1048576 | tf_op jit(solution)/shard_map/pallas_call | solution.py:418
  7.5 0.0 collective-permute-done.in0
  7.5 1.4 %collective-permute-done.1.in1 = bf16[272,128]{1,0:T(8,128)(2,1)S(1)} collective-permute-done((bf16[272,128]{1,0:T(8,128)(2,1)S(1)}, bf16[272,128]{1,0:T(8,128)(2,1)S(1)}, u32[]{:S(2)}, u32[]{:S(2)}) %collective-permute-start.1) | collective-permute-done | bytes 69664 | tf_op jit(solution)/shard_map/ppermute | solution.py:54
  8.9 0.0 collective-permute-done.2.in2
  8.9 0.0 collective-permute-done.3.in3
  8.9 1.2 %shard_map.151 = (bf16[24,128,128]{2,1,0:T(8,128)(2,1)S(1)}, bf16[256,128]{1,0:T(8,128)(2,1)S(1)}, bf16[256,128]{1,0:T(8,128)(2,1)S(1)}, bf16[256,128]{1,0:T(8,128)(2,1)S(1)}, bf16[256,128]{1,0:T(8,128)(2,1)S(1)}) custom-call(s32[2,16]{1,0:T(2,128)S(1)} %get-tuple-element.33.links, s32[2,4]{1,0:T(2,128)S(1)} %get-tuple-element.34.sends, ...), custom_call_target="tpu_custom_call" | custom-call | flops 100663296 | tf_op jit(solution)/shard_map/pallas_call | solution.py:427
  10.1 1.7 %collective-permute-start.4 = (bf16[256,128]{1,0:T(8,128)(2,1)S(1)}, bf16[256,128]{1,0:T(8,128)(2,1)S(1)}, u32[]{:S(2)}, u32[]{:S(2)}) collective-permute-start(bf16[256,128]{1,0:T(8,128)(2,1)S(1)} %get-tuple-element.46), channel_id=1, source_target_pairs={{0,4},{1,5},{2,6},{3,7},{8,12},{9,13},{10,14},{11,15},{16,20},{17,... | collective-permute-start | bytes 196616 | tf_op jit(solution)/shard_map/ppermute | solution.py:54
  11.8 0.0 collective-permute-start.5
  11.8 0.2 collective-permute-start.6
  12.0 1.4 %collective-permute-start.7 = (bf16[256,128]{1,0:T(8,128)(2,1)S(1)}, bf16[256,128]{1,0:T(8,128)(2,1)S(1)}, u32[]{:S(2)}, u32[]{:S(2)}) collective-permute-start(bf16[256,128]{1,0:T(8,128)(2,1)S(1)} %get-tuple-element.49), channel_id=1, source_target_pairs={{1,2},{5,6},{9,10},{13,14},{17,18},{21,22},{25,26},{29,30},{0,3},{... | collective-permute-start | bytes 196616 | tf_op jit(solution)/shard_map/ppermute | solution.py:54
  13.4 1.4 %shard_map.152 = (bf16[16,128,128]{2,1,0:T(8,128)(2,1)S(1)}, f32[96,128]{1,0:T(8,128)S(1)}) custom-call(s32[2,16]{1,0:T(2,128)S(1)} %get-tuple-element.33.links, bf16[24,128,128]{2,1,0:T(8,128)(2,1)S(1)} %get-tuple-element.42.extended, bf16[16,2,128,128]{3,2,1,0:T(8,128)(2,1)S(1)} %get-tuple-element.39.couple, ...), custom_call_target="tpu_custom_call" | custom-call | flops 201326592 | tf_op jit(solution)/shard_map/pallas_call | solution.py:438
  14.8 0.4 %collective-permute-done.4.in0 = bf16[256,128]{1,0:T(8,128)(2,1)S(1)} collective-permute-done((bf16[256,128]{1,0:T(8,128)(2,1)S(1)}, bf16[256,128]{1,0:T(8,128)(2,1)S(1)}, u32[]{:S(2)}, u32[]{:S(2)}) %collective-permute-start.4) | collective-permute-done | bytes 65568 | tf_op jit(solution)/shard_map/ppermute | solution.py:54
  15.2 1.7 %collective-permute-done.5.in1 = bf16[256,128]{1,0:T(8,128)(2,1)S(1)} collective-permute-done((bf16[256,128]{1,0:T(8,128)(2,1)S(1)}, bf16[256,128]{1,0:T(8,128)(2,1)S(1)}, u32[]{:S(2)}, u32[]{:S(2)}) %collective-permute-start.5) | collective-permute-done | bytes 65568 | tf_op jit(solution)/shard_map/ppermute | solution.py:54
  17.0 0.0 collective-permute-done.6.in2
  17.0 0.0 collective-permute-done.7.in3
  17.0 1.0 %shard_map.154 = (bf16[16,128]{1,0:T(8,128)(2,1)S(1)}, bf16[16,128]{1,0:T(8,128)(2,1)S(1)}, bf16[16,128]{1,0:T(8,128)(2,1)S(1)}, bf16[16,128]{1,0:T(8,128)(2,1)S(1)}) custom-call(s32[2,16]{1,0:T(2,128)S(1)} %get-tuple-element.33.links, s32[2,4]{1,0:T(2,128)S(1)} %get-tuple-element.34.sends, bf16[16,128,128]{2,1,0:T(8,128)(2,1)S(1)} %get-tuple-element.45.own, ...), custom_call_target="tpu_custom_call" | custom-call | flops 12582912 | tf_op jit(solution)/shard_map/pallas_call | solution.py:447
  18.0 0.1 collective-permute-start.10
  18.1 1.6 %collective-permute-start.11 = (bf16[16,128]{1,0:T(8,128)(2,1)S(1)}, bf16[16,128]{1,0:T(8,128)(2,1)S(1)}, u32[]{:S(2)}, u32[]{:S(2)}) collective-permute-start(bf16[16,128]{1,0:T(8,128)(2,1)S(1)} %get-tuple-element.55), channel_id=1, source_target_pairs={{1,2},{5,6},{9,10},{13,14},{17,18},{21,22},{25,26},{29,30},{0,3},{... | collective-permute-start | bytes 12296 | tf_op jit(solution)/shard_map/ppermute | solution.py:54
  19.7 1.6 %collective-permute-start.8 = (bf16[16,128]{1,0:T(8,128)(2,1)S(1)}, bf16[16,128]{1,0:T(8,128)(2,1)S(1)}, u32[]{:S(2)}, u32[]{:S(2)}) collective-permute-start(bf16[16,128]{1,0:T(8,128)(2,1)S(1)} %get-tuple-element.52), channel_id=1, source_target_pairs={{0,4},{1,5},{2,6},{3,7},{8,12},{9,13},{10,14},{11,15},{16,20},{17,... | collective-permute-start | bytes 12296 | tf_op jit(solution)/shard_map/ppermute | solution.py:54
  21.3 0.0 collective-permute-start.9
  21.3 2.2 %shard_map.153 = (f32[16,128,128]{2,1,0:T(8,128)}, f32[16,128]{1,0:T(8,128)S(1)}) custom-call(s32[2,16]{1,0:T(2,128)S(1)} %get-tuple-element.33.links, bf16[16,128,128]{2,1,0:T(8,128)(2,1)S(1)} %get-tuple-element.45.own, bf16[256,128]{1,0:T(8,128)(2,1)S(1)} %collective-permute-done.4.in0, bf16[256,128]{1,0:T(8,128)(2,1)S(1)} %collective-permute-done.5.in1, ...), custom_call_target="tpu_custom_call" | custom-call | flops 201326592 | tf_op jit(solution)/shard_map/pallas_call | solution.py:457
  23.5 0.0 collective-permute-done.10.in2
  23.5 0.0 collective-permute-done.11.in3
  23.5 0.0 collective-permute-done.8.in0
  23.6 2.3 %collective-permute-done.9.in1 = bf16[16,128]{1,0:T(8,128)(2,1)S(1)} collective-permute-done((bf16[16,128]{1,0:T(8,128)(2,1)S(1)}, bf16[16,128]{1,0:T(8,128)(2,1)S(1)}, u32[]{:S(2)}, u32[]{:S(2)}) %collective-permute-start.9) | collective-permute-done | bytes 4128 | tf_op jit(solution)/shard_map/ppermute | solution.py:54
  25.8 1.0 %shard_map.155 = f32[64,128]{1,0:T(8,128)} custom-call(f32[16,128]{1,0:T(8,128)S(1)} %get-tuple-element.51.column, bf16[16,128]{1,0:T(8,128)(2,1)S(1)} %collective-permute-done.8.in0, bf16[16,128]{1,0:T(8,128)(2,1)S(1)} %collective-permute-done.9.in1, bf16[16,128]{1,0:T(8,128)(2,1)S(1)} %collective-permute-done.10.in2, ...), custom_call_target="tpu_custom_call" | custom-call | tf_op jit(solution)/shard_map/pallas_call | solution.py:471
  (4 shorter events, 0.0 us)
Async XLA Ops:
  2.1 5.4 %collective-permute-start = (bf16[272,128]{1,0:T(8,128)(2,1)S(1)}, bf16[272,128]{1,0:T(8,128)(2,1)S(1)}, u32[]{:S(2)}, u32[]{:S(2)}) collective-permute-start(bf16[272,128]{1,0:T(8,128)(2,1)S(1)} %get-tuple-element.35), channel_id=1, source_target_pairs={{0,4},{1,5},{2,6},{3,7},{8,12},{9,13},{10,14},{11,15},{16,20},{17,... | collective-permute-start | bytes 208904 | tf_op jit(solution)/shard_map/ppermute | solution.py:54
  3.7 5.2 %collective-permute-start.1 = (bf16[272,128]{1,0:T(8,128)(2,1)S(1)}, bf16[272,128]{1,0:T(8,128)(2,1)S(1)}, u32[]{:S(2)}, u32[]{:S(2)}) collective-permute-start(bf16[272,128]{1,0:T(8,128)(2,1)S(1)} %get-tuple-element.36), channel_id=1, source_target_pairs={{4,8},{5,9},{6,10},{7,11},{12,16},{13,17},{14,18},{15,19},{20,24},... | collective-permute-start | bytes 208904 | tf_op jit(solution)/shard_map/ppermute | solution.py:54
  3.7 5.2 %collective-permute-start.2 = (bf16[272,128]{1,0:T(8,128)(2,1)S(1)}, bf16[272,128]{1,0:T(8,128)(2,1)S(1)}, u32[]{:S(2)}, u32[]{:S(2)}) collective-permute-start(bf16[272,128]{1,0:T(8,128)(2,1)S(1)} %get-tuple-element.37), channel_id=1, source_target_pairs={{0,1},{2,3},{4,5},{6,7},{8,9},{10,11},{12,13},{14,15},{16,17},{18,... | collective-permute-start | bytes 208904 | tf_op jit(solution)/shard_map/ppermute | solution.py:54
  3.7 5.2 %collective-permute-start.3 = (bf16[272,128]{1,0:T(8,128)(2,1)S(1)}, bf16[272,128]{1,0:T(8,128)(2,1)S(1)}, u32[]{:S(2)}, u32[]{:S(2)}) collective-permute-start(bf16[272,128]{1,0:T(8,128)(2,1)S(1)} %get-tuple-element.38), channel_id=1, source_target_pairs={{1,2},{5,6},{9,10},{13,14},{17,18},{21,22},{25,26},{29,30},{0,3},{... | collective-permute-start | bytes 208904 | tf_op jit(solution)/shard_map/ppermute | solution.py:54
  10.1 5.1 %collective-permute-start.4 = (bf16[256,128]{1,0:T(8,128)(2,1)S(1)}, bf16[256,128]{1,0:T(8,128)(2,1)S(1)}, u32[]{:S(2)}, u32[]{:S(2)}) collective-permute-start(bf16[256,128]{1,0:T(8,128)(2,1)S(1)} %get-tuple-element.46), channel_id=1, source_target_pairs={{0,4},{1,5},{2,6},{3,7},{8,12},{9,13},{10,14},{11,15},{16,20},{17,... | collective-permute-start | bytes 196616 | tf_op jit(solution)/shard_map/ppermute | solution.py:54
  11.8 5.2 %collective-permute-start.5 = (bf16[256,128]{1,0:T(8,128)(2,1)S(1)}, bf16[256,128]{1,0:T(8,128)(2,1)S(1)}, u32[]{:S(2)}, u32[]{:S(2)}) collective-permute-start(bf16[256,128]{1,0:T(8,128)(2,1)S(1)} %get-tuple-element.47), channel_id=1, source_target_pairs={{4,8},{5,9},{6,10},{7,11},{12,16},{13,17},{14,18},{15,19},{20,24},... | collective-permute-start | bytes 196616 | tf_op jit(solution)/shard_map/ppermute | solution.py:54
  11.8 5.2 %collective-permute-start.6 = (bf16[256,128]{1,0:T(8,128)(2,1)S(1)}, bf16[256,128]{1,0:T(8,128)(2,1)S(1)}, u32[]{:S(2)}, u32[]{:S(2)}) collective-permute-start(bf16[256,128]{1,0:T(8,128)(2,1)S(1)} %get-tuple-element.48), channel_id=1, source_target_pairs={{0,1},{2,3},{4,5},{6,7},{8,9},{10,11},{12,13},{14,15},{16,17},{18,... | collective-permute-start | bytes 196616 | tf_op jit(solution)/shard_map/ppermute | solution.py:54
  12.0 5.0 %collective-permute-start.7 = (bf16[256,128]{1,0:T(8,128)(2,1)S(1)}, bf16[256,128]{1,0:T(8,128)(2,1)S(1)}, u32[]{:S(2)}, u32[]{:S(2)}) collective-permute-start(bf16[256,128]{1,0:T(8,128)(2,1)S(1)} %get-tuple-element.49), channel_id=1, source_target_pairs={{1,2},{5,6},{9,10},{13,14},{17,18},{21,22},{25,26},{29,30},{0,3},{... | collective-permute-start | bytes 196616 | tf_op jit(solution)/shard_map/ppermute | solution.py:54
  18.0 5.5 %collective-permute-start.10 = (bf16[16,128]{1,0:T(8,128)(2,1)S(1)}, bf16[16,128]{1,0:T(8,128)(2,1)S(1)}, u32[]{:S(2)}, u32[]{:S(2)}) collective-permute-start(bf16[16,128]{1,0:T(8,128)(2,1)S(1)} %get-tuple-element.54), channel_id=1, source_target_pairs={{0,1},{2,3},{4,5},{6,7},{8,9},{10,11},{12,13},{14,15},{16,17},{18,... | collective-permute-start | bytes 12296 | tf_op jit(solution)/shard_map/ppermute | solution.py:54
  18.1 5.5 %collective-permute-start.11 = (bf16[16,128]{1,0:T(8,128)(2,1)S(1)}, bf16[16,128]{1,0:T(8,128)(2,1)S(1)}, u32[]{:S(2)}, u32[]{:S(2)}) collective-permute-start(bf16[16,128]{1,0:T(8,128)(2,1)S(1)} %get-tuple-element.55), channel_id=1, source_target_pairs={{1,2},{5,6},{9,10},{13,14},{17,18},{21,22},{25,26},{29,30},{0,3},{... | collective-permute-start | bytes 12296 | tf_op jit(solution)/shard_map/ppermute | solution.py:54
  19.7 3.9 %collective-permute-start.8 = (bf16[16,128]{1,0:T(8,128)(2,1)S(1)}, bf16[16,128]{1,0:T(8,128)(2,1)S(1)}, u32[]{:S(2)}, u32[]{:S(2)}) collective-permute-start(bf16[16,128]{1,0:T(8,128)(2,1)S(1)} %get-tuple-element.52), channel_id=1, source_target_pairs={{0,4},{1,5},{2,6},{3,7},{8,12},{9,13},{10,14},{11,15},{16,20},{17,... | collective-permute-start | bytes 12296 | tf_op jit(solution)/shard_map/ppermute | solution.py:54
  21.3 4.5 %collective-permute-start.9 = (bf16[16,128]{1,0:T(8,128)(2,1)S(1)}, bf16[16,128]{1,0:T(8,128)(2,1)S(1)}, u32[]{:S(2)}, u32[]{:S(2)}) collective-permute-start(bf16[16,128]{1,0:T(8,128)(2,1)S(1)} %get-tuple-element.53), channel_id=1, source_target_pairs={{4,8},{5,9},{6,10},{7,11},{12,16},{13,17},{14,18},{15,19},{20,24},... | collective-permute-start | bytes 12296 | tf_op jit(solution)/shard_map/ppermute | solution.py:54

commit v3 on v2

--- a/solution.py
+++ b/solution.py
@@ -75,7 +75,7 @@
 
 def pack_kernel(
     mesh_dims, sends_far, guess_far, list_far, sat_far,
-    out0, out1, out2, out3, rounded,
+    out0, out1, out2, out3, extended,
     sends, guess, cell_list, sat, picked, arrivals,
 ):
     places = sides_of(*mesh_dims)
@@ -92,8 +92,8 @@
     ]
     for copy in copies + loads:
         copy.start()
-    copies[0].wait()
-    copies[1].wait()
+    for copy in copies:
+        copy.wait()
     blocks_sent = sends.shape[0]
     groups = sat.shape[0] // 4
     lists = cell_list.shape[0]
@@ -112,18 +112,36 @@
     for (side, _), out in zip(places, (out0, out1, out2, out3)):
         values = [picked[pl.ds(half * 4 + side, 1), :] for half in range(halves)]
         coarse = [value.astype(jnp.bfloat16).astype(jnp.float32) for value in values]
-        fine = [value - rounded_value for value, rounded_value in zip(values, coarse)]
+        fine = [value - rounded for value, rounded in zip(values, coarse)]
         blank = jnp.zeros((tail_rows - 2 * halves, lane_width), jnp.float32)
         out[pl.ds(blocks_sent * size, tail_rows), :] = jnp.concatenate(
             coarse + fine + [blank], 0
         ).astype(jnp.bfloat16)
+    listed = listed_blocks(sends, places)
     for block in range(blocks):
         loads[block].wait()
-        rounded[block] = guess[block].astype(jnp.bfloat16)
-    copies[2].wait()
-    for (side, _), out in zip(places, (out0, out1, out2, out3)):
-        for block in range(blocks_sent):
-            out[pl.ds(block * size, size), :] = rounded[sends[block, side]]
+        extended[block] = guess[block].astype(jnp.bfloat16)
+    for picks, out in zip(listed, (out0, out1, out2, out3)):
+        for slot, block in enumerate(picks):
+            out[pl.ds(slot * size, size), :] = extended[block]
+
+
+def listed_blocks(sends, places):
+    value = sends[...]
+    count = value.shape[0]
+    sides = [[value[slot, side] for slot in range(count)] for side in range(4)]
+    found = []
+    for pairing, (side, _) in enumerate(places):
+        first = 0 if pairing < 2 else 2
+        found.append(
+            [jnp.where(side == first, a, b) for a, b in zip(sides[first], sides[first + 1])]
+        )
+    return found
+
+
+def linked_blocks(links):
+    value = links[...]
+    return [[value[k, block] for k in range(2)] for block in range(value.shape[1])]
 
 
 def fetch_kernel(count, *refs):
@@ -136,6 +154,12 @@
         copy.start()
     for copy in copies:
         copy.wait()
+    links, sends = nears[-2][...], nears[-1][...]
+    for k, near in enumerate(refs[1 + 2 * count : -1]):
+        chosen = jnp.zeros_like(sends)
+        for block in range(links.shape[1]):
+            chosen = jnp.where(sends == block, links[k, block], chosen)
+        near[...] = chosen
 
 
 def product(left, right):
@@ -144,45 +168,48 @@
     )
 
 
-def relax(extended, links, couple, inverse, rhs, block):
-    near = jnp.concatenate([extended[links[0, block]], extended[links[1, block]]], 1)
-    matrix = jnp.concatenate([couple[block, 0], couple[block, 1]], 1)
-    resid = (rhs[block, 0 : near.shape[0], :] - product(near, matrix)).astype(jnp.bfloat16)
+def relax(extended, links, couple, inverse, rhs, block, rows):
+    near = jnp.concatenate([extended[link, 0:rows, :] for link in links], 1)
+    matrix = jnp.concatenate([couple[block, k] for k in range(len(links))], 1)
+    resid = (rhs[block, 0:rows, :] - product(near, matrix)).astype(jnp.bfloat16)
     return product(resid, inverse[block])
 
 
-def extend(extended, own, places, arrived, blocks_sent, size):
-    rows = extended.shape[1]
-    own_count = own.shape[0]
-    for block in range(own_count):
-        extended[block] = own[block, 0:rows, :]
+def land(extended, places, arrived, blocks_sent):
+    own_count = extended.shape[0] - 4 * blocks_sent
+    size = extended.shape[1]
     for (side, exists), came in zip(places, arrived):
         for block in range(blocks_sent):
-            value = came[pl.ds(block * size, rows), :]
+            value = came[pl.ds(block * size, size), :]
             value = jnp.where(exists, value, jnp.zeros_like(value))
             extended[own_count + side * blocks_sent + block] = value
 
 
 def first_edge_kernel(
-    mesh_dims, links, sends, own, in0, in1, in2, in3, couple, inverse, rhs,
+    mesh_dims, sends, near0, near1, _, in0, in1, in2, in3, couple, inverse, rhs,
     extended, out0, out1, out2, out3,
 ):
     places = sides_of(*mesh_dims)
-    size = own.shape[1]
-    blocks_sent = sends.shape[0]
-    extend(extended, own, places, (in0, in1, in2, in3), blocks_sent, size)
-    for (side, _), out in zip(places, (out0, out1, out2, out3)):
-        for block in range(blocks_sent):
-            fresh = relax(extended, links, couple, inverse, rhs, sends[block, side])
-            out[pl.ds(block * size, size), :] = fresh.astype(jnp.bfloat16)
-
-
-def look_up(table, first_row, rows, high, low):
-    value = jnp.zeros((8, lane_width), jnp.float32)
-    for row in range(rows):
+    size = extended.shape[1]
+    listed = listed_blocks(sends, places)
+    links = [listed_blocks(near, places) for near in (near0, near1)]
+    land(extended, places, (in0, in1, in2, in3), sends.shape[0])
+    for pairing, out in enumerate((out0, out1, out2, out3)):
+        for slot, block in enumerate(listed[pairing]):
+            pair = [links[k][pairing][slot] for k in range(2)]
+            fresh = relax(extended, pair, couple, inverse, rhs, block, size)
+            out[pl.ds(slot * size, size), :] = fresh.astype(jnp.bfloat16)
+
+
+def look_up(table, first_row, rows, high, low, value):
+    for row in rows:
         got = take_lanes(spread(table[pl.ds(first_row + row, 1), :]), low)
         value = jnp.where(high == row, got, value)
     return value
+
+
+def nothing():
+    return jnp.zeros((8, lane_width), jnp.float32)
 
 
 def first_sweep_kernel(
@@ -205,80 +232,83 @@
         across_rows[pl.ds(face * stride, groups), :] = (
             modes[0] + mode if face % 2 == 0 else modes[0] - mode
         )
-    for block in range(smoothed.shape[0]):
-        smoothed[block] = relax(extended, links, couple, inverse, rhs, block).astype(jnp.bfloat16)
+    for block, pair in enumerate(linked_blocks(links)):
+        fresh = relax(extended, pair, couple, inverse, rhs, block, extended.shape[1])
+        smoothed[block] = fresh.astype(jnp.bfloat16)
     for face in range(6):
         for start in range(0, groups, 8):
             index = neighbours[pl.ds(face * groups + start, 8), :]
             high, low = index >> 7, index & (lane_width - 1)
             if 0 < face < 4:
                 high = jnp.where(high >= groups, high - face * halves, high)
-            rows = groups + halves if face < 4 else groups
+            rows = range(groups + halves if face < 4 else groups)
             across[pl.ds(face * groups + start, 8), :] = look_up(
-                across_rows, face * stride, rows, high, low
+                across_rows, face * stride, rows, high, low, nothing()
             )
 
 
 def second_edge_kernel(
-    mesh_dims, links, sends, own, in0, in1, in2, in3, couple, inverse, rhs,
-    out0, out1, out2, out3, extended,
+    mesh_dims, sends, near0, near1, _, in0, in1, in2, in3, couple, inverse, rhs,
+    extended, out0, out1, out2, out3,
 ):
     places = sides_of(*mesh_dims)
-    size = own.shape[1]
-    blocks_sent = sends.shape[0]
-    extend(extended, own, places, (in0, in1, in2, in3), blocks_sent, size)
-    for (side, _), out in zip(places, (out0, out1, out2, out3)):
-        rows = [
-            relax(extended, links, couple, inverse, rhs, sends[block, side])[0:1, :]
-            for block in range(blocks_sent)
-        ]
-        blank = jnp.zeros((tail_rows - blocks_sent, lane_width), jnp.float32)
+    listed = listed_blocks(sends, places)
+    links = [listed_blocks(near, places) for near in (near0, near1)]
+    land(extended, places, (in0, in1, in2, in3), sends.shape[0])
+    for pairing, out in enumerate((out0, out1, out2, out3)):
+        rows = []
+        for slot, block in enumerate(listed[pairing]):
+            pair = [links[k][pairing][slot] for k in range(2)]
+            fresh = relax(extended, pair, couple, inverse, rhs, block, tail_rows)
+            rows.append(fresh[0:1, :])
+        blank = jnp.zeros((tail_rows - len(rows), lane_width), jnp.float32)
         out[...] = jnp.concatenate(rows + [blank], 0).astype(jnp.bfloat16)
 
 
 def second_sweep_kernel(
-    mesh_dims, links, own, in0, in1, in2, in3, couple, inverse, rhs,
-    traces, column, extended, fresh, departures,
-):
-    places = sides_of(*mesh_dims)
-    blocks, size = own.shape[0], own.shape[1]
-    blocks_sent = in0.shape[0] // size
-    extend(extended, own, places, (in0, in1, in2, in3), blocks_sent, size)
+    links, extended, couple, inverse, rhs, cell_faces,
+    traces, partial, fresh, column, departures,
+):
     stores = []
-    for block in range(blocks):
-        value = relax(extended, links, couple, inverse, rhs, block)
+    for block, pair in enumerate(linked_blocks(links)):
+        value = relax(extended, pair, couple, inverse, rhs, block, extended.shape[1])
         fresh[block] = value
         stores.append(
             pltpu.make_async_copy(fresh.at[block], traces.at[block], departures.at[block])
         )
         stores[block].start()
         column[pl.ds(block, 1), :] = value[0:1].astype(jnp.bfloat16).astype(jnp.float32)
+    for start in range(0, cell_faces.shape[0], 8):
+        index = cell_faces[pl.ds(start, 8), :]
+        rows = range(column.shape[0])
+        partial[pl.ds(start, 8), :] = look_up(
+            column, 0, rows, index >> 7, index & (lane_width - 1), nothing()
+        )
     for store in stores:
         store.wait()
 
 
 def cells_kernel(
-    mesh_dims, blocks_sent, column, in0, in1, in2, in3, across,
+    mesh_dims, blocks, blocks_sent, partial, in2, in3, in0, in1, across,
     cell_faces, coeff, source, flags, sat, ratio, out, faces,
 ):
     places = sides_of(*mesh_dims)
-    own_rows = column.shape[0]
-    face_rows = own_rows + 4 * blocks_sent
     groups = sat.shape[0] // 4
-    faces[pl.ds(0, own_rows), :] = column[...]
     for (side, exists), came in zip(places, (in0, in1, in2, in3)):
         value = came[...].astype(jnp.float32)[0:blocks_sent]
         value = jnp.where(exists, value, jnp.zeros_like(value))
         for block in range(blocks_sent):
-            faces[pl.ds(own_rows + side * blocks_sent + block, 1), :] = value[block : block + 1]
+            faces[pl.ds(side * blocks_sent + block, 1), :] = value[block : block + 1]
     modes = [sat[pl.ds(mode, groups, stride=4), :] for mode in range(4)]
     weights = [coeff[pl.ds(face * groups, groups), :] for face in range(6)]
     traces = []
     for face in range(6):
         parts = []
         for start in range(0, groups, 8):
-            index = cell_faces[pl.ds(face * groups + start, 8), :]
-            parts.append(look_up(faces, 0, face_rows, index >> 7, index & (lane_width - 1)))
+            rows = pl.ds(face * groups + start, 8)
+            index = cell_faces[rows, :]
+            high, low = (index >> 7) - blocks, index & (lane_width - 1)
+            parts.append(look_up(faces, 0, range(4 * blocks_sent), high, low, partial[rows, :]))
         traces.append(jnp.concatenate(parts, 0))
     total = weights[0]
     gained = source[...] + weights[0] * traces[0]
@@ -305,18 +335,18 @@
         )
 
 
-scalars = pl.BlockSpec(memory_space=pltpu.SMEM)
 whole = pl.BlockSpec(memory_space=pltpu.VMEM)
 far = pl.BlockSpec(memory_space=pl.ANY)
 
 
-def call(kernel, outs, specs, scratch=(), flops=0, traffic=0, out_specs=None):
+def call(kernel, outs, specs, scratch=(), flops=0, traffic=0, out_specs=None, aliases=None):
     return pl.pallas_call(
         kernel,
         out_shape=outs,
         in_specs=specs,
         out_specs=[whole] * len(outs) if out_specs is None else out_specs,
         scratch_shapes=list(scratch),
+        input_output_aliases=aliases or {},
         compiler_params=pltpu.CompilerParams(vmem_limit_bytes=vmem_bytes),
         cost_estimate=pl.CostEstimate(flops=flops, bytes_accessed=traffic, transcendentals=0),
     )
@@ -372,13 +402,14 @@
     def like(array):
         return jax.ShapeDtypeStruct(array.shape, array.dtype)
 
-    *packed, own = call(
+    widened = (extended_blocks, columns, size)
+    *packed, extended = call(
         functools.partial(pack_kernel, mesh_dims),
         [jax.ShapeDtypeStruct((halo_rows + tail_rows, size), half)] * 4
-        + [jax.ShapeDtypeStruct(guess.shape, half)],
+        + [jax.ShapeDtypeStruct(widened, half)],
         [far] * 4,
         [
-            pltpu.SMEM(sends.shape, jnp.int32),
+            pltpu.VMEM(sends.shape, jnp.int32),
             pltpu.VMEM(guess.shape, single),
             pltpu.VMEM(cell_list.shape, jnp.int32),
             pltpu.VMEM(sat.shape, single),
@@ -415,65 +446,64 @@
         ratio,
         links,
         sends,
+        near0,
+        near1,
     ) = call(
         functools.partial(fetch_kernel, len(remote)),
-        [like(array) for array in remote],
+        [like(array) for array in remote] + [like(sends)] * 2,
         [far] * (1 + len(remote)),
         [pltpu.SemaphoreType.DMA((len(remote),))],
         traffic=4 * guess.size,
-    )(own, *map(keep_far, remote))
+    )(packed[0], *map(keep_far, remote))
 
     sweep_flops = 6 * blocks * columns * size * size
     extended, *packed = call(
         functools.partial(first_edge_kernel, mesh_dims),
-        [jax.ShapeDtypeStruct((extended_blocks, columns, size), half)]
-        + [jax.ShapeDtypeStruct((halo_rows, size), half)] * 4,
-        [scalars, scalars] + [whole] * 8,
+        [like(extended)] + [jax.ShapeDtypeStruct((halo_rows, size), half)] * 4,
+        [whole] * 11,
         flops=sweep_flops // 2,
-    )(links, sends, own, *arrived, couple, inverse, rhs)
+        aliases={3: 0},
+    )(sends, near0, near1, extended, *arrived, couple, inverse, rhs)
     swept = trade(packed, plans)
 
     tails = [piece[halo_rows:] for piece in arrived]
     cell_rows = -(-(groups + halves) // 8) * 8
-    smoothed, across = call(
+    extended, across = call(
         functools.partial(first_sweep_kernel, mesh_dims, halves),
-        [like(own), jax.ShapeDtypeStruct(neighbours.shape, single)],
-        [scalars] + [whole] * 10,
+        [like(extended), jax.ShapeDtypeStruct(neighbours.shape, single)],
+        [whole] * 11,
         [pltpu.VMEM((6 * cell_rows, lane_width), single)],
         sweep_flops,
     )(links, extended, couple, inverse, rhs, sat, neighbours, *tails)
 
-    edges = trade(
-        call(
-            functools.partial(second_edge_kernel, mesh_dims),
-            [jax.ShapeDtypeStruct((tail_rows, size), half)] * 4,
-            [scalars, scalars] + [whole] * 8,
-            [pltpu.VMEM((extended_blocks, tail_rows, size), half)],
-            sweep_flops // 16,
-        )(links, sends, smoothed, *swept, couple, inverse, rhs),
-        plans,
-    )
-
-    traces, column = call(
-        functools.partial(second_sweep_kernel, mesh_dims),
-        [jax.ShapeDtypeStruct(guess.shape, single), jax.ShapeDtypeStruct((blocks, size), single)],
-        [scalars] + [whole] * 8,
+    extended, *packed = call(
+        functools.partial(second_edge_kernel, mesh_dims),
+        [like(extended)] + [jax.ShapeDtypeStruct((tail_rows, size), half)] * 4,
+        [whole] * 11,
+        flops=sweep_flops // 16,
+        aliases={3: 0},
+    )(sends, near0, near1, extended, *swept, couple, inverse, rhs)
+    edges = trade(packed, plans)
+
+    traces, partial = call(
+        second_sweep_kernel,
+        [jax.ShapeDtypeStruct(guess.shape, single), jax.ShapeDtypeStruct(coeff.shape, single)],
+        [whole] * 6,
         [
-            pltpu.VMEM((extended_blocks, columns, size), half),
             pltpu.VMEM(guess.shape, single),
+            pltpu.VMEM((blocks, size), single),
             pltpu.SemaphoreType.DMA((blocks,)),
         ],
         sweep_flops,
         out_specs=[far, whole],
-    )(links, smoothed, *swept, couple, inverse, rhs)
-
-    face_rows = -(-extended_blocks // 8) * 8
+    )(links, extended, couple, inverse, rhs, cell_faces)
+
     (following,) = call(
-        functools.partial(cells_kernel, mesh_dims, blocks_sent),
+        functools.partial(cells_kernel, mesh_dims, blocks, blocks_sent),
         [like(sat)],
         [whole] * 12,
-        [pltpu.VMEM((face_rows, lane_width), single)],
-    )(column, *edges, across, cell_faces, coeff, source, flags, sat, ratio)
+        [pltpu.VMEM((4 * blocks_sent, lane_width), single)],
+    )(partial, *edges[2:], *edges[:2], across, cell_faces, coeff, source, flags, sat, ratio)
     saturation_next = jnp.swapaxes(following.reshape(groups, 4, lane_width), 0, 1).reshape(4, -1)
     return traces[None, None], saturation_next[None, None]
 

time: 27.1 us -> 25 us (0.923)
  the two profiles are of different devices: /device:TPU:8 before, /device:TPU:5 now
where the time goes in v3:
time: 25 us; the launch traced here: 24.8 us
  starting transfers between devices  13.3 us (53%)
  Pallas kernels  8.08 us (32%)
  waiting for transfers between devices  2.58 us (10%)
  between operations  0.78 us (3%)
    ppermute x12, starting transfers between devices, trade(): lax.ppermute(piece, axes, plan)  13.3 us
    ppermute x12, waiting for transfers between devices, trade(): lax.ppermute(piece, axes, plan)  2.58 us
    pallas_call x1, Pallas kernels, per_device(): call(functools.partial(fetch_kernel, len(remote)), [like(array) for array...  1.96 us
    pallas_call x1, Pallas kernels, per_device(): call(second_sweep_kernel, [jax.ShapeDtypeStruct(guess.shape, single), jax...  1.67 us
    pallas_call x1, Pallas kernels, per_device(): call(functools.partial(pack_kernel, mesh_dims), [jax.ShapeDtypeStruct((ha...  1.47 us
    pallas_call x1, Pallas kernels, per_device(): call(functools.partial(first_sweep_kernel, mesh_dims, halves), [like(exte...  0.92 us
    pallas_call x1, Pallas kernels, per_device(): call(functools.partial(cells_kernel, mesh_dims, blocks, blocks_sent), [li...  0.88 us
    pallas_call x1, Pallas kernels, per_device(): call(functools.partial(first_edge_kernel, mesh_dims), [like(extended)] +...  0.63 us
  transfers between devices with their start and end apart: 12, of which 3 were waited for; matrix products, arithmetic and copies ran while one was open for 0% of the time, Pallas kernels for 18%

profile of v3, /device:TPU:5, one launch (start us, length us, event | category | flops | bytes accessed | tf_op | source)
XLA Modules:
  0.0 24.8 jit_solution(3022820772249518099)
XLA Ops:
  0.6 1.5 %shard_map.149 = (bf16[272,128]{1,0:T(8,128)(2,1)S(1)}, bf16[272,128]{1,0:T(8,128)(2,1)S(1)}, bf16[272,128]{1,0:T(8,128)(2,1)S(1)}, bf16[272,128]{1,0:T(8,128)(2,1)S(1)}, bf16[24,128,128]{2,1,0:T(8,128)(2,1)S(1)}) custom-call(s32[2,4]{1,0:T(2,128)} %bitcast.45, f32[16,128,128]{2,1,0:T(8,128)} %bitcast.34, s32[8,128]{1,0:T(8,128)} %bitcast.47, f32[64,128]{1,0:T(8,128)} %bitcast.36), custom_call_target="tpu_custom_call" | custom-call | tf_op jit(solution)/shard_map/pallas_call | solution.py:406
  2.1 0.1 collective-permute-start
  2.2 2.5 %collective-permute-start.1 = (bf16[272,128]{1,0:T(8,128)(2,1)S(1)}, bf16[272,128]{1,0:T(8,128)(2,1)S(1)}, u32[]{:S(2)}, u32[]{:S(2)}) collective-permute-start(bf16[272,128]{1,0:T(8,128)(2,1)S(1)} %get-tuple-element.41), channel_id=1, source_target_pairs={{4,8},{5,9},{6,10},{7,11},{12,16},{13,17},{14,18},{15,19},{20,24},... | collective-permute-start | bytes 208904 | tf_op jit(solution)/shard_map/ppermute | solution.py:54
  4.7 1.2 %collective-permute-start.2 = (bf16[272,128]{1,0:T(8,128)(2,1)S(1)}, bf16[272,128]{1,0:T(8,128)(2,1)S(1)}, u32[]{:S(2)}, u32[]{:S(2)}) collective-permute-start(bf16[272,128]{1,0:T(8,128)(2,1)S(1)} %get-tuple-element.42), channel_id=1, source_target_pairs={{0,1},{2,3},{4,5},{6,7},{8,9},{10,11},{12,13},{14,15},{16,17},{18,... | collective-permute-start | bytes 208904 | tf_op jit(solution)/shard_map/ppermute | solution.py:54
  5.9 1.1 %collective-permute-start.3 = (bf16[272,128]{1,0:T(8,128)(2,1)S(1)}, bf16[272,128]{1,0:T(8,128)(2,1)S(1)}, u32[]{:S(2)}, u32[]{:S(2)}) collective-permute-start(bf16[272,128]{1,0:T(8,128)(2,1)S(1)} %get-tuple-element.43), channel_id=1, source_target_pairs={{1,2},{5,6},{9,10},{13,14},{17,18},{21,22},{25,26},{29,30},{0,3},{... | collective-permute-start | bytes 208904 | tf_op jit(solution)/shard_map/ppermute | solution.py:54
  7.0 2.0 %shard_map.150 = (bf16[16,2,128,128]{3,2,1,0:T(8,128)(2,1)S(1)}, bf16[16,128,128]{2,1,0:T(8,128)(2,1)S(1)}, f32[16,128,128]{2,1,0:T(8,128)S(1)}, s32[96,128]{1,0...) custom-call(bf16[272,128]{1,0:T(8,128)(2,1)S(1)} %get-tuple-element., ...), custom_call_target="tpu_custom_call" | custom-call | bytes 1048576 | tf_op jit(solution)/shard_map/pallas_call | solution.py:451
  9.0 0.0 collective-permute-done.in0
  9.0 0.0 collective-permute-done.1.in1
  9.0 0.0 collective-permute-done.2.in2
  9.0 0.7 %collective-permute-done.3.in3 = bf16[272,128]{1,0:T(8,128)(2,1)S(1)} collective-permute-done((bf16[272,128]{1,0:T(8,128)(2,1)S(1)}, bf16[272,128]{1,0:T(8,128)(2,1)S(1)}, u32[]{:S(2)}, u32[]{:S(2)}) %collective-permute-start.3) | collective-permute-done | bytes 69664 | tf_op jit(solution)/shard_map/ppermute | solution.py:54
  9.7 0.6 %shard_map.151 = (bf16[24,128,128]{2,1,0:T(8,128)(2,1)S(1)}, bf16[256,128]{1,0:T(8,128)(2,1)S(1)}, bf16[256,128]{1,0:T(8,128)(2,1)S(1)}, bf16[256,128]{1,0:T(8,128)(2,1)S(1)}, bf16[256,128]{1,0:T(8,128)(2,1)S(1)}) custom-call(s32[2,4]{1,0:T(2,128)S(1)} %get-tuple-element.37.sends, ...), custom_call_target="tpu_custom_call", output_to_operand_aliasing={{0}: (3, {})} | custom-call | flops 100663296 | tf_op jit(solution)/shard_map/pallas_call | solution.py:460
  10.3 0.1 collective-permute-start.4
  10.4 2.5 %collective-permute-start.5 = (bf16[256,128]{1,0:T(8,128)(2,1)S(1)}, bf16[256,128]{1,0:T(8,128)(2,1)S(1)}, u32[]{:S(2)}, u32[]{:S(2)}) collective-permute-start(bf16[256,128]{1,0:T(8,128)(2,1)S(1)} %get-tuple-element.52), channel_id=1, source_target_pairs={{4,8},{5,9},{6,10},{7,11},{12,16},{13,17},{14,18},{15,19},{20,24},... | collective-permute-start | bytes 196616 | tf_op jit(solution)/shard_map/ppermute | solution.py:54
  12.9 0.6 %collective-permute-start.6 = (bf16[256,128]{1,0:T(8,128)(2,1)S(1)}, bf16[256,128]{1,0:T(8,128)(2,1)S(1)}, u32[]{:S(2)}, u32[]{:S(2)}) collective-permute-start(bf16[256,128]{1,0:T(8,128)(2,1)S(1)} %get-tuple-element.53), channel_id=1, source_target_pairs={{0,1},{2,3},{4,5},{6,7},{8,9},{10,11},{12,13},{14,15},{16,17},{18,... | collective-permute-start | bytes 196616 | tf_op jit(solution)/shard_map/ppermute | solution.py:54
  13.5 1.1 %collective-permute-start.7 = (bf16[256,128]{1,0:T(8,128)(2,1)S(1)}, bf16[256,128]{1,0:T(8,128)(2,1)S(1)}, u32[]{:S(2)}, u32[]{:S(2)}) collective-permute-start(bf16[256,128]{1,0:T(8,128)(2,1)S(1)} %get-tuple-element.54), channel_id=1, source_target_pairs={{1,2},{5,6},{9,10},{13,14},{17,18},{21,22},{25,26},{29,30},{0,3},{... | collective-permute-start | bytes 196616 | tf_op jit(solution)/shard_map/ppermute | solution.py:54
  14.6 0.9 %shard_map.152 = (bf16[24,128,128]{2,1,0:T(8,128)(2,1)S(1)}, f32[96,128]{1,0:T(8,128)S(1)}) custom-call(s32[2,16]{1,0:T(2,128)S(1)} %get-tuple-element.36.links, bf16[24,128,128]{2,1,0:T(8,128)(2,1)S(1)} %get-tuple-element.47.extended, bf16[16,2,128,128]{3,2,1,0:T(8,128)(2,1)S(1)} %get-tuple-element.44.couple, ...), custom_call_target="tpu_custom_call" | custom-call | flops 201326592 | tf_op jit(solution)/shard_map/pallas_call | solution.py:471
  15.5 0.0 collective-permute-done.4.in0
  15.5 0.0 collective-permute-done.5.in1
  15.5 0.0 collective-permute-done.6.in2
  15.5 1.6 %collective-permute-done.7.in3 = bf16[256,128]{1,0:T(8,128)(2,1)S(1)} collective-permute-done((bf16[256,128]{1,0:T(8,128)(2,1)S(1)}, bf16[256,128]{1,0:T(8,128)(2,1)S(1)}, u32[]{:S(2)}, u32[]{:S(2)}) %collective-permute-start.7) | collective-permute-done | bytes 65568 | tf_op jit(solution)/shard_map/ppermute | solution.py:54
  17.2 0.6 %shard_map.153 = (bf16[24,128,128]{2,1,0:T(8,128)(2,1)S(1)}, bf16[16,128]{1,0:T(8,128)(2,1)S(1)}, bf16[16,128]{1,0:T(8,128)(2,1)S(1)}, bf16[16,128]{1,0:T(8,128)(2,1)S(1)}, bf16[16,128]{1,0:T(8,128)(2,1)S(1)}) custom-call(s32[2,4]{1,0:T(2,128)S(1)} %get-tuple-element.37.sends, s32[2,4]{1,0:T(2,128)S(1)} %get-tuple-element.38.near0, ...), custom_call_target="tpu_custom_call", output_to_operand_aliasing={{0}: (3, {})} | custom-call | flops 12582912 | tf_op jit(solution)/shard_map/pallas_call | solution.py:479
  17.7 0.1 collective-permute-start.10
  17.8 2.5 %collective-permute-start.11 = (bf16[16,128]{1,0:T(8,128)(2,1)S(1)}, bf16[16,128]{1,0:T(8,128)(2,1)S(1)}, u32[]{:S(2)}, u32[]{:S(2)}) collective-permute-start(bf16[16,128]{1,0:T(8,128)(2,1)S(1)} %get-tuple-element.62), channel_id=1, source_target_pairs={{4,8},{5,9},{6,10},{7,11},{12,16},{13,17},{14,18},{15,19},{20,24},... | collective-permute-start | bytes 12296 | tf_op jit(solution)/shard_map/ppermute | solution.py:54
  20.3 0.6 %collective-permute-start.8 = (bf16[16,128]{1,0:T(8,128)(2,1)S(1)}, bf16[16,128]{1,0:T(8,128)(2,1)S(1)}, u32[]{:S(2)}, u32[]{:S(2)}) collective-permute-start(bf16[16,128]{1,0:T(8,128)(2,1)S(1)} %get-tuple-element.59), channel_id=1, source_target_pairs={{0,1},{2,3},{4,5},{6,7},{8,9},{10,11},{12,13},{14,15},{16,17},{18,... | collective-permute-start | bytes 12296 | tf_op jit(solution)/shard_map/ppermute | solution.py:54
  20.9 1.1 %collective-permute-start.9 = (bf16[16,128]{1,0:T(8,128)(2,1)S(1)}, bf16[16,128]{1,0:T(8,128)(2,1)S(1)}, u32[]{:S(2)}, u32[]{:S(2)}) collective-permute-start(bf16[16,128]{1,0:T(8,128)(2,1)S(1)} %get-tuple-element.60), channel_id=1, source_target_pairs={{1,2},{5,6},{9,10},{13,14},{17,18},{21,22},{25,26},{29,30},{0,3},{... | collective-permute-start | bytes 12296 | tf_op jit(solution)/shard_map/ppermute | solution.py:54
  22.0 1.7 %shard_map.154 = (f32[16,128,128]{2,1,0:T(8,128)}, f32[96,128]{1,0:T(8,128)S(1)}) custom-call(s32[2,16]{1,0:T(2,128)S(1)} %get-tuple-element.36.links, bf16[24,128,128]{2,1,0:T(8,128)(2,1)S(1)} %get-tuple-element.55.extended, bf16[16,2,128,128]{3,2,1,0:T(8,128)(2,1)S(1)} %get-tuple-element.44.couple, bf16[16,128,128]{2,1,0:T(8,128)(2,1)S(1)} %get-tuple-element.45.inverse, ...), custom_call_target="tpu_custom_call" | custom-call | flops 201326592 | tf_op jit(solution)/shard_map/pallas_call | solution.py:488
  23.7 0.0 collective-permute-done.10.in0
  23.7 0.0 collective-permute-done.11.in1
  23.7 0.0 collective-permute-done.8.in2
  23.7 0.2 collective-permute-done.9.in3
  23.9 0.9 %shard_map.155 = f32[64,128]{1,0:T(8,128)} custom-call(f32[96,128]{1,0:T(8,128)S(1)} %get-tuple-element.58.partial, bf16[16,128]{1,0:T(8,128)(2,1)S(1)} %collective-permute-done.8.in2, bf16[16,128]{1,0:T(8,128)(2,1)S(1)} %collective-permute-done.9.in3, bf16[16,128]{1,0:T(8,128)(2,1)S(1)} %collective-permute-done.10.in0, ...), custom_call_target="tpu_custom_call" | custom-call | tf_op jit(solution)/shard_map/pallas_call | solution.py:501
  (4 shorter events, 0.0 us)
Async XLA Ops:
  2.1 6.8 %collective-permute-start = (bf16[272,128]{1,0:T(8,128)(2,1)S(1)}, bf16[272,128]{1,0:T(8,128)(2,1)S(1)}, u32[]{:S(2)}, u32[]{:S(2)}) collective-permute-start(bf16[272,128]{1,0:T(8,128)(2,1)S(1)} %get-tuple-element.35.refs_0_), channel_id=1, source_target_pairs={{0,4},{1,5},{2,6},{3,7},{8,12},{9,13},{10,14},{11,15},{16,20},{17,... | collective-permute-start | bytes 208904 | tf_op jit(solution)/shard_map/ppermute | solution.py:54
  2.2 6.8 %collective-permute-start.1 = (bf16[272,128]{1,0:T(8,128)(2,1)S(1)}, bf16[272,128]{1,0:T(8,128)(2,1)S(1)}, u32[]{:S(2)}, u32[]{:S(2)}) collective-permute-start(bf16[272,128]{1,0:T(8,128)(2,1)S(1)} %get-tuple-element.41), channel_id=1, source_target_pairs={{4,8},{5,9},{6,10},{7,11},{12,16},{13,17},{14,18},{15,19},{20,24},... | collective-permute-start | bytes 208904 | tf_op jit(solution)/shard_map/ppermute | solution.py:54
  4.7 4.3 %collective-permute-start.2 = (bf16[272,128]{1,0:T(8,128)(2,1)S(1)}, bf16[272,128]{1,0:T(8,128)(2,1)S(1)}, u32[]{:S(2)}, u32[]{:S(2)}) collective-permute-start(bf16[272,128]{1,0:T(8,128)(2,1)S(1)} %get-tuple-element.42), channel_id=1, source_target_pairs={{0,1},{2,3},{4,5},{6,7},{8,9},{10,11},{12,13},{14,15},{16,17},{18,... | collective-permute-start | bytes 208904 | tf_op jit(solution)/shard_map/ppermute | solution.py:54
  5.9 3.8 %collective-permute-start.3 = (bf16[272,128]{1,0:T(8,128)(2,1)S(1)}, bf16[272,128]{1,0:T(8,128)(2,1)S(1)}, u32[]{:S(2)}, u32[]{:S(2)}) collective-permute-start(bf16[272,128]{1,0:T(8,128)(2,1)S(1)} %get-tuple-element.43), channel_id=1, source_target_pairs={{1,2},{5,6},{9,10},{13,14},{17,18},{21,22},{25,26},{29,30},{0,3},{... | collective-permute-start | bytes 208904 | tf_op jit(solution)/shard_map/ppermute | solution.py:54
  10.3 5.2 %collective-permute-start.4 = (bf16[256,128]{1,0:T(8,128)(2,1)S(1)}, bf16[256,128]{1,0:T(8,128)(2,1)S(1)}, u32[]{:S(2)}, u32[]{:S(2)}) collective-permute-start(bf16[256,128]{1,0:T(8,128)(2,1)S(1)} %get-tuple-element.51), channel_id=1, source_target_pairs={{0,4},{1,5},{2,6},{3,7},{8,12},{9,13},{10,14},{11,15},{16,20},{17,... | collective-permute-start | bytes 196616 | tf_op jit(solution)/shard_map/ppermute | solution.py:54
  10.4 5.1 %collective-permute-start.5 = (bf16[256,128]{1,0:T(8,128)(2,1)S(1)}, bf16[256,128]{1,0:T(8,128)(2,1)S(1)}, u32[]{:S(2)}, u32[]{:S(2)}) collective-permute-start(bf16[256,128]{1,0:T(8,128)(2,1)S(1)} %get-tuple-element.52), channel_id=1, source_target_pairs={{4,8},{5,9},{6,10},{7,11},{12,16},{13,17},{14,18},{15,19},{20,24},... | collective-permute-start | bytes 196616 | tf_op jit(solution)/shard_map/ppermute | solution.py:54
  12.9 2.7 %collective-permute-start.6 = (bf16[256,128]{1,0:T(8,128)(2,1)S(1)}, bf16[256,128]{1,0:T(8,128)(2,1)S(1)}, u32[]{:S(2)}, u32[]{:S(2)}) collective-permute-start(bf16[256,128]{1,0:T(8,128)(2,1)S(1)} %get-tuple-element.53), channel_id=1, source_target_pairs={{0,1},{2,3},{4,5},{6,7},{8,9},{10,11},{12,13},{14,15},{16,17},{18,... | collective-permute-start | bytes 196616 | tf_op jit(solution)/shard_map/ppermute | solution.py:54
  13.5 3.7 %collective-permute-start.7 = (bf16[256,128]{1,0:T(8,128)(2,1)S(1)}, bf16[256,128]{1,0:T(8,128)(2,1)S(1)}, u32[]{:S(2)}, u32[]{:S(2)}) collective-permute-start(bf16[256,128]{1,0:T(8,128)(2,1)S(1)} %get-tuple-element.54), channel_id=1, source_target_pairs={{1,2},{5,6},{9,10},{13,14},{17,18},{21,22},{25,26},{29,30},{0,3},{... | collective-permute-start | bytes 196616 | tf_op jit(solution)/shard_map/ppermute | solution.py:54
  17.7 5.9 %collective-permute-start.10 = (bf16[16,128]{1,0:T(8,128)(2,1)S(1)}, bf16[16,128]{1,0:T(8,128)(2,1)S(1)}, u32[]{:S(2)}, u32[]{:S(2)}) collective-permute-start(bf16[16,128]{1,0:T(8,128)(2,1)S(1)} %get-tuple-element.61), channel_id=1, source_target_pairs={{0,4},{1,5},{2,6},{3,7},{8,12},{9,13},{10,14},{11,15},{16,20},{17,... | collective-permute-start | bytes 12296 | tf_op jit(solution)/shard_map/ppermute | solution.py:54
  17.8 5.9 %collective-permute-start.11 = (bf16[16,128]{1,0:T(8,128)(2,1)S(1)}, bf16[16,128]{1,0:T(8,128)(2,1)S(1)}, u32[]{:S(2)}, u32[]{:S(2)}) collective-permute-start(bf16[16,128]{1,0:T(8,128)(2,1)S(1)} %get-tuple-element.62), channel_id=1, source_target_pairs={{4,8},{5,9},{6,10},{7,11},{12,16},{13,17},{14,18},{15,19},{20,24},... | collective-permute-start | bytes 12296 | tf_op jit(solution)/shard_map/ppermute | solution.py:54
  20.3 3.4 %collective-permute-start.8 = (bf16[16,128]{1,0:T(8,128)(2,1)S(1)}, bf16[16,128]{1,0:T(8,128)(2,1)S(1)}, u32[]{:S(2)}, u32[]{:S(2)}) collective-permute-start(bf16[16,128]{1,0:T(8,128)(2,1)S(1)} %get-tuple-element.59), channel_id=1, source_target_pairs={{0,1},{2,3},{4,5},{6,7},{8,9},{10,11},{12,13},{14,15},{16,17},{18,... | collective-permute-start | bytes 12296 | tf_op jit(solution)/shard_map/ppermute | solution.py:54
  20.9 3.0 %collective-permute-start.9 = (bf16[16,128]{1,0:T(8,128)(2,1)S(1)}, bf16[16,128]{1,0:T(8,128)(2,1)S(1)}, u32[]{:S(2)}, u32[]{:S(2)}) collective-permute-start(bf16[16,128]{1,0:T(8,128)(2,1)S(1)} %get-tuple-element.60), channel_id=1, source_target_pairs={{1,2},{5,6},{9,10},{13,14},{17,18},{21,22},{25,26},{29,30},{0,3},{... | collective-permute-start | bytes 12296 | tf_op jit(solution)/shard_map/ppermute | solution.py:54

commit v4 on v3

--- a/solution.py
+++ b/solution.py
@@ -75,8 +75,8 @@
 
 def pack_kernel(
     mesh_dims, sends_far, guess_far, list_far, sat_far,
-    out0, out1, out2, out3, extended,
-    sends, guess, cell_list, sat, picked, arrivals,
+    out0, out1, out2, out3, guess,
+    sends, cell_list, sat, picked, arrivals,
 ):
     places = sides_of(*mesh_dims)
     blocks, size = guess.shape[0], guess.shape[1]
@@ -118,12 +118,11 @@
             coarse + fine + [blank], 0
         ).astype(jnp.bfloat16)
     listed = listed_blocks(sends, places)
-    for block in range(blocks):
-        loads[block].wait()
-        extended[block] = guess[block].astype(jnp.bfloat16)
+    for load in loads:
+        load.wait()
     for picks, out in zip(listed, (out0, out1, out2, out3)):
         for slot, block in enumerate(picks):
-            out[pl.ds(slot * size, size), :] = extended[block]
+            out[pl.ds(slot * size, size), :] = guess[block].astype(jnp.bfloat16)
 
 
 def listed_blocks(sends, places):
@@ -139,23 +138,39 @@
     return found
 
 
+def flatten(listed, links):
+    near0, near1 = links
+    blocks = [block for picks in listed for block in picks]
+    pairs = [pair for picks in zip(near0, near1) for pair in zip(*picks)]
+    return blocks, pairs
+
+
 def linked_blocks(links):
     value = links[...]
     return [[value[k, block] for k in range(2)] for block in range(value.shape[1])]
 
 
+def in_parts(links):
+    pairs = linked_blocks(links)
+    for start in range(0, len(pairs), 8):
+        yield range(start, min(start + 8, len(pairs))), pairs[start : start + 8]
+
+
 def fetch_kernel(count, *refs):
-    fars, nears, arrivals = refs[1 : 1 + count], refs[1 + count : 1 + 2 * count], refs[-1]
+    guess, fars, nears = refs[0], refs[1 : 1 + count], refs[1 + count : 1 + 2 * count]
+    near0, near1, extended, arrivals = refs[1 + 2 * count :]
     copies = [
         pltpu.make_async_copy(far, near, arrivals.at[slot])
         for slot, (far, near) in enumerate(zip(fars, nears))
     ]
     for copy in copies:
         copy.start()
+    for block in range(guess.shape[0]):
+        extended[block] = guess[block].astype(jnp.bfloat16)
     for copy in copies:
         copy.wait()
     links, sends = nears[-2][...], nears[-1][...]
-    for k, near in enumerate(refs[1 + 2 * count : -1]):
+    for k, near in enumerate((near0, near1)):
         chosen = jnp.zeros_like(sends)
         for block in range(links.shape[1]):
             chosen = jnp.where(sends == block, links[k, block], chosen)
@@ -168,11 +183,13 @@
     )
 
 
-def relax(extended, links, couple, inverse, rhs, block, rows):
-    near = jnp.concatenate([extended[link, 0:rows, :] for link in links], 1)
-    matrix = jnp.concatenate([couple[block, k] for k in range(len(links))], 1)
-    resid = (rhs[block, 0:rows, :] - product(near, matrix)).astype(jnp.bfloat16)
-    return product(resid, inverse[block])
+def relax(extended, couple, inverse, rhs, blocks, links, rows):
+    resid = []
+    for block, pair in zip(blocks, links):
+        near = jnp.concatenate([extended[link, 0:rows, :] for link in pair], 1)
+        matrix = jnp.concatenate([couple[block, k] for k in range(len(pair))], 1)
+        resid.append((rhs[block, 0:rows, :] - product(near, matrix)).astype(jnp.bfloat16))
+    return [product(part, inverse[block]) for part, block in zip(resid, blocks)]
 
 
 def land(extended, places, arrived, blocks_sent):
@@ -194,11 +211,12 @@
     listed = listed_blocks(sends, places)
     links = [listed_blocks(near, places) for near in (near0, near1)]
     land(extended, places, (in0, in1, in2, in3), sends.shape[0])
+    fresh = relax(extended, couple, inverse, rhs, *flatten(listed, links), size)
+    slots = sends.shape[0]
     for pairing, out in enumerate((out0, out1, out2, out3)):
-        for slot, block in enumerate(listed[pairing]):
-            pair = [links[k][pairing][slot] for k in range(2)]
-            fresh = relax(extended, pair, couple, inverse, rhs, block, size)
-            out[pl.ds(slot * size, size), :] = fresh.astype(jnp.bfloat16)
+        for slot in range(slots):
+            value = fresh[pairing * slots + slot]
+            out[pl.ds(slot * size, size), :] = value.astype(jnp.bfloat16)
 
 
 def look_up(table, first_row, rows, high, low, value):
@@ -232,9 +250,10 @@
         across_rows[pl.ds(face * stride, groups), :] = (
             modes[0] + mode if face % 2 == 0 else modes[0] - mode
         )
-    for block, pair in enumerate(linked_blocks(links)):
-        fresh = relax(extended, pair, couple, inverse, rhs, block, extended.shape[1])
-        smoothed[block] = fresh.astype(jnp.bfloat16)
+    for blocks, pairs in in_parts(links):
+        fresh = relax(extended, couple, inverse, rhs, blocks, pairs, extended.shape[1])
+        for block, value in zip(blocks, fresh):
+            smoothed[block] = value.astype(jnp.bfloat16)
     for face in range(6):
         for start in range(0, groups, 8):
             index = neighbours[pl.ds(face * groups + start, 8), :]
@@ -248,19 +267,17 @@
 
 
 def second_edge_kernel(
-    mesh_dims, sends, near0, near1, _, in0, in1, in2, in3, couple, inverse, rhs,
+    mesh_dims, sends, near0, near1, _, in1, in0, in3, in2, couple, inverse, rhs,
     extended, out0, out1, out2, out3,
 ):
     places = sides_of(*mesh_dims)
     listed = listed_blocks(sends, places)
     links = [listed_blocks(near, places) for near in (near0, near1)]
     land(extended, places, (in0, in1, in2, in3), sends.shape[0])
+    fresh = relax(extended, couple, inverse, rhs, *flatten(listed, links), tail_rows)
+    slots = sends.shape[0]
     for pairing, out in enumerate((out0, out1, out2, out3)):
-        rows = []
-        for slot, block in enumerate(listed[pairing]):
-            pair = [links[k][pairing][slot] for k in range(2)]
-            fresh = relax(extended, pair, couple, inverse, rhs, block, tail_rows)
-            rows.append(fresh[0:1, :])
+        rows = [fresh[pairing * slots + slot][0:1, :] for slot in range(slots)]
         blank = jnp.zeros((tail_rows - len(rows), lane_width), jnp.float32)
         out[...] = jnp.concatenate(rows + [blank], 0).astype(jnp.bfloat16)
 
@@ -270,14 +287,15 @@
     traces, partial, fresh, column, departures,
 ):
     stores = []
-    for block, pair in enumerate(linked_blocks(links)):
-        value = relax(extended, pair, couple, inverse, rhs, block, extended.shape[1])
-        fresh[block] = value
-        stores.append(
-            pltpu.make_async_copy(fresh.at[block], traces.at[block], departures.at[block])
-        )
-        stores[block].start()
-        column[pl.ds(block, 1), :] = value[0:1].astype(jnp.bfloat16).astype(jnp.float32)
+    for blocks, pairs in in_parts(links):
+        values = relax(extended, couple, inverse, rhs, blocks, pairs, extended.shape[1])
+        for block, value in zip(blocks, values):
+            fresh[block] = value
+            stores.append(
+                pltpu.make_async_copy(fresh.at[block], traces.at[block], departures.at[block])
+            )
+            stores[block].start()
+            column[pl.ds(block, 1), :] = value[0:1].astype(jnp.bfloat16).astype(jnp.float32)
     for start in range(0, cell_faces.shape[0], 8):
         index = cell_faces[pl.ds(start, 8), :]
         rows = range(column.shape[0])
@@ -289,7 +307,7 @@
 
 
 def cells_kernel(
-    mesh_dims, blocks, blocks_sent, partial, in2, in3, in0, in1, across,
+    mesh_dims, blocks, blocks_sent, partial, in1, in3, in0, in2, across,
     cell_faces, coeff, source, flags, sat, ratio, out, faces,
 ):
     places = sides_of(*mesh_dims)
@@ -403,14 +421,12 @@
         return jax.ShapeDtypeStruct(array.shape, array.dtype)
 
     widened = (extended_blocks, columns, size)
-    *packed, extended = call(
+    *packed, guess = call(
         functools.partial(pack_kernel, mesh_dims),
-        [jax.ShapeDtypeStruct((halo_rows + tail_rows, size), half)] * 4
-        + [jax.ShapeDtypeStruct(widened, half)],
+        [jax.ShapeDtypeStruct((halo_rows + tail_rows, size), half)] * 4 + [like(guess)],
         [far] * 4,
         [
             pltpu.VMEM(sends.shape, jnp.int32),
-            pltpu.VMEM(guess.shape, single),
             pltpu.VMEM(cell_list.shape, jnp.int32),
             pltpu.VMEM(sat.shape, single),
             pltpu.VMEM((4 * halves, lane_width), single),
@@ -448,13 +464,16 @@
         sends,
         near0,
         near1,
+        extended,
     ) = call(
         functools.partial(fetch_kernel, len(remote)),
-        [like(array) for array in remote] + [like(sends)] * 2,
-        [far] * (1 + len(remote)),
+        [like(array) for array in remote]
+        + [like(sends)] * 2
+        + [jax.ShapeDtypeStruct(widened, half)],
+        [whole] + [far] * len(remote),
         [pltpu.SemaphoreType.DMA((len(remote),))],
         traffic=4 * guess.size,
-    )(packed[0], *map(keep_far, remote))
+    )(guess, *map(keep_far, remote))
 
     sweep_flops = 6 * blocks * columns * size * size
     extended, *packed = call(
@@ -482,7 +501,7 @@
         [whole] * 11,
         flops=sweep_flops // 16,
         aliases={3: 0},
-    )(sends, near0, near1, extended, *swept, couple, inverse, rhs)
+    )(sends, near0, near1, extended, *(swept[k] for k in (1, 0, 3, 2)), couple, inverse, rhs)
     edges = trade(packed, plans)
 
     traces, partial = call(
@@ -503,7 +522,7 @@
         [like(sat)],
         [whole] * 12,
         [pltpu.VMEM((4 * blocks_sent, lane_width), single)],
-    )(partial, *edges[2:], *edges[:2], across, cell_faces, coeff, source, flags, sat, ratio)
+    )(partial, *(edges[k] for k in (1, 3, 0, 2)), across, cell_faces, coeff, source, flags, sat, ratio)
     saturation_next = jnp.swapaxes(following.reshape(groups, 4, lane_width), 0, 1).reshape(4, -1)
     return traces[None, None], saturation_next[None, None]
 

time: 25 us -> 24.1 us (0.964)
  starting transfers between devices: 13.3 us -> 12.6 us
    ppermute x12, starting transfers between devices: 13.3 us -> 12.6 us  [trade(): lax.ppermute(piece, axes, plan)]
  transfers between devices with their start and end apart: 12 -> 12, of which waited for: 3 -> 3; matrix products, arithmetic and copies ran while one was open for 0% -> 0% of each run, Pallas kernels for 18% -> 19%
where the time goes in v4:
time: 24.1 us; the launch traced here: 23.9 us
  starting transfers between devices  12.6 us (52%)
  Pallas kernels  7.85 us (33%)
  waiting for transfers between devices  2.73 us (11%)
  between operations  0.76 us (3%)
    ppermute x12, starting transfers between devices, trade(): lax.ppermute(piece, axes, plan)  12.6 us
    ppermute x12, waiting for transfers between devices, trade(): lax.ppermute(piece, axes, plan)  2.73 us
    pallas_call x1, Pallas kernels, per_device(): call(functools.partial(fetch_kernel, len(remote)), [like(array) for array...  1.96 us
    pallas_call x1, Pallas kernels, per_device(): call(second_sweep_kernel, [jax.ShapeDtypeStruct(guess.shape, single), jax...  1.65 us
    pallas_call x1, Pallas kernels, per_device(): call(functools.partial(pack_kernel, mesh_dims), [jax.ShapeDtypeStruct((ha...  1.47 us
    pallas_call x1, Pallas kernels, per_device(): call(functools.partial(cells_kernel, mesh_dims, blocks, blocks_sent), [li...  0.89 us
    pallas_call x1, Pallas kernels, per_device(): call(functools.partial(first_sweep_kernel, mesh_dims, halves), [like(exte...  0.86 us
    pallas_call x1, Pallas kernels, per_device(): call(functools.partial(first_edge_kernel, mesh_dims), [like(extended)] +...  0.55 us
  transfers between devices with their start and end apart: 12, of which 3 were waited for; matrix products, arithmetic and copies ran while one was open for 0% of the time, Pallas kernels for 19%

profile of v4, /device:TPU:5, one launch (start us, length us, event | category | flops | bytes accessed | tf_op | source)
XLA Modules:
  0.0 23.9 jit_solution(11287402030607767626)
XLA Ops:
  0.6 1.5 %shard_map.149 = (bf16[272,128]{1,0:T(8,128)(2,1)S(1)}, bf16[272,128]{1,0:T(8,128)(2,1)S(1)}, bf16[272,128]{1,0:T(8,128)(2,1)S(1)}, bf16[272,128]{1,0:T(8,128)(2,1)S(1)}, f32[16,128,128]{2,1,0:T(8,128)S(1)}) custom-call(s32[2,4]{1,0:T(2,128)} %bitcast.46, f32[16,128,128]{2,1,0:T(8,128)} %bitcast.34, s32[8,128]{1,0:T(8,128)} %bitcast.45, f32[64,128]{1,0:T(8,128)} %bitcast.36), custom_call_target="tpu_custom_call" | custom-call | tf_op jit(solution)/shard_map/pallas_call | solution.py:424
  2.1 0.1 collective-permute-start
  2.2 2.5 %collective-permute-start.1 = (bf16[272,128]{1,0:T(8,128)(2,1)S(1)}, bf16[272,128]{1,0:T(8,128)(2,1)S(1)}, u32[]{:S(2)}, u32[]{:S(2)}) collective-permute-start(bf16[272,128]{1,0:T(8,128)(2,1)S(1)} %get-tuple-element.43), channel_id=1, source_target_pairs={{4,8},{5,9},{6,10},{7,11},{12,16},{13,17},{14,18},{15,19},{20,24},... | collective-permute-start | bytes 208904 | tf_op jit(solution)/shard_map/ppermute | solution.py:54
  4.7 1.2 %collective-permute-start.2 = (bf16[272,128]{1,0:T(8,128)(2,1)S(1)}, bf16[272,128]{1,0:T(8,128)(2,1)S(1)}, u32[]{:S(2)}, u32[]{:S(2)}) collective-permute-start(bf16[272,128]{1,0:T(8,128)(2,1)S(1)} %get-tuple-element.44), channel_id=1, source_target_pairs={{0,1},{2,3},{4,5},{6,7},{8,9},{10,11},{12,13},{14,15},{16,17},{18,... | collective-permute-start | bytes 208904 | tf_op jit(solution)/shard_map/ppermute | solution.py:54
  5.9 1.1 %collective-permute-start.3 = (bf16[272,128]{1,0:T(8,128)(2,1)S(1)}, bf16[272,128]{1,0:T(8,128)(2,1)S(1)}, u32[]{:S(2)}, u32[]{:S(2)}) collective-permute-start(bf16[272,128]{1,0:T(8,128)(2,1)S(1)} %get-tuple-element.45), channel_id=1, source_target_pairs={{1,2},{5,6},{9,10},{13,14},{17,18},{21,22},{25,26},{29,30},{0,3},{... | collective-permute-start | bytes 208904 | tf_op jit(solution)/shard_map/ppermute | solution.py:54
  7.0 2.0 %shard_map.150 = (bf16[16,2,128,128]{3,2,1,0:T(8,128)(2,1)S(1)}, bf16[16,128,128]{2,1,0:T(8,128)(2,1)S(1)}, f32[16,128,128]{2,1,0:T(8,128)S(1)}, s32[96,128]{1,0...) custom-call(f32[16,128,128]{2,1,0:T(8,128)S(1)} %get-tuple-element.3, ...), custom_call_target="tpu_custom_call" | custom-call | bytes 1048576 | tf_op jit(solution)/shard_map/pallas_call | solution.py:468
  9.0 0.0 collective-permute-done.in0
  9.0 0.0 collective-permute-done.1.in1
  9.0 0.0 collective-permute-done.2.in2
  9.0 0.7 %collective-permute-done.3.in3 = bf16[272,128]{1,0:T(8,128)(2,1)S(1)} collective-permute-done((bf16[272,128]{1,0:T(8,128)(2,1)S(1)}, bf16[272,128]{1,0:T(8,128)(2,1)S(1)}, u32[]{:S(2)}, u32[]{:S(2)}) %collective-permute-start.3) | collective-permute-done | bytes 69664 | tf_op jit(solution)/shard_map/ppermute | solution.py:54
  9.7 0.6 %shard_map.151 = (bf16[24,128,128]{2,1,0:T(8,128)(2,1)S(1)}, bf16[256,128]{1,0:T(8,128)(2,1)S(1)}, bf16[256,128]{1,0:T(8,128)(2,1)S(1)}, bf16[256,128]{1,0:T(8,128)(2,1)S(1)}, bf16[256,128]{1,0:T(8,128)(2,1)S(1)}) custom-call(s32[2,4]{1,0:T(2,128)S(1)} %get-tuple-element.38.sends, ...), custom_call_target="tpu_custom_call", output_to_operand_aliasing={{0}: (3, {})} | custom-call | flops 100663296 | tf_op jit(solution)/shard_map/pallas_call | solution.py:479
  10.2 0.3 %collective-permute-start.4 = (bf16[256,128]{1,0:T(8,128)(2,1)S(1)}, bf16[256,128]{1,0:T(8,128)(2,1)S(1)}, u32[]{:S(2)}, u32[]{:S(2)}) collective-permute-start(bf16[256,128]{1,0:T(8,128)(2,1)S(1)} %get-tuple-element.53), channel_id=1, source_target_pairs={{4,8},{5,9},{6,10},{7,11},{12,16},{13,17},{14,18},{15,19},{20,24},... | collective-permute-start | bytes 196616 | tf_op jit(solution)/shard_map/ppermute | solution.py:54
  10.6 0.0 collective-permute-start.5
  10.6 2.3 %collective-permute-start.6 = (bf16[256,128]{1,0:T(8,128)(2,1)S(1)}, bf16[256,128]{1,0:T(8,128)(2,1)S(1)}, u32[]{:S(2)}, u32[]{:S(2)}) collective-permute-start(bf16[256,128]{1,0:T(8,128)(2,1)S(1)} %get-tuple-element.55), channel_id=1, source_target_pairs={{1,2},{5,6},{9,10},{13,14},{17,18},{21,22},{25,26},{29,30},{0,3},{... | collective-permute-start | bytes 196616 | tf_op jit(solution)/shard_map/ppermute | solution.py:54
  12.8 0.0 collective-permute-start.7
  12.9 0.9 %shard_map.152 = (bf16[24,128,128]{2,1,0:T(8,128)(2,1)S(1)}, f32[96,128]{1,0:T(8,128)S(1)}) custom-call(s32[2,16]{1,0:T(2,128)S(1)} %get-tuple-element.37.links, bf16[24,128,128]{2,1,0:T(8,128)(2,1)S(1)} %get-tuple-element.49.extended, bf16[16,2,128,128]{3,2,1,0:T(8,128)(2,1)S(1)} %get-tuple-element.46.couple, ...), custom_call_target="tpu_custom_call" | custom-call | flops 201326592 | tf_op jit(solution)/shard_map/pallas_call | solution.py:490
  13.7 1.2 %collective-permute-done.4.in1 = bf16[256,128]{1,0:T(8,128)(2,1)S(1)} collective-permute-done((bf16[256,128]{1,0:T(8,128)(2,1)S(1)}, bf16[256,128]{1,0:T(8,128)(2,1)S(1)}, u32[]{:S(2)}, u32[]{:S(2)}) %collective-permute-start.4) | collective-permute-done | bytes 65568 | tf_op jit(solution)/shard_map/ppermute | solution.py:54
  14.9 0.0 collective-permute-done.5.in0
  14.9 0.8 %collective-permute-done.6.in3 = bf16[256,128]{1,0:T(8,128)(2,1)S(1)} collective-permute-done((bf16[256,128]{1,0:T(8,128)(2,1)S(1)}, bf16[256,128]{1,0:T(8,128)(2,1)S(1)}, u32[]{:S(2)}, u32[]{:S(2)}) %collective-permute-start.6) | collective-permute-done | bytes 65568 | tf_op jit(solution)/shard_map/ppermute | solution.py:54
  15.7 0.0 collective-permute-done.7.in2
  15.7 0.5 %shard_map.153 = (bf16[24,128,128]{2,1,0:T(8,128)(2,1)S(1)}, bf16[16,128]{1,0:T(8,128)(2,1)S(1)}, bf16[16,128]{1,0:T(8,128)(2,1)S(1)}, bf16[16,128]{1,0:T(8,128)(2,1)S(1)}, bf16[16,128]{1,0:T(8,128)(2,1)S(1)}) custom-call(s32[2,4]{1,0:T(2,128)S(1)} %get-tuple-element.38.sends, s32[2,4]{1,0:T(2,128)S(1)} %get-tuple-element.39.near0, ...), custom_call_target="tpu_custom_call", output_to_operand_aliasing={{0}: (3, {})} | custom-call | flops 12582912 | tf_op jit(solution)/shard_map/pallas_call | solution.py:498
  16.2 1.8 %collective-permute-start.10 = (bf16[16,128]{1,0:T(8,128)(2,1)S(1)}, bf16[16,128]{1,0:T(8,128)(2,1)S(1)}, u32[]{:S(2)}, u32[]{:S(2)}) collective-permute-start(bf16[16,128]{1,0:T(8,128)(2,1)S(1)} %get-tuple-element.63), channel_id=1, source_target_pairs={{0,4},{1,5},{2,6},{3,7},{8,12},{9,13},{10,14},{11,15},{16,20},{17,... | collective-permute-start | bytes 12296 | tf_op jit(solution)/shard_map/ppermute | solution.py:54
  18.0 0.7 %collective-permute-start.11 = (bf16[16,128]{1,0:T(8,128)(2,1)S(1)}, bf16[16,128]{1,0:T(8,128)(2,1)S(1)}, u32[]{:S(2)}, u32[]{:S(2)}) collective-permute-start(bf16[16,128]{1,0:T(8,128)(2,1)S(1)} %get-tuple-element.64), channel_id=1, source_target_pairs={{0,1},{2,3},{4,5},{6,7},{8,9},{10,11},{12,13},{14,15},{16,17},{18,... | collective-permute-start | bytes 12296 | tf_op jit(solution)/shard_map/ppermute | solution.py:54
  18.6 1.3 %collective-permute-start.8 = (bf16[16,128]{1,0:T(8,128)(2,1)S(1)}, bf16[16,128]{1,0:T(8,128)(2,1)S(1)}, u32[]{:S(2)}, u32[]{:S(2)}) collective-permute-start(bf16[16,128]{1,0:T(8,128)(2,1)S(1)} %get-tuple-element.61), channel_id=1, source_target_pairs={{4,8},{5,9},{6,10},{7,11},{12,16},{13,17},{14,18},{15,19},{20,24},... | collective-permute-start | bytes 12296 | tf_op jit(solution)/shard_map/ppermute | solution.py:54
  19.9 1.4 %collective-permute-start.9 = (bf16[16,128]{1,0:T(8,128)(2,1)S(1)}, bf16[16,128]{1,0:T(8,128)(2,1)S(1)}, u32[]{:S(2)}, u32[]{:S(2)}) collective-permute-start(bf16[16,128]{1,0:T(8,128)(2,1)S(1)} %get-tuple-element.62), channel_id=1, source_target_pairs={{1,2},{5,6},{9,10},{13,14},{17,18},{21,22},{25,26},{29,30},{0,3},{... | collective-permute-start | bytes 12296 | tf_op jit(solution)/shard_map/ppermute | solution.py:54
  21.3 1.6 %shard_map.154 = (f32[16,128,128]{2,1,0:T(8,128)}, f32[96,128]{1,0:T(8,128)S(1)}) custom-call(s32[2,16]{1,0:T(2,128)S(1)} %get-tuple-element.37.links, bf16[24,128,128]{2,1,0:T(8,128)(2,1)S(1)} %get-tuple-element.57.extended, bf16[16,2,128,128]{3,2,1,0:T(8,128)(2,1)S(1)} %get-tuple-element.46.couple, bf16[16,128,128]{2,1,0:T(8,128)(2,1)S(1)} %get-tuple-element.47.inverse, ...), custom_call_target="tpu_custom_call" | custom-call | flops 201326592 | tf_op jit(solution)/shard_map/pallas_call | solution.py:507
  23.0 0.0 collective-permute-done.10.in0
  23.0 0.0 collective-permute-done.11.in2
  23.0 0.0 collective-permute-done.8.in1
  23.0 0.0 collective-permute-done.9.in3
  23.0 0.9 %shard_map.155 = f32[64,128]{1,0:T(8,128)} custom-call(f32[96,128]{1,0:T(8,128)S(1)} %get-tuple-element.60.partial, bf16[16,128]{1,0:T(8,128)(2,1)S(1)} %collective-permute-done.8.in1, bf16[16,128]{1,0:T(8,128)(2,1)S(1)} %collective-permute-done.9.in3, bf16[16,128]{1,0:T(8,128)(2,1)S(1)} %collective-permute-done.10.in0, ...), custom_call_target="tpu_custom_call" | custom-call | tf_op jit(solution)/shard_map/pallas_call | solution.py:520
  (4 shorter events, 0.0 us)
Async XLA Ops:
  2.1 6.9 %collective-permute-start = (bf16[272,128]{1,0:T(8,128)(2,1)S(1)}, bf16[272,128]{1,0:T(8,128)(2,1)S(1)}, u32[]{:S(2)}, u32[]{:S(2)}) collective-permute-start(bf16[272,128]{1,0:T(8,128)(2,1)S(1)} %get-tuple-element.42), channel_id=1, source_target_pairs={{0,4},{1,5},{2,6},{3,7},{8,12},{9,13},{10,14},{11,15},{16,20},{17,... | collective-permute-start | bytes 208904 | tf_op jit(solution)/shard_map/ppermute | solution.py:54
  2.2 6.8 %collective-permute-start.1 = (bf16[272,128]{1,0:T(8,128)(2,1)S(1)}, bf16[272,128]{1,0:T(8,128)(2,1)S(1)}, u32[]{:S(2)}, u32[]{:S(2)}) collective-permute-start(bf16[272,128]{1,0:T(8,128)(2,1)S(1)} %get-tuple-element.43), channel_id=1, source_target_pairs={{4,8},{5,9},{6,10},{7,11},{12,16},{13,17},{14,18},{15,19},{20,24},... | collective-permute-start | bytes 208904 | tf_op jit(solution)/shard_map/ppermute | solution.py:54
  4.7 4.3 %collective-permute-start.2 = (bf16[272,128]{1,0:T(8,128)(2,1)S(1)}, bf16[272,128]{1,0:T(8,128)(2,1)S(1)}, u32[]{:S(2)}, u32[]{:S(2)}) collective-permute-start(bf16[272,128]{1,0:T(8,128)(2,1)S(1)} %get-tuple-element.44), channel_id=1, source_target_pairs={{0,1},{2,3},{4,5},{6,7},{8,9},{10,11},{12,13},{14,15},{16,17},{18,... | collective-permute-start | bytes 208904 | tf_op jit(solution)/shard_map/ppermute | solution.py:54
  5.9 3.8 %collective-permute-start.3 = (bf16[272,128]{1,0:T(8,128)(2,1)S(1)}, bf16[272,128]{1,0:T(8,128)(2,1)S(1)}, u32[]{:S(2)}, u32[]{:S(2)}) collective-permute-start(bf16[272,128]{1,0:T(8,128)(2,1)S(1)} %get-tuple-element.45), channel_id=1, source_target_pairs={{1,2},{5,6},{9,10},{13,14},{17,18},{21,22},{25,26},{29,30},{0,3},{... | collective-permute-start | bytes 208904 | tf_op jit(solution)/shard_map/ppermute | solution.py:54
  10.2 4.7 %collective-permute-start.4 = (bf16[256,128]{1,0:T(8,128)(2,1)S(1)}, bf16[256,128]{1,0:T(8,128)(2,1)S(1)}, u32[]{:S(2)}, u32[]{:S(2)}) collective-permute-start(bf16[256,128]{1,0:T(8,128)(2,1)S(1)} %get-tuple-element.53), channel_id=1, source_target_pairs={{4,8},{5,9},{6,10},{7,11},{12,16},{13,17},{14,18},{15,19},{20,24},... | collective-permute-start | bytes 196616 | tf_op jit(solution)/shard_map/ppermute | solution.py:54
  10.6 4.3 %collective-permute-start.5 = (bf16[256,128]{1,0:T(8,128)(2,1)S(1)}, bf16[256,128]{1,0:T(8,128)(2,1)S(1)}, u32[]{:S(2)}, u32[]{:S(2)}) collective-permute-start(bf16[256,128]{1,0:T(8,128)(2,1)S(1)} %get-tuple-element.54), channel_id=1, source_target_pairs={{0,4},{1,5},{2,6},{3,7},{8,12},{9,13},{10,14},{11,15},{16,20},{17,... | collective-permute-start | bytes 196616 | tf_op jit(solution)/shard_map/ppermute | solution.py:54
  10.6 5.2 %collective-permute-start.6 = (bf16[256,128]{1,0:T(8,128)(2,1)S(1)}, bf16[256,128]{1,0:T(8,128)(2,1)S(1)}, u32[]{:S(2)}, u32[]{:S(2)}) collective-permute-start(bf16[256,128]{1,0:T(8,128)(2,1)S(1)} %get-tuple-element.55), channel_id=1, source_target_pairs={{1,2},{5,6},{9,10},{13,14},{17,18},{21,22},{25,26},{29,30},{0,3},{... | collective-permute-start | bytes 196616 | tf_op jit(solution)/shard_map/ppermute | solution.py:54
  12.8 2.9 %collective-permute-start.7 = (bf16[256,128]{1,0:T(8,128)(2,1)S(1)}, bf16[256,128]{1,0:T(8,128)(2,1)S(1)}, u32[]{:S(2)}, u32[]{:S(2)}) collective-permute-start(bf16[256,128]{1,0:T(8,128)(2,1)S(1)} %get-tuple-element.56), channel_id=1, source_target_pairs={{0,1},{2,3},{4,5},{6,7},{8,9},{10,11},{12,13},{14,15},{16,17},{18,... | collective-permute-start | bytes 196616 | tf_op jit(solution)/shard_map/ppermute | solution.py:54
  16.2 6.8 %collective-permute-start.10 = (bf16[16,128]{1,0:T(8,128)(2,1)S(1)}, bf16[16,128]{1,0:T(8,128)(2,1)S(1)}, u32[]{:S(2)}, u32[]{:S(2)}) collective-permute-start(bf16[16,128]{1,0:T(8,128)(2,1)S(1)} %get-tuple-element.63), channel_id=1, source_target_pairs={{0,4},{1,5},{2,6},{3,7},{8,12},{9,13},{10,14},{11,15},{16,20},{17,... | collective-permute-start | bytes 12296 | tf_op jit(solution)/shard_map/ppermute | solution.py:54
  18.0 5.0 %collective-permute-start.11 = (bf16[16,128]{1,0:T(8,128)(2,1)S(1)}, bf16[16,128]{1,0:T(8,128)(2,1)S(1)}, u32[]{:S(2)}, u32[]{:S(2)}) collective-permute-start(bf16[16,128]{1,0:T(8,128)(2,1)S(1)} %get-tuple-element.64), channel_id=1, source_target_pairs={{0,1},{2,3},{4,5},{6,7},{8,9},{10,11},{12,13},{14,15},{16,17},{18,... | collective-permute-start | bytes 12296 | tf_op jit(solution)/shard_map/ppermute | solution.py:54
  18.6 4.4 %collective-permute-start.8 = (bf16[16,128]{1,0:T(8,128)(2,1)S(1)}, bf16[16,128]{1,0:T(8,128)(2,1)S(1)}, u32[]{:S(2)}, u32[]{:S(2)}) collective-permute-start(bf16[16,128]{1,0:T(8,128)(2,1)S(1)} %get-tuple-element.61), channel_id=1, source_target_pairs={{4,8},{5,9},{6,10},{7,11},{12,16},{13,17},{14,18},{15,19},{20,24},... | collective-permute-start | bytes 12296 | tf_op jit(solution)/shard_map/ppermute | solution.py:54
  19.9 3.1 %collective-permute-start.9 = (bf16[16,128]{1,0:T(8,128)(2,1)S(1)}, bf16[16,128]{1,0:T(8,128)(2,1)S(1)}, u32[]{:S(2)}, u32[]{:S(2)}) collective-permute-start(bf16[16,128]{1,0:T(8,128)(2,1)S(1)} %get-tuple-element.62), channel_id=1, source_target_pairs={{1,2},{5,6},{9,10},{13,14},{17,18},{21,22},{25,26},{29,30},{0,3},{... | collective-permute-start | bytes 12296 | tf_op jit(solution)/shard_map/ppermute | solution.py:54

commit v5 on v4

--- a/solution.py
+++ b/solution.py
@@ -138,11 +138,14 @@
     return found
 
 
-def flatten(listed, links):
-    near0, near1 = links
-    blocks = [block for picks in listed for block in picks]
-    pairs = [pair for picks in zip(near0, near1) for pair in zip(*picks)]
-    return blocks, pairs
+def listed_links(near0, near1):
+    values = near0[...], near1[...]
+    slots, pairings = values[0].shape
+    return [
+        [value[slot, pairing] for value in values]
+        for pairing in range(pairings)
+        for slot in range(slots)
+    ]
 
 
 def linked_blocks(links):
@@ -156,9 +159,11 @@
         yield range(start, min(start + 8, len(pairs))), pairs[start : start + 8]
 
 
-def fetch_kernel(count, *refs):
+def fetch_kernel(mesh_dims, count, *refs):
     guess, fars, nears = refs[0], refs[1 : 1 + count], refs[1 + count : 1 + 2 * count]
-    near0, near1, extended, arrivals = refs[1 + 2 * count :]
+    near0, near1, extended, couple_listed, inverse_listed, rhs_listed, arrivals = refs[
+        1 + 2 * count :
+    ]
     copies = [
         pltpu.make_async_copy(far, near, arrivals.at[slot])
         for slot, (far, near) in enumerate(zip(fars, nears))
@@ -170,11 +175,25 @@
     for copy in copies:
         copy.wait()
     links, sends = nears[-2][...], nears[-1][...]
+    columns = []
+    for pairing, (side, _) in enumerate(sides_of(*mesh_dims)):
+        first = 0 if pairing < 2 else 2
+        columns.append(
+            jnp.where(side == first, sends[:, first : first + 1], sends[:, first + 1 : first + 2])
+        )
+    listed = jnp.concatenate(columns, 1)
     for k, near in enumerate((near0, near1)):
-        chosen = jnp.zeros_like(sends)
+        chosen = jnp.zeros_like(listed)
         for block in range(links.shape[1]):
-            chosen = jnp.where(sends == block, links[k, block], chosen)
+            chosen = jnp.where(listed == block, links[k, block], chosen)
         near[...] = chosen
+    couple, inverse, rhs = nears[:3]
+    slots = listed.shape[0]
+    for place in range(couple_listed.shape[0]):
+        block = listed[place % slots, place // slots]
+        couple_listed[place] = couple[block]
+        inverse_listed[place] = inverse[block]
+        rhs_listed[place] = rhs[block]
 
 
 def product(left, right):
@@ -192,27 +211,25 @@
     return [product(part, inverse[block]) for part, block in zip(resid, blocks)]
 
 
-def land(extended, places, arrived, blocks_sent):
+def land(extended, places, arrived, blocks_sent, rows):
     own_count = extended.shape[0] - 4 * blocks_sent
     size = extended.shape[1]
     for (side, exists), came in zip(places, arrived):
         for block in range(blocks_sent):
-            value = came[pl.ds(block * size, size), :]
+            value = came[pl.ds(block * size, rows), :]
             value = jnp.where(exists, value, jnp.zeros_like(value))
-            extended[own_count + side * blocks_sent + block] = value
+            extended[own_count + side * blocks_sent + block, 0:rows, :] = value
 
 
 def first_edge_kernel(
-    mesh_dims, sends, near0, near1, _, in0, in1, in2, in3, couple, inverse, rhs,
+    mesh_dims, near0, near1, _, in1, in0, in2, in3, couple, inverse, rhs,
     extended, out0, out1, out2, out3,
 ):
-    places = sides_of(*mesh_dims)
     size = extended.shape[1]
-    listed = listed_blocks(sends, places)
-    links = [listed_blocks(near, places) for near in (near0, near1)]
-    land(extended, places, (in0, in1, in2, in3), sends.shape[0])
-    fresh = relax(extended, couple, inverse, rhs, *flatten(listed, links), size)
-    slots = sends.shape[0]
+    slots = near0.shape[0]
+    links = listed_links(near0, near1)
+    land(extended, sides_of(*mesh_dims), (in0, in1, in2, in3), slots, size)
+    fresh = relax(extended, couple, inverse, rhs, range(len(links)), links, size)
     for pairing, out in enumerate((out0, out1, out2, out3)):
         for slot in range(slots):
             value = fresh[pairing * slots + slot]
@@ -267,15 +284,13 @@
 
 
 def second_edge_kernel(
-    mesh_dims, sends, near0, near1, _, in1, in0, in3, in2, couple, inverse, rhs,
+    mesh_dims, near0, near1, _, in1, in0, in2, in3, couple, inverse, rhs,
     extended, out0, out1, out2, out3,
 ):
-    places = sides_of(*mesh_dims)
-    listed = listed_blocks(sends, places)
-    links = [listed_blocks(near, places) for near in (near0, near1)]
-    land(extended, places, (in0, in1, in2, in3), sends.shape[0])
-    fresh = relax(extended, couple, inverse, rhs, *flatten(listed, links), tail_rows)
-    slots = sends.shape[0]
+    slots = near0.shape[0]
+    links = listed_links(near0, near1)
+    land(extended, sides_of(*mesh_dims), (in0, in1, in2, in3), slots, tail_rows)
+    fresh = relax(extended, couple, inverse, rhs, range(len(links)), links, tail_rows)
     for pairing, out in enumerate((out0, out1, out2, out3)):
         rows = [fresh[pairing * slots + slot][0:1, :] for slot in range(slots)]
         blank = jnp.zeros((tail_rows - len(rows), lane_width), jnp.float32)
@@ -283,9 +298,10 @@
 
 
 def second_sweep_kernel(
-    links, extended, couple, inverse, rhs, cell_faces,
-    traces, partial, fresh, column, departures,
-):
+    mesh_dims, blocks_sent, links, _, in0, in1, in2, in3, couple, inverse, rhs, cell_faces,
+    traces, partial, extended, fresh, column, departures,
+):
+    land(extended, sides_of(*mesh_dims), (in0, in1, in2, in3), blocks_sent, extended.shape[1])
     stores = []
     for blocks, pairs in in_parts(links):
         values = relax(extended, couple, inverse, rhs, blocks, pairs, extended.shape[1])
@@ -461,15 +477,20 @@
         sat,
         ratio,
         links,
-        sends,
+        _,
         near0,
         near1,
         extended,
+        *listed,
     ) = call(
-        functools.partial(fetch_kernel, len(remote)),
+        functools.partial(fetch_kernel, mesh_dims, len(remote)),
         [like(array) for array in remote]
         + [like(sends)] * 2
-        + [jax.ShapeDtypeStruct(widened, half)],
+        + [jax.ShapeDtypeStruct(widened, half)]
+        + [
+            jax.ShapeDtypeStruct((4 * blocks_sent,) + array.shape[1:], array.dtype)
+            for array in remote[:3]
+        ],
         [whole] + [far] * len(remote),
         [pltpu.SemaphoreType.DMA((len(remote),))],
         traffic=4 * guess.size,
@@ -479,10 +500,10 @@
     extended, *packed = call(
         functools.partial(first_edge_kernel, mesh_dims),
         [like(extended)] + [jax.ShapeDtypeStruct((halo_rows, size), half)] * 4,
-        [whole] * 11,
+        [whole] * 10,
         flops=sweep_flops // 2,
-        aliases={3: 0},
-    )(sends, near0, near1, extended, *arrived, couple, inverse, rhs)
+        aliases={2: 0},
+    )(near0, near1, extended, *(arrived[k] for k in (1, 0, 2, 3)), *listed)
     swept = trade(packed, plans)
 
     tails = [piece[halo_rows:] for piece in arrived]
@@ -498,24 +519,29 @@
     extended, *packed = call(
         functools.partial(second_edge_kernel, mesh_dims),
         [like(extended)] + [jax.ShapeDtypeStruct((tail_rows, size), half)] * 4,
-        [whole] * 11,
+        [whole] * 10,
         flops=sweep_flops // 16,
-        aliases={3: 0},
-    )(sends, near0, near1, extended, *(swept[k] for k in (1, 0, 3, 2)), couple, inverse, rhs)
+        aliases={2: 0},
+    )(near0, near1, extended, *(swept[k] for k in (1, 0, 2, 3)), *listed)
     edges = trade(packed, plans)
 
-    traces, partial = call(
-        second_sweep_kernel,
-        [jax.ShapeDtypeStruct(guess.shape, single), jax.ShapeDtypeStruct(coeff.shape, single)],
-        [whole] * 6,
+    traces, partial, _ = call(
+        functools.partial(second_sweep_kernel, mesh_dims, blocks_sent),
+        [
+            jax.ShapeDtypeStruct(guess.shape, single),
+            jax.ShapeDtypeStruct(coeff.shape, single),
+            like(extended),
+        ],
+        [whole] * 10,
         [
             pltpu.VMEM(guess.shape, single),
             pltpu.VMEM((blocks, size), single),
             pltpu.SemaphoreType.DMA((blocks,)),
         ],
         sweep_flops,
-        out_specs=[far, whole],
-    )(links, extended, couple, inverse, rhs, cell_faces)
+        out_specs=[far, whole, whole],
+        aliases={1: 2},
+    )(links, extended, *swept, couple, inverse, rhs, cell_faces)
 
     (following,) = call(
         functools.partial(cells_kernel, mesh_dims, blocks, blocks_sent),

time: 24.1 us -> 23.7 us (0.983)
  starting transfers between devices: 12.6 us -> 12.1 us
  Pallas kernels: 7.85 us -> 8.15 us
    ppermute x12, starting transfers between devices: 12.6 us -> 12.1 us  [trade(): lax.ppermute(piece, axes, plan)]
    pallas_call x2, Pallas kernels: 3.61 us -> 4.04 us  [the longest x1 2.38 us: per_device(): call(functools.partial(fetch_kernel, mesh_dims, len(remote)), [like(array...]
  transfers between devices with their start and end apart: 12 -> 12, of which waited for: 3 -> 4; matrix products, arithmetic and copies ran while one was open for 0% -> 0% of each run, Pallas kernels for 19% -> 21%
where the time goes in v5:
time: 23.7 us; the launch traced here: 23.5 us
  starting transfers between devices  12.1 us (51%)
  Pallas kernels  8.15 us (34%)
  waiting for transfers between devices  2.52 us (11%)
  between operations  0.74 us (3%)
    ppermute x12, starting transfers between devices, trade(): lax.ppermute(piece, axes, plan)  12.1 us
    ppermute x12, waiting for transfers between devices, trade(): lax.ppermute(piece, axes, plan)  2.52 us
    pallas_call x1, Pallas kernels, per_device(): call(functools.partial(fetch_kernel, mesh_dims, len(remote)), [like(array...  2.38 us
    pallas_call x1, Pallas kernels, per_device(): call(functools.partial(second_sweep_kernel, mesh_dims, blocks_sent), [jax...  1.66 us
    pallas_call x1, Pallas kernels, per_device(): call(functools.partial(pack_kernel, mesh_dims), [jax.ShapeDtypeStruct((ha...  1.47 us
    pallas_call x1, Pallas kernels, per_device(): call(functools.partial(cells_kernel, mesh_dims, blocks, blocks_sent), [li...  0.89 us
    pallas_call x1, Pallas kernels, per_device(): call(functools.partial(first_sweep_kernel, mesh_dims, halves), [like(exte...  0.86 us
    pallas_call x1, Pallas kernels, per_device(): call(functools.partial(first_edge_kernel, mesh_dims), [like(extended)] +...  0.49 us
  transfers between devices with their start and end apart: 12, of which 4 were waited for; matrix products, arithmetic and copies ran while one was open for 0% of the time, Pallas kernels for 21%

profile of v5, /device:TPU:5, one launch (start us, length us, event | category | flops | bytes accessed | tf_op | source)
XLA Modules:
  0.0 23.5 jit_solution(4141901585504717629)
XLA Ops:
  0.6 1.5 %shard_map.149 = (bf16[272,128]{1,0:T(8,128)(2,1)S(1)}, bf16[272,128]{1,0:T(8,128)(2,1)S(1)}, bf16[272,128]{1,0:T(8,128)(2,1)S(1)}, bf16[272,128]{1,0:T(8,128)(2,1)S(1)}, f32[16,128,128]{2,1,0:T(8,128)S(1)}) custom-call(s32[2,4]{1,0:T(2,128)} %bitcast.46, f32[16,128,128]{2,1,0:T(8,128)} %bitcast.34, s32[8,128]{1,0:T(8,128)} %bitcast.45, f32[64,128]{1,0:T(8,128)} %bitcast.36), custom_call_target="tpu_custom_call" | custom-call | tf_op jit(solution)/shard_map/pallas_call | solution.py:440
  2.1 1.3 %collective-permute-start = (bf16[272,128]{1,0:T(8,128)(2,1)S(1)}, bf16[272,128]{1,0:T(8,128)(2,1)S(1)}, u32[]{:S(2)}, u32[]{:S(2)}) collective-permute-start(bf16[272,128]{1,0:T(8,128)(2,1)S(1)} %get-tuple-element.43), channel_id=1, source_target_pairs={{4,8},{5,9},{6,10},{7,11},{12,16},{13,17},{14,18},{15,19},{20,24},... | collective-permute-start | bytes 208904 | tf_op jit(solution)/shard_map/ppermute | solution.py:54
  3.4 0.0 collective-permute-start.1
  3.4 1.0 %collective-permute-start.2 = (bf16[272,128]{1,0:T(8,128)(2,1)S(1)}, bf16[272,128]{1,0:T(8,128)(2,1)S(1)}, u32[]{:S(2)}, u32[]{:S(2)}) collective-permute-start(bf16[272,128]{1,0:T(8,128)(2,1)S(1)} %get-tuple-element.45), channel_id=1, source_target_pairs={{0,1},{2,3},{4,5},{6,7},{8,9},{10,11},{12,13},{14,15},{16,17},{18,... | collective-permute-start | bytes 208904 | tf_op jit(solution)/shard_map/ppermute | solution.py:54
  4.4 1.1 %collective-permute-start.3 = (bf16[272,128]{1,0:T(8,128)(2,1)S(1)}, bf16[272,128]{1,0:T(8,128)(2,1)S(1)}, u32[]{:S(2)}, u32[]{:S(2)}) collective-permute-start(bf16[272,128]{1,0:T(8,128)(2,1)S(1)} %get-tuple-element.46), channel_id=1, source_target_pairs={{1,2},{5,6},{9,10},{13,14},{17,18},{21,22},{25,26},{29,30},{0,3},{... | collective-permute-start | bytes 208904 | tf_op jit(solution)/shard_map/ppermute | solution.py:54
  5.5 2.4 %shard_map.150 = (bf16[16,2,128,128]{3,2,1,0:T(8,128)(2,1)S(1)}, bf16[16,128,128]{2,1,0:T(8,128)(2,1)S(1)}, f32[16,128,128]{2,1,0:T(8,128)S(1)}, s32[96,128]{1,0...) custom-call(f32[16,128,128]{2,1,0:T(8,128)S(1)} %get-tuple-element.3, ...), custom_call_target="tpu_custom_call" | custom-call | bytes 1048576 | tf_op jit(solution)/shard_map/pallas_call | solution.py:485
  7.9 0.0 collective-permute-done.in1
  7.9 0.4 %collective-permute-done.1.in0 = bf16[272,128]{1,0:T(8,128)(2,1)S(1)} collective-permute-done((bf16[272,128]{1,0:T(8,128)(2,1)S(1)}, bf16[272,128]{1,0:T(8,128)(2,1)S(1)}, u32[]{:S(2)}, u32[]{:S(2)}) %collective-permute-start.1) | collective-permute-done | bytes 69664 | tf_op jit(solution)/shard_map/ppermute | solution.py:54
  8.3 0.0 collective-permute-done.2.in2
  8.3 0.2 collective-permute-done.3.in3
  8.5 0.5 %shard_map.151 = (bf16[24,128,128]{2,1,0:T(8,128)(2,1)S(1)}, bf16[256,128]{1,0:T(8,128)(2,1)S(1)}, bf16[256,128]{1,0:T(8,128)(2,1)S(1)}, bf16[256,128]{1,0:T(8,128)(2,1)S(1)}, bf16[256,128]{1,0:T(8,128)(2,1)S(1)}) custom-call(s32[2,4]{1,0:T(2,128)S(1)} %get-tuple-element.40.near0, ...), custom_call_target="tpu_custom_call", output_to_operand_aliasing={{0}: (2, {})} | custom-call | flops 100663296 | tf_op jit(solution)/shard_map/pallas_call | solution.py:500
  9.0 2.5 %collective-permute-start.4 = (bf16[256,128]{1,0:T(8,128)(2,1)S(1)}, bf16[256,128]{1,0:T(8,128)(2,1)S(1)}, u32[]{:S(2)}, u32[]{:S(2)}) collective-permute-start(bf16[256,128]{1,0:T(8,128)(2,1)S(1)} %get-tuple-element.57), channel_id=1, source_target_pairs={{4,8},{5,9},{6,10},{7,11},{12,16},{13,17},{14,18},{15,19},{20,24},... | collective-permute-start | bytes 196616 | tf_op jit(solution)/shard_map/ppermute | solution.py:54
  11.5 0.0 collective-permute-start.5
  11.5 0.5 %collective-permute-start.6 = (bf16[256,128]{1,0:T(8,128)(2,1)S(1)}, bf16[256,128]{1,0:T(8,128)(2,1)S(1)}, u32[]{:S(2)}, u32[]{:S(2)}) collective-permute-start(bf16[256,128]{1,0:T(8,128)(2,1)S(1)} %get-tuple-element.59), channel_id=1, source_target_pairs={{0,1},{2,3},{4,5},{6,7},{8,9},{10,11},{12,13},{14,15},{16,17},{18,... | collective-permute-start | bytes 196616 | tf_op jit(solution)/shard_map/ppermute | solution.py:54
  12.0 1.1 %collective-permute-start.7 = (bf16[256,128]{1,0:T(8,128)(2,1)S(1)}, bf16[256,128]{1,0:T(8,128)(2,1)S(1)}, u32[]{:S(2)}, u32[]{:S(2)}) collective-permute-start(bf16[256,128]{1,0:T(8,128)(2,1)S(1)} %get-tuple-element.60), channel_id=1, source_target_pairs={{1,2},{5,6},{9,10},{13,14},{17,18},{21,22},{25,26},{29,30},{0,3},{... | collective-permute-start | bytes 196616 | tf_op jit(solution)/shard_map/ppermute | solution.py:54
  13.1 0.9 %shard_map.152 = (bf16[24,128,128]{2,1,0:T(8,128)(2,1)S(1)}, f32[96,128]{1,0:T(8,128)S(1)}) custom-call(s32[2,16]{1,0:T(2,128)S(1)} %get-tuple-element.39.links, bf16[24,128,128]{2,1,0:T(8,128)(2,1)S(1)} %get-tuple-element.50.extended, bf16[16,2,128,128]{3,2,1,0:T(8,128)(2,1)S(1)} %get-tuple-element.51.couple, ...), custom_call_target="tpu_custom_call" | custom-call | flops 201326592 | tf_op jit(solution)/shard_map/pallas_call | solution.py:511
  14.0 0.0 collective-permute-done.4.in1
  14.0 1.2 %collective-permute-done.5.in0 = bf16[256,128]{1,0:T(8,128)(2,1)S(1)} collective-permute-done((bf16[256,128]{1,0:T(8,128)(2,1)S(1)}, bf16[256,128]{1,0:T(8,128)(2,1)S(1)}, u32[]{:S(2)}, u32[]{:S(2)}) %collective-permute-start.5) | collective-permute-done | bytes 65568 | tf_op jit(solution)/shard_map/ppermute | solution.py:54
  15.2 0.0 collective-permute-done.6.in2
  15.2 0.7 %collective-permute-done.7.in3 = bf16[256,128]{1,0:T(8,128)(2,1)S(1)} collective-permute-done((bf16[256,128]{1,0:T(8,128)(2,1)S(1)}, bf16[256,128]{1,0:T(8,128)(2,1)S(1)}, u32[]{:S(2)}, u32[]{:S(2)}) %collective-permute-start.7) | collective-permute-done | bytes 65568 | tf_op jit(solution)/shard_map/ppermute | solution.py:54
  15.9 0.4 %shard_map.153 = (bf16[24,128,128]{2,1,0:T(8,128)(2,1)S(1)}, bf16[16,128]{1,0:T(8,128)(2,1)S(1)}, bf16[16,128]{1,0:T(8,128)(2,1)S(1)}, bf16[16,128]{1,0:T(8,128)(2,1)S(1)}, bf16[16,128]{1,0:T(8,128)(2,1)S(1)}) custom-call(s32[2,4]{1,0:T(2,128)S(1)} %get-tuple-element.40.near0, s32[2,4]{1,0:T(2,128)S(1)} %get-tuple-element.41.near1, ...), custom_call_target="tpu_custom_call", output_to_operand_aliasing={{0}: (2, {})} | custom-call | flops 12582912 | tf_op jit(solution)/shard_map/pallas_call | solution.py:519
  16.3 1.6 %collective-permute-start.10 = (bf16[16,128]{1,0:T(8,128)(2,1)S(1)}, bf16[16,128]{1,0:T(8,128)(2,1)S(1)}, u32[]{:S(2)}, u32[]{:S(2)}) collective-permute-start(bf16[16,128]{1,0:T(8,128)(2,1)S(1)} %get-tuple-element.67), channel_id=1, source_target_pairs={{0,4},{1,5},{2,6},{3,7},{8,12},{9,13},{10,14},{11,15},{16,20},{17,... | collective-permute-start | bytes 12296 | tf_op jit(solution)/shard_map/ppermute | solution.py:54
  17.9 0.3 %collective-permute-start.11 = (bf16[16,128]{1,0:T(8,128)(2,1)S(1)}, bf16[16,128]{1,0:T(8,128)(2,1)S(1)}, u32[]{:S(2)}, u32[]{:S(2)}) collective-permute-start(bf16[16,128]{1,0:T(8,128)(2,1)S(1)} %get-tuple-element.68), channel_id=1, source_target_pairs={{0,1},{2,3},{4,5},{6,7},{8,9},{10,11},{12,13},{14,15},{16,17},{18,... | collective-permute-start | bytes 12296 | tf_op jit(solution)/shard_map/ppermute | solution.py:54
  18.3 1.3 %collective-permute-start.8 = (bf16[16,128]{1,0:T(8,128)(2,1)S(1)}, bf16[16,128]{1,0:T(8,128)(2,1)S(1)}, u32[]{:S(2)}, u32[]{:S(2)}) collective-permute-start(bf16[16,128]{1,0:T(8,128)(2,1)S(1)} %get-tuple-element.65), channel_id=1, source_target_pairs={{4,8},{5,9},{6,10},{7,11},{12,16},{13,17},{14,18},{15,19},{20,24},... | collective-permute-start | bytes 12296 | tf_op jit(solution)/shard_map/ppermute | solution.py:54
  19.5 1.4 %collective-permute-start.9 = (bf16[16,128]{1,0:T(8,128)(2,1)S(1)}, bf16[16,128]{1,0:T(8,128)(2,1)S(1)}, u32[]{:S(2)}, u32[]{:S(2)}) collective-permute-start(bf16[16,128]{1,0:T(8,128)(2,1)S(1)} %get-tuple-element.66), channel_id=1, source_target_pairs={{1,2},{5,6},{9,10},{13,14},{17,18},{21,22},{25,26},{29,30},{0,3},{... | collective-permute-start | bytes 12296 | tf_op jit(solution)/shard_map/ppermute | solution.py:54
  20.9 1.7 %shard_map.154 = (f32[16,128,128]{2,1,0:T(8,128)}, f32[96,128]{1,0:T(8,128)S(1)}, bf16[24,128,128]{2,1,0:T(8,128)(2,1)S(1)}) custom-call(s32[2,16]{1,0:T(2,128)S(1)} %get-tuple-element.39.links, bf16[24,128,128]{2,1,0:T(8,128)(2,1)S(1)} %get-tuple-element.61._, bf16[256,128]{1,0:T(8,128)(2,1)S(1)} %collective-permute-done.5.in0, ...), custom_call_target="tpu_custom_call", output_to_operand_aliasing={{2}: (1, {})} | custom-call | flops 201326592 | tf_op jit(solution)/shard_map/pallas_call | solution.py:528
  22.6 0.0 collective-permute-done.10.in0
  22.6 0.0 collective-permute-done.11.in2
  22.6 0.0 collective-permute-done.8.in1
  22.6 0.0 collective-permute-done.9.in3
  22.6 0.9 %shard_map.155 = f32[64,128]{1,0:T(8,128)} custom-call(f32[96,128]{1,0:T(8,128)S(1)} %get-tuple-element.64.partial, bf16[16,128]{1,0:T(8,128)(2,1)S(1)} %collective-permute-done.8.in1, bf16[16,128]{1,0:T(8,128)(2,1)S(1)} %collective-permute-done.9.in3, bf16[16,128]{1,0:T(8,128)(2,1)S(1)} %collective-permute-done.10.in0, ...), custom_call_target="tpu_custom_call" | custom-call | tf_op jit(solution)/shard_map/pallas_call | solution.py:546
  (4 shorter events, 0.0 us)
Async XLA Ops:
  2.1 5.8 %collective-permute-start = (bf16[272,128]{1,0:T(8,128)(2,1)S(1)}, bf16[272,128]{1,0:T(8,128)(2,1)S(1)}, u32[]{:S(2)}, u32[]{:S(2)}) collective-permute-start(bf16[272,128]{1,0:T(8,128)(2,1)S(1)} %get-tuple-element.43), channel_id=1, source_target_pairs={{4,8},{5,9},{6,10},{7,11},{12,16},{13,17},{14,18},{15,19},{20,24},... | collective-permute-start | bytes 208904 | tf_op jit(solution)/shard_map/ppermute | solution.py:54
  3.4 4.9 %collective-permute-start.1 = (bf16[272,128]{1,0:T(8,128)(2,1)S(1)}, bf16[272,128]{1,0:T(8,128)(2,1)S(1)}, u32[]{:S(2)}, u32[]{:S(2)}) collective-permute-start(bf16[272,128]{1,0:T(8,128)(2,1)S(1)} %get-tuple-element.44), channel_id=1, source_target_pairs={{0,4},{1,5},{2,6},{3,7},{8,12},{9,13},{10,14},{11,15},{16,20},{17,... | collective-permute-start | bytes 208904 | tf_op jit(solution)/shard_map/ppermute | solution.py:54
  3.4 4.9 %collective-permute-start.2 = (bf16[272,128]{1,0:T(8,128)(2,1)S(1)}, bf16[272,128]{1,0:T(8,128)(2,1)S(1)}, u32[]{:S(2)}, u32[]{:S(2)}) collective-permute-start(bf16[272,128]{1,0:T(8,128)(2,1)S(1)} %get-tuple-element.45), channel_id=1, source_target_pairs={{0,1},{2,3},{4,5},{6,7},{8,9},{10,11},{12,13},{14,15},{16,17},{18,... | collective-permute-start | bytes 208904 | tf_op jit(solution)/shard_map/ppermute | solution.py:54
  4.4 4.1 %collective-permute-start.3 = (bf16[272,128]{1,0:T(8,128)(2,1)S(1)}, bf16[272,128]{1,0:T(8,128)(2,1)S(1)}, u32[]{:S(2)}, u32[]{:S(2)}) collective-permute-start(bf16[272,128]{1,0:T(8,128)(2,1)S(1)} %get-tuple-element.46), channel_id=1, source_target_pairs={{1,2},{5,6},{9,10},{13,14},{17,18},{21,22},{25,26},{29,30},{0,3},{... | collective-permute-start | bytes 208904 | tf_op jit(solution)/shard_map/ppermute | solution.py:54
  9.0 5.0 %collective-permute-start.4 = (bf16[256,128]{1,0:T(8,128)(2,1)S(1)}, bf16[256,128]{1,0:T(8,128)(2,1)S(1)}, u32[]{:S(2)}, u32[]{:S(2)}) collective-permute-start(bf16[256,128]{1,0:T(8,128)(2,1)S(1)} %get-tuple-element.57), channel_id=1, source_target_pairs={{4,8},{5,9},{6,10},{7,11},{12,16},{13,17},{14,18},{15,19},{20,24},... | collective-permute-start | bytes 196616 | tf_op jit(solution)/shard_map/ppermute | solution.py:54
  11.5 3.7 %collective-permute-start.5 = (bf16[256,128]{1,0:T(8,128)(2,1)S(1)}, bf16[256,128]{1,0:T(8,128)(2,1)S(1)}, u32[]{:S(2)}, u32[]{:S(2)}) collective-permute-start(bf16[256,128]{1,0:T(8,128)(2,1)S(1)} %get-tuple-element.58), channel_id=1, source_target_pairs={{0,4},{1,5},{2,6},{3,7},{8,12},{9,13},{10,14},{11,15},{16,20},{17,... | collective-permute-start | bytes 196616 | tf_op jit(solution)/shard_map/ppermute | solution.py:54
  11.5 3.7 %collective-permute-start.6 = (bf16[256,128]{1,0:T(8,128)(2,1)S(1)}, bf16[256,128]{1,0:T(8,128)(2,1)S(1)}, u32[]{:S(2)}, u32[]{:S(2)}) collective-permute-start(bf16[256,128]{1,0:T(8,128)(2,1)S(1)} %get-tuple-element.59), channel_id=1, source_target_pairs={{0,1},{2,3},{4,5},{6,7},{8,9},{10,11},{12,13},{14,15},{16,17},{18,... | collective-permute-start | bytes 196616 | tf_op jit(solution)/shard_map/ppermute | solution.py:54
  12.0 3.9 %collective-permute-start.7 = (bf16[256,128]{1,0:T(8,128)(2,1)S(1)}, bf16[256,128]{1,0:T(8,128)(2,1)S(1)}, u32[]{:S(2)}, u32[]{:S(2)}) collective-permute-start(bf16[256,128]{1,0:T(8,128)(2,1)S(1)} %get-tuple-element.60), channel_id=1, source_target_pairs={{1,2},{5,6},{9,10},{13,14},{17,18},{21,22},{25,26},{29,30},{0,3},{... | collective-permute-start | bytes 196616 | tf_op jit(solution)/shard_map/ppermute | solution.py:54
  16.3 6.3 %collective-permute-start.10 = (bf16[16,128]{1,0:T(8,128)(2,1)S(1)}, bf16[16,128]{1,0:T(8,128)(2,1)S(1)}, u32[]{:S(2)}, u32[]{:S(2)}) collective-permute-start(bf16[16,128]{1,0:T(8,128)(2,1)S(1)} %get-tuple-element.67), channel_id=1, source_target_pairs={{0,4},{1,5},{2,6},{3,7},{8,12},{9,13},{10,14},{11,15},{16,20},{17,... | collective-permute-start | bytes 12296 | tf_op jit(solution)/shard_map/ppermute | solution.py:54
  17.9 4.7 %collective-permute-start.11 = (bf16[16,128]{1,0:T(8,128)(2,1)S(1)}, bf16[16,128]{1,0:T(8,128)(2,1)S(1)}, u32[]{:S(2)}, u32[]{:S(2)}) collective-permute-start(bf16[16,128]{1,0:T(8,128)(2,1)S(1)} %get-tuple-element.68), channel_id=1, source_target_pairs={{0,1},{2,3},{4,5},{6,7},{8,9},{10,11},{12,13},{14,15},{16,17},{18,... | collective-permute-start | bytes 12296 | tf_op jit(solution)/shard_map/ppermute | solution.py:54
  18.3 4.3 %collective-permute-start.8 = (bf16[16,128]{1,0:T(8,128)(2,1)S(1)}, bf16[16,128]{1,0:T(8,128)(2,1)S(1)}, u32[]{:S(2)}, u32[]{:S(2)}) collective-permute-start(bf16[16,128]{1,0:T(8,128)(2,1)S(1)} %get-tuple-element.65), channel_id=1, source_target_pairs={{4,8},{5,9},{6,10},{7,11},{12,16},{13,17},{14,18},{15,19},{20,24},... | collective-permute-start | bytes 12296 | tf_op jit(solution)/shard_map/ppermute | solution.py:54
  19.5 3.1 %collective-permute-start.9 = (bf16[16,128]{1,0:T(8,128)(2,1)S(1)}, bf16[16,128]{1,0:T(8,128)(2,1)S(1)}, u32[]{:S(2)}, u32[]{:S(2)}) collective-permute-start(bf16[16,128]{1,0:T(8,128)(2,1)S(1)} %get-tuple-element.66), channel_id=1, source_target_pairs={{1,2},{5,6},{9,10},{13,14},{17,18},{21,22},{25,26},{29,30},{0,3},{... | collective-permute-start | bytes 12296 | tf_op jit(solution)/shard_map/ppermute | solution.py:54

commit v6 on v5

--- a/solution.py
+++ b/solution.py
@@ -75,8 +75,8 @@
 
 def pack_kernel(
     mesh_dims, sends_far, guess_far, list_far, sat_far,
-    out0, out1, out2, out3, guess,
-    sends, cell_list, sat, picked, arrivals,
+    out0, out1, out2, out3, guess, sends,
+    cell_list, sat, picked, arrivals,
 ):
     places = sides_of(*mesh_dims)
     blocks, size = guess.shape[0], guess.shape[1]
@@ -159,14 +159,25 @@
         yield range(start, min(start + 8, len(pairs))), pairs[start : start + 8]
 
 
-def fetch_kernel(mesh_dims, count, *refs):
-    guess, fars, nears = refs[0], refs[1 : 1 + count], refs[1 + count : 1 + 2 * count]
-    near0, near1, extended, couple_listed, inverse_listed, rhs_listed, arrivals = refs[
-        1 + 2 * count :
-    ]
+def fetch_kernel(mesh_dims, count, guess, sends, rhs_far, *refs):
+    fars, nears = refs[:count], refs[count : 2 * count]
+    near0, near1, extended, couple_listed, inverse_listed, rhs_listed, arrivals = refs[2 * count :]
+    listed = sends[...]
+    columns = []
+    for pairing, (side, _) in enumerate(sides_of(*mesh_dims)):
+        first = 0 if pairing < 2 else 2
+        columns.append(
+            jnp.where(side == first, listed[:, first : first + 1], listed[:, first + 1 : first + 2])
+        )
+    listed = jnp.concatenate(columns, 1)
+    slots, pairings = listed.shape
+    blocks = [listed[slot, pairing] for pairing in range(pairings) for slot in range(slots)]
     copies = [
         pltpu.make_async_copy(far, near, arrivals.at[slot])
         for slot, (far, near) in enumerate(zip(fars, nears))
+    ] + [
+        pltpu.make_async_copy(rhs_far.at[block], rhs_listed.at[place], arrivals.at[count + place])
+        for place, block in enumerate(blocks)
     ]
     for copy in copies:
         copy.start()
@@ -174,26 +185,15 @@
         extended[block] = guess[block].astype(jnp.bfloat16)
     for copy in copies:
         copy.wait()
-    links, sends = nears[-2][...], nears[-1][...]
-    columns = []
-    for pairing, (side, _) in enumerate(sides_of(*mesh_dims)):
-        first = 0 if pairing < 2 else 2
-        columns.append(
-            jnp.where(side == first, sends[:, first : first + 1], sends[:, first + 1 : first + 2])
-        )
-    listed = jnp.concatenate(columns, 1)
+    couple, inverse, links = nears[0], nears[1], nears[-1][...]
+    for place, block in enumerate(blocks):
+        couple_listed[place] = couple[block]
+        inverse_listed[place] = inverse[block]
     for k, near in enumerate((near0, near1)):
         chosen = jnp.zeros_like(listed)
         for block in range(links.shape[1]):
             chosen = jnp.where(listed == block, links[k, block], chosen)
         near[...] = chosen
-    couple, inverse, rhs = nears[:3]
-    slots = listed.shape[0]
-    for place in range(couple_listed.shape[0]):
-        block = listed[place % slots, place // slots]
-        couple_listed[place] = couple[block]
-        inverse_listed[place] = inverse[block]
-        rhs_listed[place] = rhs[block]
 
 
 def product(left, right):
@@ -236,10 +236,13 @@
             out[pl.ds(slot * size, size), :] = value.astype(jnp.bfloat16)
 
 
-def look_up(table, first_row, rows, high, low, value):
-    for row in rows:
-        got = take_lanes(spread(table[pl.ds(first_row + row, 1), :]), low)
-        value = jnp.where(high == row, got, value)
+def spread_rows(table, first_row, count):
+    return [spread(table[pl.ds(first_row + row, 1), :]) for row in range(count)]
+
+
+def look_up(rows, high, low, value):
+    for number, row in enumerate(rows):
+        value = jnp.where(high == number, take_lanes(row, low), value)
     return value
 
 
@@ -267,20 +270,18 @@
         across_rows[pl.ds(face * stride, groups), :] = (
             modes[0] + mode if face % 2 == 0 else modes[0] - mode
         )
-    for blocks, pairs in in_parts(links):
-        fresh = relax(extended, couple, inverse, rhs, blocks, pairs, extended.shape[1])
-        for block, value in zip(blocks, fresh):
-            smoothed[block] = value.astype(jnp.bfloat16)
     for face in range(6):
+        rows = spread_rows(across_rows, face * stride, groups + halves if face < 4 else groups)
         for start in range(0, groups, 8):
             index = neighbours[pl.ds(face * groups + start, 8), :]
             high, low = index >> 7, index & (lane_width - 1)
             if 0 < face < 4:
                 high = jnp.where(high >= groups, high - face * halves, high)
-            rows = range(groups + halves if face < 4 else groups)
-            across[pl.ds(face * groups + start, 8), :] = look_up(
-                across_rows, face * stride, rows, high, low, nothing()
-            )
+            across[pl.ds(face * groups + start, 8), :] = look_up(rows, high, low, nothing())
+    for blocks, pairs in in_parts(links):
+        fresh = relax(extended, couple, inverse, rhs, blocks, pairs, extended.shape[1])
+        for block, value in zip(blocks, fresh):
+            smoothed[block] = value.astype(jnp.bfloat16)
 
 
 def second_edge_kernel(
@@ -312,11 +313,11 @@
             )
             stores[block].start()
             column[pl.ds(block, 1), :] = value[0:1].astype(jnp.bfloat16).astype(jnp.float32)
+    rows = spread_rows(column, 0, column.shape[0])
     for start in range(0, cell_faces.shape[0], 8):
         index = cell_faces[pl.ds(start, 8), :]
-        rows = range(column.shape[0])
         partial[pl.ds(start, 8), :] = look_up(
-            column, 0, rows, index >> 7, index & (lane_width - 1), nothing()
+            rows, index >> 7, index & (lane_width - 1), nothing()
         )
     for store in stores:
         store.wait()
@@ -335,6 +336,7 @@
             faces[pl.ds(side * blocks_sent + block, 1), :] = value[block : block + 1]
     modes = [sat[pl.ds(mode, groups, stride=4), :] for mode in range(4)]
     weights = [coeff[pl.ds(face * groups, groups), :] for face in range(6)]
+    edge_rows = spread_rows(faces, 0, 4 * blocks_sent)
     traces = []
     for face in range(6):
         parts = []
@@ -342,7 +344,7 @@
             rows = pl.ds(face * groups + start, 8)
             index = cell_faces[rows, :]
             high, low = (index >> 7) - blocks, index & (lane_width - 1)
-            parts.append(look_up(faces, 0, range(4 * blocks_sent), high, low, partial[rows, :]))
+            parts.append(look_up(edge_rows, high, low, partial[rows, :]))
         traces.append(jnp.concatenate(parts, 0))
     total = weights[0]
     gained = source[...] + weights[0] * traces[0]
@@ -437,12 +439,12 @@
         return jax.ShapeDtypeStruct(array.shape, array.dtype)
 
     widened = (extended_blocks, columns, size)
-    *packed, guess = call(
+    *packed, guess, sends = call(
         functools.partial(pack_kernel, mesh_dims),
-        [jax.ShapeDtypeStruct((halo_rows + tail_rows, size), half)] * 4 + [like(guess)],
+        [jax.ShapeDtypeStruct((halo_rows + tail_rows, size), half)] * 4
+        + [like(guess), like(sends)],
         [far] * 4,
         [
-            pltpu.VMEM(sends.shape, jnp.int32),
             pltpu.VMEM(cell_list.shape, jnp.int32),
             pltpu.VMEM(sat.shape, single),
             pltpu.VMEM((4 * halves, lane_width), single),
@@ -454,7 +456,6 @@
     remote = [
         couple,
         inverse,
-        rhs,
         by_cells(cell_faces[0, 0]),
         by_cells(face_coeff[0, 0]),
         by_cells(cell_source[0]),
@@ -463,12 +464,10 @@
         sat,
         by_cells(step_ratio[0]),
         links,
-        sends,
     ]
     (
         couple,
         inverse,
-        rhs,
         cell_faces,
         coeff,
         source,
@@ -477,7 +476,6 @@
         sat,
         ratio,
         links,
-        _,
         near0,
         near1,
         extended,
@@ -489,12 +487,12 @@
         + [jax.ShapeDtypeStruct(widened, half)]
         + [
             jax.ShapeDtypeStruct((4 * blocks_sent,) + array.shape[1:], array.dtype)
-            for array in remote[:3]
+            for array in (couple, inverse, rhs)
         ],
-        [whole] + [far] * len(remote),
-        [pltpu.SemaphoreType.DMA((len(remote),))],
+        [whole, whole] + [far] * (1 + len(remote)),
+        [pltpu.SemaphoreType.DMA((len(remote) + 4 * blocks_sent,))],
         traffic=4 * guess.size,
-    )(guess, *map(keep_far, remote))
+    )(guess, sends, *map(keep_far, [rhs] + remote))
 
     sweep_flops = 6 * blocks * columns * size * size
     extended, *packed = call(

time: 23.7 us -> 23.7 us (level)
  Pallas kernels: 8.15 us -> 7.71 us
  waiting for transfers between devices: 2.52 us -> 2.95 us
    pallas_call x1, Pallas kernels: 2.38 us -> 1.94 us  [per_device(): call(functools.partial(fetch_kernel, mesh_dims, len(remote)), [like(array...]
    ppermute x12, waiting for transfers between devices: 2.52 us -> 2.95 us  [trade(): lax.ppermute(piece, axes, plan)]
  transfers between devices with their start and end apart: 12 -> 12, of which waited for: 4 -> 4; matrix products, arithmetic and copies ran while one was open for 0% -> 0% of each run, Pallas kernels for 21% -> 19%
where the time goes in v6:
time: 23.7 us; the launch traced here: 23.5 us
  starting transfers between devices  12.1 us (51%)
  Pallas kernels  7.71 us (33%)
  waiting for transfers between devices  2.95 us (12%)
  between operations  0.74 us (3%)
    ppermute x12, starting transfers between devices, trade(): lax.ppermute(piece, axes, plan)  12.1 us
    ppermute x12, waiting for transfers between devices, trade(): lax.ppermute(piece, axes, plan)  2.95 us
    pallas_call x1, Pallas kernels, per_device(): call(functools.partial(fetch_kernel, mesh_dims, len(remote)), [like(array...  1.94 us
    pallas_call x1, Pallas kernels, per_device(): call(functools.partial(second_sweep_kernel, mesh_dims, blocks_sent), [jax...  1.65 us
    pallas_call x1, Pallas kernels, per_device(): call(functools.partial(pack_kernel, mesh_dims), [jax.ShapeDtypeStruct((ha...  1.47 us
    pallas_call x1, Pallas kernels, per_device(): call(functools.partial(cells_kernel, mesh_dims, blocks, blocks_sent), [li...  0.89 us
    pallas_call x1, Pallas kernels, per_device(): call(functools.partial(first_sweep_kernel, mesh_dims, halves), [like(exte...  0.87 us
    pallas_call x1, Pallas kernels, per_device(): call(functools.partial(first_edge_kernel, mesh_dims), [like(extended)] +...  0.49 us
  transfers between devices with their start and end apart: 12, of which 4 were waited for; matrix products, arithmetic and copies ran while one was open for 0% of the time, Pallas kernels for 19%

profile of v6, /device:TPU:5, one launch (start us, length us, event | category | flops | bytes accessed | tf_op | source)
XLA Modules:
  0.0 23.5 jit_solution(17835212723490052931)
XLA Ops:
  0.6 1.5 %shard_map.149 = (bf16[272,128]{1,0:T(8,128)(2,1)S(1)}, bf16[272,128]{1,0:T(8,128)(2,1)S(1)}, bf16[272,128]{1,0:T(8,128)(2,1)S(1)}, bf16[272,128]{1,0:T(8,128)(2...) custom-call(s32[2,4]{1,0:T(2,128)} %bitcast.48, f32[16,128,128]{2,1,0:T(8,128)} %bitcast.36, s32[8,128]{1,0:T(8,128)} %bitcast.47, ...), custom_call_target="tpu_custom_call" | custom-call | tf_op jit(solution)/shard_map/pallas_call | solution.py:442
  2.1 1.3 %collective-permute-start = (bf16[272,128]{1,0:T(8,128)(2,1)S(1)}, bf16[272,128]{1,0:T(8,128)(2,1)S(1)}, u32[]{:S(2)}, u32[]{:S(2)}) collective-permute-start(bf16[272,128]{1,0:T(8,128)(2,1)S(1)} %get-tuple-element.44), channel_id=1, source_target_pairs={{4,8},{5,9},{6,10},{7,11},{12,16},{13,17},{14,18},{15,19},{20,24},... | collective-permute-start | bytes 208904 | tf_op jit(solution)/shard_map/ppermute | solution.py:54
  3.4 0.0 collective-permute-start.1
  3.4 1.0 %collective-permute-start.2 = (bf16[272,128]{1,0:T(8,128)(2,1)S(1)}, bf16[272,128]{1,0:T(8,128)(2,1)S(1)}, u32[]{:S(2)}, u32[]{:S(2)}) collective-permute-start(bf16[272,128]{1,0:T(8,128)(2,1)S(1)} %get-tuple-element.46), channel_id=1, source_target_pairs={{0,1},{2,3},{4,5},{6,7},{8,9},{10,11},{12,13},{14,15},{16,17},{18,... | collective-permute-start | bytes 208904 | tf_op jit(solution)/shard_map/ppermute | solution.py:54
  4.4 1.1 %collective-permute-start.3 = (bf16[272,128]{1,0:T(8,128)(2,1)S(1)}, bf16[272,128]{1,0:T(8,128)(2,1)S(1)}, u32[]{:S(2)}, u32[]{:S(2)}) collective-permute-start(bf16[272,128]{1,0:T(8,128)(2,1)S(1)} %get-tuple-element.47), channel_id=1, source_target_pairs={{1,2},{5,6},{9,10},{13,14},{17,18},{21,22},{25,26},{29,30},{0,3},{... | collective-permute-start | bytes 208904 | tf_op jit(solution)/shard_map/ppermute | solution.py:54
  5.5 1.9 %shard_map.150 = (bf16[16,2,128,128]{3,2,1,0:T(8,128)(2,1)S(1)}, bf16[16,128,128]{2,1,0:T(8,128)(2,1)S(1)}, s32[96,128]{1,0:T(8,128)S(1)}, f32[96,128]{1,0:T(8,1...) custom-call(f32[16,128,128]{2,1,0:T(8,128)S(1)} %get-tuple-element.3, ...), custom_call_target="tpu_custom_call" | custom-call | bytes 1048576 | tf_op jit(solution)/shard_map/pallas_call | solution.py:483
  7.4 0.0 collective-permute-done.in1
  7.4 0.8 %collective-permute-done.1.in0 = bf16[272,128]{1,0:T(8,128)(2,1)S(1)} collective-permute-done((bf16[272,128]{1,0:T(8,128)(2,1)S(1)}, bf16[272,128]{1,0:T(8,128)(2,1)S(1)}, u32[]{:S(2)}, u32[]{:S(2)}) %collective-permute-start.1) | collective-permute-done | bytes 69664 | tf_op jit(solution)/shard_map/ppermute | solution.py:54
  8.3 0.0 collective-permute-done.2.in2
  8.3 0.2 collective-permute-done.3.in3
  8.5 0.5 %shard_map.151 = (bf16[24,128,128]{2,1,0:T(8,128)(2,1)S(1)}, bf16[256,128]{1,0:T(8,128)(2,1)S(1)}, bf16[256,128]{1,0:T(8,128)(2,1)S(1)}, bf16[256,128]{1,0:T(8,128)(2,1)S(1)}, bf16[256,128]{1,0:T(8,128)(2,1)S(1)}) custom-call(s32[2,4]{1,0:T(2,128)S(1)} %get-tuple-element.41.near0, ...), custom_call_target="tpu_custom_call", output_to_operand_aliasing={{0}: (2, {})} | custom-call | flops 100663296 | tf_op jit(solution)/shard_map/pallas_call | solution.py:498
  9.0 2.5 %collective-permute-start.4 = (bf16[256,128]{1,0:T(8,128)(2,1)S(1)}, bf16[256,128]{1,0:T(8,128)(2,1)S(1)}, u32[]{:S(2)}, u32[]{:S(2)}) collective-permute-start(bf16[256,128]{1,0:T(8,128)(2,1)S(1)} %get-tuple-element.57), channel_id=1, source_target_pairs={{4,8},{5,9},{6,10},{7,11},{12,16},{13,17},{14,18},{15,19},{20,24},... | collective-permute-start | bytes 196616 | tf_op jit(solution)/shard_map/ppermute | solution.py:54
  11.5 0.0 collective-permute-start.5
  11.5 0.3 %collective-permute-start.6 = (bf16[256,128]{1,0:T(8,128)(2,1)S(1)}, bf16[256,128]{1,0:T(8,128)(2,1)S(1)}, u32[]{:S(2)}, u32[]{:S(2)}) collective-permute-start(bf16[256,128]{1,0:T(8,128)(2,1)S(1)} %get-tuple-element.59), channel_id=1, source_target_pairs={{0,1},{2,3},{4,5},{6,7},{8,9},{10,11},{12,13},{14,15},{16,17},{18,... | collective-permute-start | bytes 196616 | tf_op jit(solution)/shard_map/ppermute | solution.py:54
  11.8 1.3 %collective-permute-start.7 = (bf16[256,128]{1,0:T(8,128)(2,1)S(1)}, bf16[256,128]{1,0:T(8,128)(2,1)S(1)}, u32[]{:S(2)}, u32[]{:S(2)}) collective-permute-start(bf16[256,128]{1,0:T(8,128)(2,1)S(1)} %get-tuple-element.60), channel_id=1, source_target_pairs={{1,2},{5,6},{9,10},{13,14},{17,18},{21,22},{25,26},{29,30},{0,3},{... | collective-permute-start | bytes 196616 | tf_op jit(solution)/shard_map/ppermute | solution.py:54
  13.1 0.0 copy-done
  13.1 0.9 %shard_map.152 = (bf16[24,128,128]{2,1,0:T(8,128)(2,1)S(1)}, f32[96,128]{1,0:T(8,128)S(1)}) custom-call(s32[2,16]{1,0:T(2,128)S(1)} %get-tuple-element.40.links, bf16[24,128,128]{2,1,0:T(8,128)(2,1)S(1)} %get-tuple-element.51.extended, bf16[16,2,128,128]{3,2,1,0:T(8,128)(2,1)S(1)} %get-tuple-element.52.couple, ...), custom_call_target="tpu_custom_call" | custom-call | flops 201326592 | tf_op jit(solution)/shard_map/pallas_call | solution.py:509
  14.0 0.0 collective-permute-done.4.in1
  14.0 1.5 %collective-permute-done.5.in0 = bf16[256,128]{1,0:T(8,128)(2,1)S(1)} collective-permute-done((bf16[256,128]{1,0:T(8,128)(2,1)S(1)}, bf16[256,128]{1,0:T(8,128)(2,1)S(1)}, u32[]{:S(2)}, u32[]{:S(2)}) %collective-permute-start.5) | collective-permute-done | bytes 65568 | tf_op jit(solution)/shard_map/ppermute | solution.py:54
  15.5 0.0 collective-permute-done.6.in2
  15.5 0.4 %collective-permute-done.7.in3 = bf16[256,128]{1,0:T(8,128)(2,1)S(1)} collective-permute-done((bf16[256,128]{1,0:T(8,128)(2,1)S(1)}, bf16[256,128]{1,0:T(8,128)(2,1)S(1)}, u32[]{:S(2)}, u32[]{:S(2)}) %collective-permute-start.7) | collective-permute-done | bytes 65568 | tf_op jit(solution)/shard_map/ppermute | solution.py:54
  15.9 0.4 %shard_map.153 = (bf16[24,128,128]{2,1,0:T(8,128)(2,1)S(1)}, bf16[16,128]{1,0:T(8,128)(2,1)S(1)}, bf16[16,128]{1,0:T(8,128)(2,1)S(1)}, bf16[16,128]{1,0:T(8,128)(2,1)S(1)}, bf16[16,128]{1,0:T(8,128)(2,1)S(1)}) custom-call(s32[2,4]{1,0:T(2,128)S(1)} %get-tuple-element.41.near0, s32[2,4]{1,0:T(2,128)S(1)} %get-tuple-element.42.near1, ...), custom_call_target="tpu_custom_call", output_to_operand_aliasing={{0}: (2, {})} | custom-call | flops 12582912 | tf_op jit(solution)/shard_map/pallas_call | solution.py:517
  16.3 1.4 %collective-permute-start.10 = (bf16[16,128]{1,0:T(8,128)(2,1)S(1)}, bf16[16,128]{1,0:T(8,128)(2,1)S(1)}, u32[]{:S(2)}, u32[]{:S(2)}) collective-permute-start(bf16[16,128]{1,0:T(8,128)(2,1)S(1)} %get-tuple-element.67), channel_id=1, source_target_pairs={{0,4},{1,5},{2,6},{3,7},{8,12},{9,13},{10,14},{11,15},{16,20},{17,... | collective-permute-start | bytes 12296 | tf_op jit(solution)/shard_map/ppermute | solution.py:54
  17.7 0.3 %collective-permute-start.11 = (bf16[16,128]{1,0:T(8,128)(2,1)S(1)}, bf16[16,128]{1,0:T(8,128)(2,1)S(1)}, u32[]{:S(2)}, u32[]{:S(2)}) collective-permute-start(bf16[16,128]{1,0:T(8,128)(2,1)S(1)} %get-tuple-element.68), channel_id=1, source_target_pairs={{0,1},{2,3},{4,5},{6,7},{8,9},{10,11},{12,13},{14,15},{16,17},{18,... | collective-permute-start | bytes 12296 | tf_op jit(solution)/shard_map/ppermute | solution.py:54
  18.1 1.5 %collective-permute-start.8 = (bf16[16,128]{1,0:T(8,128)(2,1)S(1)}, bf16[16,128]{1,0:T(8,128)(2,1)S(1)}, u32[]{:S(2)}, u32[]{:S(2)}) collective-permute-start(bf16[16,128]{1,0:T(8,128)(2,1)S(1)} %get-tuple-element.65), channel_id=1, source_target_pairs={{4,8},{5,9},{6,10},{7,11},{12,16},{13,17},{14,18},{15,19},{20,24},... | collective-permute-start | bytes 12296 | tf_op jit(solution)/shard_map/ppermute | solution.py:54
  19.6 1.4 %collective-permute-start.9 = (bf16[16,128]{1,0:T(8,128)(2,1)S(1)}, bf16[16,128]{1,0:T(8,128)(2,1)S(1)}, u32[]{:S(2)}, u32[]{:S(2)}) collective-permute-start(bf16[16,128]{1,0:T(8,128)(2,1)S(1)} %get-tuple-element.66), channel_id=1, source_target_pairs={{1,2},{5,6},{9,10},{13,14},{17,18},{21,22},{25,26},{29,30},{0,3},{... | collective-permute-start | bytes 12296 | tf_op jit(solution)/shard_map/ppermute | solution.py:54
  20.9 1.6 %shard_map.154 = (f32[16,128,128]{2,1,0:T(8,128)}, f32[96,128]{1,0:T(8,128)S(1)}, bf16[24,128,128]{2,1,0:T(8,128)(2,1)S(1)}) custom-call(s32[2,16]{1,0:T(2,128)S(1)} %get-tuple-element.40.links, bf16[24,128,128]{2,1,0:T(8,128)(2,1)S(1)} %get-tuple-element.61._, bf16[256,128]{1,0:T(8,128)(2,1)S(1)} %collective-permute-done.5.in0, ...), custom_call_target="tpu_custom_call", output_to_operand_aliasing={{2}: (1, {})} | custom-call | flops 201326592 | tf_op jit(solution)/shard_map/pallas_call | solution.py:526
  22.6 0.0 collective-permute-done.10.in0
  22.6 0.0 collective-permute-done.11.in2
  22.6 0.0 collective-permute-done.8.in1
  22.6 0.0 collective-permute-done.9.in3
  22.6 0.9 %shard_map.155 = f32[64,128]{1,0:T(8,128)} custom-call(f32[96,128]{1,0:T(8,128)S(1)} %get-tuple-element.64.partial, bf16[16,128]{1,0:T(8,128)(2,1)S(1)} %collective-permute-done.8.in1, bf16[16,128]{1,0:T(8,128)(2,1)S(1)} %collective-permute-done.9.in3, bf16[16,128]{1,0:T(8,128)(2,1)S(1)} %collective-permute-done.10.in0, ...), custom_call_target="tpu_custom_call" | custom-call | tf_op jit(solution)/shard_map/pallas_call | solution.py:544
  (5 shorter events, 0.0 us)
Async XLA Ops:
  2.1 5.3 %collective-permute-start = (bf16[272,128]{1,0:T(8,128)(2,1)S(1)}, bf16[272,128]{1,0:T(8,128)(2,1)S(1)}, u32[]{:S(2)}, u32[]{:S(2)}) collective-permute-start(bf16[272,128]{1,0:T(8,128)(2,1)S(1)} %get-tuple-element.44), channel_id=1, source_target_pairs={{4,8},{5,9},{6,10},{7,11},{12,16},{13,17},{14,18},{15,19},{20,24},... | collective-permute-start | bytes 208904 | tf_op jit(solution)/shard_map/ppermute | solution.py:54
  3.4 4.9 %collective-permute-start.1 = (bf16[272,128]{1,0:T(8,128)(2,1)S(1)}, bf16[272,128]{1,0:T(8,128)(2,1)S(1)}, u32[]{:S(2)}, u32[]{:S(2)}) collective-permute-start(bf16[272,128]{1,0:T(8,128)(2,1)S(1)} %get-tuple-element.45), channel_id=1, source_target_pairs={{0,4},{1,5},{2,6},{3,7},{8,12},{9,13},{10,14},{11,15},{16,20},{17,... | collective-permute-start | bytes 208904 | tf_op jit(solution)/shard_map/ppermute | solution.py:54
  3.4 4.9 %collective-permute-start.2 = (bf16[272,128]{1,0:T(8,128)(2,1)S(1)}, bf16[272,128]{1,0:T(8,128)(2,1)S(1)}, u32[]{:S(2)}, u32[]{:S(2)}) collective-permute-start(bf16[272,128]{1,0:T(8,128)(2,1)S(1)} %get-tuple-element.46), channel_id=1, source_target_pairs={{0,1},{2,3},{4,5},{6,7},{8,9},{10,11},{12,13},{14,15},{16,17},{18,... | collective-permute-start | bytes 208904 | tf_op jit(solution)/shard_map/ppermute | solution.py:54
  4.4 4.1 %collective-permute-start.3 = (bf16[272,128]{1,0:T(8,128)(2,1)S(1)}, bf16[272,128]{1,0:T(8,128)(2,1)S(1)}, u32[]{:S(2)}, u32[]{:S(2)}) collective-permute-start(bf16[272,128]{1,0:T(8,128)(2,1)S(1)} %get-tuple-element.47), channel_id=1, source_target_pairs={{1,2},{5,6},{9,10},{13,14},{17,18},{21,22},{25,26},{29,30},{0,3},{... | collective-permute-start | bytes 208904 | tf_op jit(solution)/shard_map/ppermute | solution.py:54
  8.5 4.7 %copy-start = (f32[1,1,16,128,128]{4,3,2,1,0:T(8,128)S(1)}, f32[1,1,16,128,128]{4,3,2,1,0:T(8,128)}, u32[]{:S(2)}) copy-start(f32[1,1,16,128,128]{4,3,2,1,0:T(8,128)} %param.15) | copy-start | bytes 3145732
  9.0 5.0 %collective-permute-start.4 = (bf16[256,128]{1,0:T(8,128)(2,1)S(1)}, bf16[256,128]{1,0:T(8,128)(2,1)S(1)}, u32[]{:S(2)}, u32[]{:S(2)}) collective-permute-start(bf16[256,128]{1,0:T(8,128)(2,1)S(1)} %get-tuple-element.57), channel_id=1, source_target_pairs={{4,8},{5,9},{6,10},{7,11},{12,16},{13,17},{14,18},{15,19},{20,24},... | collective-permute-start | bytes 196616 | tf_op jit(solution)/shard_map/ppermute | solution.py:54
  11.5 4.0 %collective-permute-start.5 = (bf16[256,128]{1,0:T(8,128)(2,1)S(1)}, bf16[256,128]{1,0:T(8,128)(2,1)S(1)}, u32[]{:S(2)}, u32[]{:S(2)}) collective-permute-start(bf16[256,128]{1,0:T(8,128)(2,1)S(1)} %get-tuple-element.58), channel_id=1, source_target_pairs={{0,4},{1,5},{2,6},{3,7},{8,12},{9,13},{10,14},{11,15},{16,20},{17,... | collective-permute-start | bytes 196616 | tf_op jit(solution)/shard_map/ppermute | solution.py:54
  11.5 4.0 %collective-permute-start.6 = (bf16[256,128]{1,0:T(8,128)(2,1)S(1)}, bf16[256,128]{1,0:T(8,128)(2,1)S(1)}, u32[]{:S(2)}, u32[]{:S(2)}) collective-permute-start(bf16[256,128]{1,0:T(8,128)(2,1)S(1)} %get-tuple-element.59), channel_id=1, source_target_pairs={{0,1},{2,3},{4,5},{6,7},{8,9},{10,11},{12,13},{14,15},{16,17},{18,... | collective-permute-start | bytes 196616 | tf_op jit(solution)/shard_map/ppermute | solution.py:54
  11.8 4.1 %collective-permute-start.7 = (bf16[256,128]{1,0:T(8,128)(2,1)S(1)}, bf16[256,128]{1,0:T(8,128)(2,1)S(1)}, u32[]{:S(2)}, u32[]{:S(2)}) collective-permute-start(bf16[256,128]{1,0:T(8,128)(2,1)S(1)} %get-tuple-element.60), channel_id=1, source_target_pairs={{1,2},{5,6},{9,10},{13,14},{17,18},{21,22},{25,26},{29,30},{0,3},{... | collective-permute-start | bytes 196616 | tf_op jit(solution)/shard_map/ppermute | solution.py:54
  16.3 6.3 %collective-permute-start.10 = (bf16[16,128]{1,0:T(8,128)(2,1)S(1)}, bf16[16,128]{1,0:T(8,128)(2,1)S(1)}, u32[]{:S(2)}, u32[]{:S(2)}) collective-permute-start(bf16[16,128]{1,0:T(8,128)(2,1)S(1)} %get-tuple-element.67), channel_id=1, source_target_pairs={{0,4},{1,5},{2,6},{3,7},{8,12},{9,13},{10,14},{11,15},{16,20},{17,... | collective-permute-start | bytes 12296 | tf_op jit(solution)/shard_map/ppermute | solution.py:54
  17.7 4.9 %collective-permute-start.11 = (bf16[16,128]{1,0:T(8,128)(2,1)S(1)}, bf16[16,128]{1,0:T(8,128)(2,1)S(1)}, u32[]{:S(2)}, u32[]{:S(2)}) collective-permute-start(bf16[16,128]{1,0:T(8,128)(2,1)S(1)} %get-tuple-element.68), channel_id=1, source_target_pairs={{0,1},{2,3},{4,5},{6,7},{8,9},{10,11},{12,13},{14,15},{16,17},{18,... | collective-permute-start | bytes 12296 | tf_op jit(solution)/shard_map/ppermute | solution.py:54
  18.1 4.5 %collective-permute-start.8 = (bf16[16,128]{1,0:T(8,128)(2,1)S(1)}, bf16[16,128]{1,0:T(8,128)(2,1)S(1)}, u32[]{:S(2)}, u32[]{:S(2)}) collective-permute-start(bf16[16,128]{1,0:T(8,128)(2,1)S(1)} %get-tuple-element.65), channel_id=1, source_target_pairs={{4,8},{5,9},{6,10},{7,11},{12,16},{13,17},{14,18},{15,19},{20,24},... | collective-permute-start | bytes 12296 | tf_op jit(solution)/shard_map/ppermute | solution.py:54
  19.6 3.1 %collective-permute-start.9 = (bf16[16,128]{1,0:T(8,128)(2,1)S(1)}, bf16[16,128]{1,0:T(8,128)(2,1)S(1)}, u32[]{:S(2)}, u32[]{:S(2)}) collective-permute-start(bf16[16,128]{1,0:T(8,128)(2,1)S(1)} %get-tuple-element.66), channel_id=1, source_target_pairs={{1,2},{5,6},{9,10},{13,14},{17,18},{21,22},{25,26},{29,30},{0,3},{... | collective-permute-start | bytes 12296 | tf_op jit(solution)/shard_map/ppermute | solution.py:54

commit v7 on v6

--- a/solution.py
+++ b/solution.py
@@ -161,7 +161,7 @@
 
 def fetch_kernel(mesh_dims, count, guess, sends, rhs_far, *refs):
     fars, nears = refs[:count], refs[count : 2 * count]
-    near0, near1, extended, couple_listed, inverse_listed, rhs_listed, arrivals = refs[2 * count :]
+    near0, near1, own, couple_listed, inverse_listed, rhs_listed, arrivals = refs[2 * count :]
     listed = sends[...]
     columns = []
     for pairing, (side, _) in enumerate(sides_of(*mesh_dims)):
@@ -182,7 +182,7 @@
     for copy in copies:
         copy.start()
     for block in range(guess.shape[0]):
-        extended[block] = guess[block].astype(jnp.bfloat16)
+        own[block] = guess[block].astype(jnp.bfloat16)
     for copy in copies:
         copy.wait()
     couple, inverse, links = nears[0], nears[1], nears[-1][...]
@@ -211,24 +211,26 @@
     return [product(part, inverse[block]) for part, block in zip(resid, blocks)]
 
 
-def land(extended, places, arrived, blocks_sent, rows):
-    own_count = extended.shape[0] - 4 * blocks_sent
-    size = extended.shape[1]
+def extend(extended, own, places, arrived, blocks_sent):
+    own_count, size = own.shape[:2]
+    rows = extended.shape[1]
+    for block in range(own_count):
+        extended[block] = own[block, 0:rows, :]
     for (side, exists), came in zip(places, arrived):
         for block in range(blocks_sent):
             value = came[pl.ds(block * size, rows), :]
             value = jnp.where(exists, value, jnp.zeros_like(value))
-            extended[own_count + side * blocks_sent + block, 0:rows, :] = value
+            extended[own_count + side * blocks_sent + block] = value
 
 
 def first_edge_kernel(
-    mesh_dims, near0, near1, _, in1, in0, in2, in3, couple, inverse, rhs,
+    mesh_dims, near0, near1, own, in1, in0, in2, in3, couple, inverse, rhs,
     extended, out0, out1, out2, out3,
 ):
     size = extended.shape[1]
     slots = near0.shape[0]
     links = listed_links(near0, near1)
-    land(extended, sides_of(*mesh_dims), (in0, in1, in2, in3), slots, size)
+    extend(extended, own, sides_of(*mesh_dims), (in0, in1, in2, in3), slots)
     fresh = relax(extended, couple, inverse, rhs, range(len(links)), links, size)
     for pairing, out in enumerate((out0, out1, out2, out3)):
         for slot in range(slots):
@@ -285,12 +287,12 @@
 
 
 def second_edge_kernel(
-    mesh_dims, near0, near1, _, in1, in0, in2, in3, couple, inverse, rhs,
-    extended, out0, out1, out2, out3,
+    mesh_dims, near0, near1, own, in1, in0, in2, in3, couple, inverse, rhs,
+    out0, out1, out2, out3, extended,
 ):
     slots = near0.shape[0]
     links = listed_links(near0, near1)
-    land(extended, sides_of(*mesh_dims), (in0, in1, in2, in3), slots, tail_rows)
+    extend(extended, own, sides_of(*mesh_dims), (in0, in1, in2, in3), slots)
     fresh = relax(extended, couple, inverse, rhs, range(len(links)), links, tail_rows)
     for pairing, out in enumerate((out0, out1, out2, out3)):
         rows = [fresh[pairing * slots + slot][0:1, :] for slot in range(slots)]
@@ -299,10 +301,10 @@
 
 
 def second_sweep_kernel(
-    mesh_dims, blocks_sent, links, _, in0, in1, in2, in3, couple, inverse, rhs, cell_faces,
+    mesh_dims, blocks_sent, links, own, in1, in0, in2, in3, couple, inverse, rhs, cell_faces,
     traces, partial, extended, fresh, column, departures,
 ):
-    land(extended, sides_of(*mesh_dims), (in0, in1, in2, in3), blocks_sent, extended.shape[1])
+    extend(extended, own, sides_of(*mesh_dims), (in0, in1, in2, in3), blocks_sent)
     stores = []
     for blocks, pairs in in_parts(links):
         values = relax(extended, couple, inverse, rhs, blocks, pairs, extended.shape[1])
@@ -375,14 +377,13 @@
 far = pl.BlockSpec(memory_space=pl.ANY)
 
 
-def call(kernel, outs, specs, scratch=(), flops=0, traffic=0, out_specs=None, aliases=None):
+def call(kernel, outs, specs, scratch=(), flops=0, traffic=0, out_specs=None):
     return pl.pallas_call(
         kernel,
         out_shape=outs,
         in_specs=specs,
         out_specs=[whole] * len(outs) if out_specs is None else out_specs,
         scratch_shapes=list(scratch),
-        input_output_aliases=aliases or {},
         compiler_params=pltpu.CompilerParams(vmem_limit_bytes=vmem_bytes),
         cost_estimate=pl.CostEstimate(flops=flops, bytes_accessed=traffic, transcendentals=0),
     )
@@ -478,13 +479,13 @@
         links,
         near0,
         near1,
-        extended,
+        own,
         *listed,
     ) = call(
         functools.partial(fetch_kernel, mesh_dims, len(remote)),
         [like(array) for array in remote]
         + [like(sends)] * 2
-        + [jax.ShapeDtypeStruct(widened, half)]
+        + [jax.ShapeDtypeStruct(guess.shape, half)]
         + [
             jax.ShapeDtypeStruct((4 * blocks_sent,) + array.shape[1:], array.dtype)
             for array in (couple, inverse, rhs)
@@ -497,49 +498,45 @@
     sweep_flops = 6 * blocks * columns * size * size
     extended, *packed = call(
         functools.partial(first_edge_kernel, mesh_dims),
-        [like(extended)] + [jax.ShapeDtypeStruct((halo_rows, size), half)] * 4,
+        [jax.ShapeDtypeStruct(widened, half)]
+        + [jax.ShapeDtypeStruct((halo_rows, size), half)] * 4,
         [whole] * 10,
         flops=sweep_flops // 2,
-        aliases={2: 0},
-    )(near0, near1, extended, *(arrived[k] for k in (1, 0, 2, 3)), *listed)
+    )(near0, near1, own, *(arrived[k] for k in (1, 0, 2, 3)), *listed)
     swept = trade(packed, plans)
 
     tails = [piece[halo_rows:] for piece in arrived]
     cell_rows = -(-(groups + halves) // 8) * 8
-    extended, across = call(
+    own, across = call(
         functools.partial(first_sweep_kernel, mesh_dims, halves),
-        [like(extended), jax.ShapeDtypeStruct(neighbours.shape, single)],
+        [like(own), jax.ShapeDtypeStruct(neighbours.shape, single)],
         [whole] * 11,
         [pltpu.VMEM((6 * cell_rows, lane_width), single)],
         sweep_flops,
     )(links, extended, couple, inverse, rhs, sat, neighbours, *tails)
 
-    extended, *packed = call(
+    packed = call(
         functools.partial(second_edge_kernel, mesh_dims),
-        [like(extended)] + [jax.ShapeDtypeStruct((tail_rows, size), half)] * 4,
+        [jax.ShapeDtypeStruct((tail_rows, size), half)] * 4,
         [whole] * 10,
-        flops=sweep_flops // 16,
-        aliases={2: 0},
-    )(near0, near1, extended, *(swept[k] for k in (1, 0, 2, 3)), *listed)
+        [pltpu.VMEM((extended_blocks, tail_rows, size), half)],
+        sweep_flops // 16,
+    )(near0, near1, own, *(swept[k] for k in (1, 0, 2, 3)), *listed)
     edges = trade(packed, plans)
 
-    traces, partial, _ = call(
+    traces, partial = call(
         functools.partial(second_sweep_kernel, mesh_dims, blocks_sent),
-        [
-            jax.ShapeDtypeStruct(guess.shape, single),
-            jax.ShapeDtypeStruct(coeff.shape, single),
-            like(extended),
-        ],
+        [jax.ShapeDtypeStruct(guess.shape, single), jax.ShapeDtypeStruct(coeff.shape, single)],
         [whole] * 10,
         [
+            pltpu.VMEM(widened, half),
             pltpu.VMEM(guess.shape, single),
             pltpu.VMEM((blocks, size), single),
             pltpu.SemaphoreType.DMA((blocks,)),
         ],
         sweep_flops,
-        out_specs=[far, whole, whole],
-        aliases={1: 2},
-    )(links, extended, *swept, couple, inverse, rhs, cell_faces)
+        out_specs=[far, whole],
+    )(links, own, *(swept[k] for k in (1, 0, 2, 3)), couple, inverse, rhs, cell_faces)
 
     (following,) = call(
         functools.partial(cells_kernel, mesh_dims, blocks, blocks_sent),

time: 23.7 us -> 23.8 us (level)
  no operation moved by 1% of the time
where the time goes in v7:
time: 23.8 us; the launch traced here: 23.6 us
  starting transfers between devices  12.1 us (51%)
  Pallas kernels  7.78 us (33%)
  waiting for transfers between devices  2.95 us (12%)
  between operations  0.74 us (3%)
    ppermute x12, starting transfers between devices, trade(): lax.ppermute(piece, axes, plan)  12.1 us
    ppermute x12, waiting for transfers between devices, trade(): lax.ppermute(piece, axes, plan)  2.95 us
    pallas_call x1, Pallas kernels, per_device(): call(functools.partial(fetch_kernel, mesh_dims, len(remote)), [like(array...  1.94 us
    pallas_call x1, Pallas kernels, per_device(): call(functools.partial(second_sweep_kernel, mesh_dims, blocks_sent), [jax...  1.67 us
    pallas_call x1, Pallas kernels, per_device(): call(functools.partial(pack_kernel, mesh_dims), [jax.ShapeDtypeStruct((ha...  1.47 us
    pallas_call x1, Pallas kernels, per_device(): call(functools.partial(cells_kernel, mesh_dims, blocks, blocks_sent), [li...  0.89 us
    pallas_call x1, Pallas kernels, per_device(): call(functools.partial(first_sweep_kernel, mesh_dims, halves), [like(own)...  0.87 us
    pallas_call x1, Pallas kernels, per_device(): call(functools.partial(first_edge_kernel, mesh_dims), [jax.ShapeDtypeStru...  0.53 us
  transfers between devices with their start and end apart: 12, of which 4 were waited for; matrix products, arithmetic and copies ran while one was open for 0% of the time, Pallas kernels for 19%

profile of v7, /device:TPU:5, one launch (start us, length us, event | category | flops | bytes accessed | tf_op | source)
XLA Modules:
  0.0 23.6 jit_solution(8559531206693177578)
XLA Ops:
  0.6 1.5 %shard_map.149 = (bf16[272,128]{1,0:T(8,128)(2,1)S(1)}, bf16[272,128]{1,0:T(8,128)(2,1)S(1)}, bf16[272,128]{1,0:T(8,128)(2,1)S(1)}, bf16[272,128]{1,0:T(8,128)(2...) custom-call(s32[2,4]{1,0:T(2,128)} %bitcast.48, f32[16,128,128]{2,1,0:T(8,128)} %bitcast.36, s32[8,128]{1,0:T(8,128)} %bitcast.47, ...), custom_call_target="tpu_custom_call" | custom-call | tf_op jit(solution)/shard_map/pallas_call | solution.py:443
  2.1 1.3 %collective-permute-start = (bf16[272,128]{1,0:T(8,128)(2,1)S(1)}, bf16[272,128]{1,0:T(8,128)(2,1)S(1)}, u32[]{:S(2)}, u32[]{:S(2)}) collective-permute-start(bf16[272,128]{1,0:T(8,128)(2,1)S(1)} %get-tuple-element.43), channel_id=1, source_target_pairs={{4,8},{5,9},{6,10},{7,11},{12,16},{13,17},{14,18},{15,19},{20,24},... | collective-permute-start | bytes 208904 | tf_op jit(solution)/shard_map/ppermute | solution.py:54
  3.4 0.0 collective-permute-start.1
  3.4 1.0 %collective-permute-start.2 = (bf16[272,128]{1,0:T(8,128)(2,1)S(1)}, bf16[272,128]{1,0:T(8,128)(2,1)S(1)}, u32[]{:S(2)}, u32[]{:S(2)}) collective-permute-start(bf16[272,128]{1,0:T(8,128)(2,1)S(1)} %get-tuple-element.45), channel_id=1, source_target_pairs={{0,1},{2,3},{4,5},{6,7},{8,9},{10,11},{12,13},{14,15},{16,17},{18,... | collective-permute-start | bytes 208904 | tf_op jit(solution)/shard_map/ppermute | solution.py:54
  4.4 1.1 %collective-permute-start.3 = (bf16[272,128]{1,0:T(8,128)(2,1)S(1)}, bf16[272,128]{1,0:T(8,128)(2,1)S(1)}, u32[]{:S(2)}, u32[]{:S(2)}) collective-permute-start(bf16[272,128]{1,0:T(8,128)(2,1)S(1)} %get-tuple-element.46), channel_id=1, source_target_pairs={{1,2},{5,6},{9,10},{13,14},{17,18},{21,22},{25,26},{29,30},{0,3},{... | collective-permute-start | bytes 208904 | tf_op jit(solution)/shard_map/ppermute | solution.py:54
  5.5 1.9 %shard_map.150 = (bf16[16,2,128,128]{3,2,1,0:T(8,128)(2,1)S(1)}, bf16[16,128,128]{2,1,0:T(8,128)(2,1)S(1)}, s32[96,128]{1,0:T(8,128)S(1)}, f32[96,128]{1,0:T(8,1...) custom-call(f32[16,128,128]{2,1,0:T(8,128)S(1)} %get-tuple-element.3, ...), custom_call_target="tpu_custom_call" | custom-call | bytes 1048576 | tf_op jit(solution)/shard_map/pallas_call | solution.py:484
  7.4 0.0 collective-permute-done.in1
  7.4 0.8 %collective-permute-done.1.in0 = bf16[272,128]{1,0:T(8,128)(2,1)S(1)} collective-permute-done((bf16[272,128]{1,0:T(8,128)(2,1)S(1)}, bf16[272,128]{1,0:T(8,128)(2,1)S(1)}, u32[]{:S(2)}, u32[]{:S(2)}) %collective-permute-start.1) | collective-permute-done | bytes 69664 | tf_op jit(solution)/shard_map/ppermute | solution.py:54
  8.3 0.0 collective-permute-done.2.in2
  8.3 0.2 collective-permute-done.3.in3
  8.5 0.5 %shard_map.151 = (bf16[24,128,128]{2,1,0:T(8,128)(2,1)S(1)}, bf16[256,128]{1,0:T(8,128)(2,1)S(1)}, bf16[256,128]{1,0:T(8,128)(2,1)S(1)}, bf16[256,128]{1,0:T(8,128)(2,1)S(1)}, bf16[256,128]{1,0:T(8,128)(2,1)S(1)}) custom-call(s32[2,4]{1,0:T(2,128)S(1)} %get-tuple-element.40.near0, s32[2,4]{1,0:T(2,128)S(1)} %get-tuple-element.41.near1, ...), custom_call_target="tpu_custom_call" | custom-call | flops 100663296 | tf_op jit(solution)/shard_map/pallas_call | solution.py:499
  9.0 2.5 %collective-permute-start.4 = (bf16[256,128]{1,0:T(8,128)(2,1)S(1)}, bf16[256,128]{1,0:T(8,128)(2,1)S(1)}, u32[]{:S(2)}, u32[]{:S(2)}) collective-permute-start(bf16[256,128]{1,0:T(8,128)(2,1)S(1)} %get-tuple-element.56), channel_id=1, source_target_pairs={{4,8},{5,9},{6,10},{7,11},{12,16},{13,17},{14,18},{15,19},{20,24},... | collective-permute-start | bytes 196616 | tf_op jit(solution)/shard_map/ppermute | solution.py:54
  11.5 0.0 collective-permute-start.5
  11.5 0.3 %collective-permute-start.6 = (bf16[256,128]{1,0:T(8,128)(2,1)S(1)}, bf16[256,128]{1,0:T(8,128)(2,1)S(1)}, u32[]{:S(2)}, u32[]{:S(2)}) collective-permute-start(bf16[256,128]{1,0:T(8,128)(2,1)S(1)} %get-tuple-element.58), channel_id=1, source_target_pairs={{0,1},{2,3},{4,5},{6,7},{8,9},{10,11},{12,13},{14,15},{16,17},{18,... | collective-permute-start | bytes 196616 | tf_op jit(solution)/shard_map/ppermute | solution.py:54
  11.9 1.3 %collective-permute-start.7 = (bf16[256,128]{1,0:T(8,128)(2,1)S(1)}, bf16[256,128]{1,0:T(8,128)(2,1)S(1)}, u32[]{:S(2)}, u32[]{:S(2)}) collective-permute-start(bf16[256,128]{1,0:T(8,128)(2,1)S(1)} %get-tuple-element.59), channel_id=1, source_target_pairs={{1,2},{5,6},{9,10},{13,14},{17,18},{21,22},{25,26},{29,30},{0,3},{... | collective-permute-start | bytes 196616 | tf_op jit(solution)/shard_map/ppermute | solution.py:54
  13.2 0.0 copy-done
  13.2 0.9 %shard_map.152 = (bf16[16,128,128]{2,1,0:T(8,128)(2,1)S(1)}, f32[96,128]{1,0:T(8,128)S(1)}) custom-call(s32[2,16]{1,0:T(2,128)S(1)} %get-tuple-element.39.links, bf16[24,128,128]{2,1,0:T(8,128)(2,1)S(1)} %get-tuple-element.50.extended, bf16[16,2,128,128]{3,2,1,0:T(8,128)(2,1)S(1)} %get-tuple-element.51.couple, ...), custom_call_target="tpu_custom_call" | custom-call | flops 201326592 | tf_op jit(solution)/shard_map/pallas_call | solution.py:510
  14.0 0.0 collective-permute-done.4.in1
  14.1 1.5 %collective-permute-done.5.in0 = bf16[256,128]{1,0:T(8,128)(2,1)S(1)} collective-permute-done((bf16[256,128]{1,0:T(8,128)(2,1)S(1)}, bf16[256,128]{1,0:T(8,128)(2,1)S(1)}, u32[]{:S(2)}, u32[]{:S(2)}) %collective-permute-start.5) | collective-permute-done | bytes 65568 | tf_op jit(solution)/shard_map/ppermute | solution.py:54
  15.5 0.0 collective-permute-done.6.in2
  15.5 0.4 %collective-permute-done.7.in3 = bf16[256,128]{1,0:T(8,128)(2,1)S(1)} collective-permute-done((bf16[256,128]{1,0:T(8,128)(2,1)S(1)}, bf16[256,128]{1,0:T(8,128)(2,1)S(1)}, u32[]{:S(2)}, u32[]{:S(2)}) %collective-permute-start.7) | collective-permute-done | bytes 65568 | tf_op jit(solution)/shard_map/ppermute | solution.py:54
  16.0 0.4 %shard_map.154 = (bf16[16,128]{1,0:T(8,128)(2,1)S(1)}, bf16[16,128]{1,0:T(8,128)(2,1)S(1)}, bf16[16,128]{1,0:T(8,128)(2,1)S(1)}, bf16[16,128]{1,0:T(8,128)(2,1)S(1)}) custom-call(s32[2,4]{1,0:T(2,128)S(1)} %get-tuple-element.40.near0, s32[2,4]{1,0:T(2,128)S(1)} %get-tuple-element.41.near1, bf16[16,128,128]{2,1,0:T(8,128)(2,1)S(1)} %get-tuple-element.55.own, ...), custom_call_target="tpu_custom_call" | custom-call | flops 12582912 | tf_op jit(solution)/shard_map/pallas_call | solution.py:518
  16.4 1.4 %collective-permute-start.10 = (bf16[16,128]{1,0:T(8,128)(2,1)S(1)}, bf16[16,128]{1,0:T(8,128)(2,1)S(1)}, u32[]{:S(2)}, u32[]{:S(2)}) collective-permute-start(bf16[16,128]{1,0:T(8,128)(2,1)S(1)} %get-tuple-element.65), channel_id=1, source_target_pairs={{0,4},{1,5},{2,6},{3,7},{8,12},{9,13},{10,14},{11,15},{16,20},{17,... | collective-permute-start | bytes 12296 | tf_op jit(solution)/shard_map/ppermute | solution.py:54
  17.8 0.3 %collective-permute-start.11 = (bf16[16,128]{1,0:T(8,128)(2,1)S(1)}, bf16[16,128]{1,0:T(8,128)(2,1)S(1)}, u32[]{:S(2)}, u32[]{:S(2)}) collective-permute-start(bf16[16,128]{1,0:T(8,128)(2,1)S(1)} %get-tuple-element.66), channel_id=1, source_target_pairs={{0,1},{2,3},{4,5},{6,7},{8,9},{10,11},{12,13},{14,15},{16,17},{18,... | collective-permute-start | bytes 12296 | tf_op jit(solution)/shard_map/ppermute | solution.py:54
  18.1 1.5 %collective-permute-start.8 = (bf16[16,128]{1,0:T(8,128)(2,1)S(1)}, bf16[16,128]{1,0:T(8,128)(2,1)S(1)}, u32[]{:S(2)}, u32[]{:S(2)}) collective-permute-start(bf16[16,128]{1,0:T(8,128)(2,1)S(1)} %get-tuple-element.63), channel_id=1, source_target_pairs={{4,8},{5,9},{6,10},{7,11},{12,16},{13,17},{14,18},{15,19},{20,24},... | collective-permute-start | bytes 12296 | tf_op jit(solution)/shard_map/ppermute | solution.py:54
  19.6 1.4 %collective-permute-start.9 = (bf16[16,128]{1,0:T(8,128)(2,1)S(1)}, bf16[16,128]{1,0:T(8,128)(2,1)S(1)}, u32[]{:S(2)}, u32[]{:S(2)}) collective-permute-start(bf16[16,128]{1,0:T(8,128)(2,1)S(1)} %get-tuple-element.64), channel_id=1, source_target_pairs={{1,2},{5,6},{9,10},{13,14},{17,18},{21,22},{25,26},{29,30},{0,3},{... | collective-permute-start | bytes 12296 | tf_op jit(solution)/shard_map/ppermute | solution.py:54
  21.0 1.7 %shard_map.153 = (f32[16,128,128]{2,1,0:T(8,128)}, f32[96,128]{1,0:T(8,128)S(1)}) custom-call(s32[2,16]{1,0:T(2,128)S(1)} %get-tuple-element.39.links, bf16[16,128,128]{2,1,0:T(8,128)(2,1)S(1)} %get-tuple-element.55.own, bf16[256,128]{1,0:T(8,128)(2,1)S(1)} %collective-permute-done.4.in1, bf16[256,128]{1,0:T(8,128)(2,1)S(1)} %collective-permute-done.5.in0, ...), custom_call_target="tpu_custom_call" | custom-call | flops 201326592 | tf_op jit(solution)/shard_map/pallas_call | solution.py:527
  22.7 0.0 collective-permute-done.10.in0
  22.7 0.0 collective-permute-done.11.in2
  22.7 0.0 collective-permute-done.8.in1
  22.7 0.0 collective-permute-done.9.in3
  22.7 0.9 %shard_map.155 = f32[64,128]{1,0:T(8,128)} custom-call(f32[96,128]{1,0:T(8,128)S(1)} %get-tuple-element.62.partial, bf16[16,128]{1,0:T(8,128)(2,1)S(1)} %collective-permute-done.8.in1, bf16[16,128]{1,0:T(8,128)(2,1)S(1)} %collective-permute-done.9.in3, bf16[16,128]{1,0:T(8,128)(2,1)S(1)} %collective-permute-done.10.in0, ...), custom_call_target="tpu_custom_call" | custom-call | tf_op jit(solution)/shard_map/pallas_call | solution.py:541
  (5 shorter events, 0.0 us)
Async XLA Ops:
  2.1 5.3 %collective-permute-start = (bf16[272,128]{1,0:T(8,128)(2,1)S(1)}, bf16[272,128]{1,0:T(8,128)(2,1)S(1)}, u32[]{:S(2)}, u32[]{:S(2)}) collective-permute-start(bf16[272,128]{1,0:T(8,128)(2,1)S(1)} %get-tuple-element.43), channel_id=1, source_target_pairs={{4,8},{5,9},{6,10},{7,11},{12,16},{13,17},{14,18},{15,19},{20,24},... | collective-permute-start | bytes 208904 | tf_op jit(solution)/shard_map/ppermute | solution.py:54
  3.4 4.9 %collective-permute-start.1 = (bf16[272,128]{1,0:T(8,128)(2,1)S(1)}, bf16[272,128]{1,0:T(8,128)(2,1)S(1)}, u32[]{:S(2)}, u32[]{:S(2)}) collective-permute-start(bf16[272,128]{1,0:T(8,128)(2,1)S(1)} %get-tuple-element.44), channel_id=1, source_target_pairs={{0,4},{1,5},{2,6},{3,7},{8,12},{9,13},{10,14},{11,15},{16,20},{17,... | collective-permute-start | bytes 208904 | tf_op jit(solution)/shard_map/ppermute | solution.py:54
  3.4 4.9 %collective-permute-start.2 = (bf16[272,128]{1,0:T(8,128)(2,1)S(1)}, bf16[272,128]{1,0:T(8,128)(2,1)S(1)}, u32[]{:S(2)}, u32[]{:S(2)}) collective-permute-start(bf16[272,128]{1,0:T(8,128)(2,1)S(1)} %get-tuple-element.45), channel_id=1, source_target_pairs={{0,1},{2,3},{4,5},{6,7},{8,9},{10,11},{12,13},{14,15},{16,17},{18,... | collective-permute-start | bytes 208904 | tf_op jit(solution)/shard_map/ppermute | solution.py:54
  4.4 4.1 %collective-permute-start.3 = (bf16[272,128]{1,0:T(8,128)(2,1)S(1)}, bf16[272,128]{1,0:T(8,128)(2,1)S(1)}, u32[]{:S(2)}, u32[]{:S(2)}) collective-permute-start(bf16[272,128]{1,0:T(8,128)(2,1)S(1)} %get-tuple-element.46), channel_id=1, source_target_pairs={{1,2},{5,6},{9,10},{13,14},{17,18},{21,22},{25,26},{29,30},{0,3},{... | collective-permute-start | bytes 208904 | tf_op jit(solution)/shard_map/ppermute | solution.py:54
  8.5 4.7 %copy-start = (f32[1,1,16,128,128]{4,3,2,1,0:T(8,128)S(1)}, f32[1,1,16,128,128]{4,3,2,1,0:T(8,128)}, u32[]{:S(2)}) copy-start(f32[1,1,16,128,128]{4,3,2,1,0:T(8,128)} %param.15) | copy-start | bytes 3145732
  9.0 5.0 %collective-permute-start.4 = (bf16[256,128]{1,0:T(8,128)(2,1)S(1)}, bf16[256,128]{1,0:T(8,128)(2,1)S(1)}, u32[]{:S(2)}, u32[]{:S(2)}) collective-permute-start(bf16[256,128]{1,0:T(8,128)(2,1)S(1)} %get-tuple-element.56), channel_id=1, source_target_pairs={{4,8},{5,9},{6,10},{7,11},{12,16},{13,17},{14,18},{15,19},{20,24},... | collective-permute-start | bytes 196616 | tf_op jit(solution)/shard_map/ppermute | solution.py:54
  11.5 4.0 %collective-permute-start.5 = (bf16[256,128]{1,0:T(8,128)(2,1)S(1)}, bf16[256,128]{1,0:T(8,128)(2,1)S(1)}, u32[]{:S(2)}, u32[]{:S(2)}) collective-permute-start(bf16[256,128]{1,0:T(8,128)(2,1)S(1)} %get-tuple-element.57), channel_id=1, source_target_pairs={{0,4},{1,5},{2,6},{3,7},{8,12},{9,13},{10,14},{11,15},{16,20},{17,... | collective-permute-start | bytes 196616 | tf_op jit(solution)/shard_map/ppermute | solution.py:54
  11.5 4.0 %collective-permute-start.6 = (bf16[256,128]{1,0:T(8,128)(2,1)S(1)}, bf16[256,128]{1,0:T(8,128)(2,1)S(1)}, u32[]{:S(2)}, u32[]{:S(2)}) collective-permute-start(bf16[256,128]{1,0:T(8,128)(2,1)S(1)} %get-tuple-element.58), channel_id=1, source_target_pairs={{0,1},{2,3},{4,5},{6,7},{8,9},{10,11},{12,13},{14,15},{16,17},{18,... | collective-permute-start | bytes 196616 | tf_op jit(solution)/shard_map/ppermute | solution.py:54
  11.9 4.1 %collective-permute-start.7 = (bf16[256,128]{1,0:T(8,128)(2,1)S(1)}, bf16[256,128]{1,0:T(8,128)(2,1)S(1)}, u32[]{:S(2)}, u32[]{:S(2)}) collective-permute-start(bf16[256,128]{1,0:T(8,128)(2,1)S(1)} %get-tuple-element.59), channel_id=1, source_target_pairs={{1,2},{5,6},{9,10},{13,14},{17,18},{21,22},{25,26},{29,30},{0,3},{... | collective-permute-start | bytes 196616 | tf_op jit(solution)/shard_map/ppermute | solution.py:54
  16.4 6.3 %collective-permute-start.10 = (bf16[16,128]{1,0:T(8,128)(2,1)S(1)}, bf16[16,128]{1,0:T(8,128)(2,1)S(1)}, u32[]{:S(2)}, u32[]{:S(2)}) collective-permute-start(bf16[16,128]{1,0:T(8,128)(2,1)S(1)} %get-tuple-element.65), channel_id=1, source_target_pairs={{0,4},{1,5},{2,6},{3,7},{8,12},{9,13},{10,14},{11,15},{16,20},{17,... | collective-permute-start | bytes 12296 | tf_op jit(solution)/shard_map/ppermute | solution.py:54
  17.8 4.9 %collective-permute-start.11 = (bf16[16,128]{1,0:T(8,128)(2,1)S(1)}, bf16[16,128]{1,0:T(8,128)(2,1)S(1)}, u32[]{:S(2)}, u32[]{:S(2)}) collective-permute-start(bf16[16,128]{1,0:T(8,128)(2,1)S(1)} %get-tuple-element.66), channel_id=1, source_target_pairs={{0,1},{2,3},{4,5},{6,7},{8,9},{10,11},{12,13},{14,15},{16,17},{18,... | collective-permute-start | bytes 12296 | tf_op jit(solution)/shard_map/ppermute | solution.py:54
  18.1 4.6 %collective-permute-start.8 = (bf16[16,128]{1,0:T(8,128)(2,1)S(1)}, bf16[16,128]{1,0:T(8,128)(2,1)S(1)}, u32[]{:S(2)}, u32[]{:S(2)}) collective-permute-start(bf16[16,128]{1,0:T(8,128)(2,1)S(1)} %get-tuple-element.63), channel_id=1, source_target_pairs={{4,8},{5,9},{6,10},{7,11},{12,16},{13,17},{14,18},{15,19},{20,24},... | collective-permute-start | bytes 12296 | tf_op jit(solution)/shard_map/ppermute | solution.py:54
  19.6 3.1 %collective-permute-start.9 = (bf16[16,128]{1,0:T(8,128)(2,1)S(1)}, bf16[16,128]{1,0:T(8,128)(2,1)S(1)}, u32[]{:S(2)}, u32[]{:S(2)}) collective-permute-start(bf16[16,128]{1,0:T(8,128)(2,1)S(1)} %get-tuple-element.64), channel_id=1, source_target_pairs={{1,2},{5,6},{9,10},{13,14},{17,18},{21,22},{25,26},{29,30},{0,3},{... | collective-permute-start | bytes 12296 | tf_op jit(solution)/shard_map/ppermute | solution.py:54

commit v8 on v6

--- a/solution.py
+++ b/solution.py
@@ -240,8 +240,8 @@
     return [spread(table[pl.ds(first_row + row, 1), :]) for row in range(count)]
 
 
-def look_up(rows, high, low, value):
-    for number, row in enumerate(rows):
+def look_up(rows, high, low, value, numbers=None):
+    for number, row in zip(numbers or range(len(rows)), rows):
         value = jnp.where(high == number, take_lanes(row, low), value)
     return value
 
@@ -325,18 +325,19 @@
 
 def cells_kernel(
     mesh_dims, blocks, blocks_sent, partial, in1, in3, in0, in2, across,
-    cell_faces, coeff, source, flags, sat, ratio, out, faces,
+    cell_faces, coeff, source, flags, sat, ratio, out,
 ):
     places = sides_of(*mesh_dims)
     groups = sat.shape[0] // 4
+    edge_rows, numbers = [], []
     for (side, exists), came in zip(places, (in0, in1, in2, in3)):
         value = came[...].astype(jnp.float32)[0:blocks_sent]
         value = jnp.where(exists, value, jnp.zeros_like(value))
         for block in range(blocks_sent):
-            faces[pl.ds(side * blocks_sent + block, 1), :] = value[block : block + 1]
+            edge_rows.append(spread(value[block : block + 1]))
+            numbers.append(side * blocks_sent + block)
     modes = [sat[pl.ds(mode, groups, stride=4), :] for mode in range(4)]
     weights = [coeff[pl.ds(face * groups, groups), :] for face in range(6)]
-    edge_rows = spread_rows(faces, 0, 4 * blocks_sent)
     traces = []
     for face in range(6):
         parts = []
@@ -344,7 +345,7 @@
             rows = pl.ds(face * groups + start, 8)
             index = cell_faces[rows, :]
             high, low = (index >> 7) - blocks, index & (lane_width - 1)
-            parts.append(look_up(edge_rows, high, low, partial[rows, :]))
+            parts.append(look_up(edge_rows, high, low, partial[rows, :], numbers))
         traces.append(jnp.concatenate(parts, 0))
     total = weights[0]
     gained = source[...] + weights[0] * traces[0]
@@ -386,6 +387,10 @@
         compiler_params=pltpu.CompilerParams(vmem_limit_bytes=vmem_bytes),
         cost_estimate=pl.CostEstimate(flops=flops, bytes_accessed=traffic, transcendentals=0),
     )
+
+
+def keep_near(array):
+    return pltpu.with_memory_space_constraint(array, pltpu.VMEM)
 
 
 def keep_far(array):
@@ -501,7 +506,7 @@
         [whole] * 10,
         flops=sweep_flops // 2,
         aliases={2: 0},
-    )(near0, near1, extended, *(arrived[k] for k in (1, 0, 2, 3)), *listed)
+    )(near0, near1, keep_near(extended), *(arrived[k] for k in (1, 0, 2, 3)), *listed)
     swept = trade(packed, plans)
 
     tails = [piece[halo_rows:] for piece in arrived]
@@ -520,7 +525,7 @@
         [whole] * 10,
         flops=sweep_flops // 16,
         aliases={2: 0},
-    )(near0, near1, extended, *(swept[k] for k in (1, 0, 2, 3)), *listed)
+    )(near0, near1, keep_near(extended), *(swept[k] for k in (1, 0, 2, 3)), *listed)
     edges = trade(packed, plans)
 
     traces, partial, _ = call(
@@ -539,13 +544,12 @@
         sweep_flops,
         out_specs=[far, whole, whole],
         aliases={1: 2},
-    )(links, extended, *swept, couple, inverse, rhs, cell_faces)
+    )(links, keep_near(extended), *swept, couple, inverse, rhs, cell_faces)
 
     (following,) = call(
         functools.partial(cells_kernel, mesh_dims, blocks, blocks_sent),
         [like(sat)],
         [whole] * 12,
-        [pltpu.VMEM((4 * blocks_sent, lane_width), single)],
     )(partial, *(edges[k] for k in (1, 3, 0, 2)), across, cell_faces, coeff, source, flags, sat, ratio)
     saturation_next = jnp.swapaxes(following.reshape(groups, 4, lane_width), 0, 1).reshape(4, -1)
     return traces[None, None], saturation_next[None, None]

time: 23.7 us -> 23.7 us (level)
  no operation moved by 1% of the time
where the time goes in v8:
time: 23.7 us; the launch traced here: 23.5 us
  starting transfers between devices  12.1 us (51%)
  Pallas kernels  7.71 us (33%)
  waiting for transfers between devices  2.95 us (12%)
  between operations  0.74 us (3%)
    ppermute x12, starting transfers between devices, trade(): lax.ppermute(piece, axes, plan)  12.1 us
    ppermute x12, waiting for transfers between devices, trade(): lax.ppermute(piece, axes, plan)  2.95 us
    pallas_call x1, Pallas kernels, per_device(): call(functools.partial(fetch_kernel, mesh_dims, len(remote)), [like(array...  1.94 us
    pallas_call x1, Pallas kernels, per_device(): call(functools.partial(second_sweep_kernel, mesh_dims, blocks_sent), [jax...  1.65 us
    pallas_call x1, Pallas kernels, per_device(): call(functools.partial(pack_kernel, mesh_dims), [jax.ShapeDtypeStruct((ha...  1.47 us
    pallas_call x1, Pallas kernels, per_device(): call(functools.partial(cells_kernel, mesh_dims, blocks, blocks_sent), [li...  0.88 us
    pallas_call x1, Pallas kernels, per_device(): call(functools.partial(first_sweep_kernel, mesh_dims, halves), [like(exte...  0.87 us
    pallas_call x1, Pallas kernels, per_device(): call(functools.partial(first_edge_kernel, mesh_dims), [like(extended)] +...  0.49 us
  transfers between devices with their start and end apart: 12, of which 4 were waited for; matrix products, arithmetic and copies ran while one was open for 0% of the time, Pallas kernels for 19%

profile of v8, /device:TPU:5, one launch (start us, length us, event | category | flops | bytes accessed | tf_op | source)
XLA Modules:
  0.0 23.5 jit_solution(6086444337376481733)
XLA Ops:
  0.6 1.5 %shard_map.149 = (bf16[272,128]{1,0:T(8,128)(2,1)S(1)}, bf16[272,128]{1,0:T(8,128)(2,1)S(1)}, bf16[272,128]{1,0:T(8,128)(2,1)S(1)}, bf16[272,128]{1,0:T(8,128)(2...) custom-call(s32[2,4]{1,0:T(2,128)} %bitcast.48, f32[16,128,128]{2,1,0:T(8,128)} %bitcast.36, s32[8,128]{1,0:T(8,128)} %bitcast.47, ...), custom_call_target="tpu_custom_call" | custom-call | tf_op jit(solution)/shard_map/pallas_call | solution.py:447
  2.1 1.3 %collective-permute-start = (bf16[272,128]{1,0:T(8,128)(2,1)S(1)}, bf16[272,128]{1,0:T(8,128)(2,1)S(1)}, u32[]{:S(2)}, u32[]{:S(2)}) collective-permute-start(bf16[272,128]{1,0:T(8,128)(2,1)S(1)} %get-tuple-element.44), channel_id=1, source_target_pairs={{4,8},{5,9},{6,10},{7,11},{12,16},{13,17},{14,18},{15,19},{20,24},... | collective-permute-start | bytes 208904 | tf_op jit(solution)/shard_map/ppermute | solution.py:54
  3.4 0.0 collective-permute-start.1
  3.4 1.0 %collective-permute-start.2 = (bf16[272,128]{1,0:T(8,128)(2,1)S(1)}, bf16[272,128]{1,0:T(8,128)(2,1)S(1)}, u32[]{:S(2)}, u32[]{:S(2)}) collective-permute-start(bf16[272,128]{1,0:T(8,128)(2,1)S(1)} %get-tuple-element.46), channel_id=1, source_target_pairs={{0,1},{2,3},{4,5},{6,7},{8,9},{10,11},{12,13},{14,15},{16,17},{18,... | collective-permute-start | bytes 208904 | tf_op jit(solution)/shard_map/ppermute | solution.py:54
  4.4 1.1 %collective-permute-start.3 = (bf16[272,128]{1,0:T(8,128)(2,1)S(1)}, bf16[272,128]{1,0:T(8,128)(2,1)S(1)}, u32[]{:S(2)}, u32[]{:S(2)}) collective-permute-start(bf16[272,128]{1,0:T(8,128)(2,1)S(1)} %get-tuple-element.47), channel_id=1, source_target_pairs={{1,2},{5,6},{9,10},{13,14},{17,18},{21,22},{25,26},{29,30},{0,3},{... | collective-permute-start | bytes 208904 | tf_op jit(solution)/shard_map/ppermute | solution.py:54
  5.5 1.9 %shard_map.150 = (bf16[16,2,128,128]{3,2,1,0:T(8,128)(2,1)S(1)}, bf16[16,128,128]{2,1,0:T(8,128)(2,1)S(1)}, s32[96,128]{1,0:T(8,128)S(1)}, f32[96,128]{1,0:T(8,1...) custom-call(f32[16,128,128]{2,1,0:T(8,128)S(1)} %get-tuple-element.3, ...), custom_call_target="tpu_custom_call" | custom-call | bytes 1048576 | tf_op jit(solution)/shard_map/pallas_call | solution.py:488
  7.4 0.0 collective-permute-done.in1
  7.4 0.8 %collective-permute-done.1.in0 = bf16[272,128]{1,0:T(8,128)(2,1)S(1)} collective-permute-done((bf16[272,128]{1,0:T(8,128)(2,1)S(1)}, bf16[272,128]{1,0:T(8,128)(2,1)S(1)}, u32[]{:S(2)}, u32[]{:S(2)}) %collective-permute-start.1) | collective-permute-done | bytes 69664 | tf_op jit(solution)/shard_map/ppermute | solution.py:54
  8.3 0.0 collective-permute-done.2.in2
  8.3 0.2 collective-permute-done.3.in3
  8.5 0.5 %shard_map.151 = (bf16[24,128,128]{2,1,0:T(8,128)(2,1)S(1)}, bf16[256,128]{1,0:T(8,128)(2,1)S(1)}, bf16[256,128]{1,0:T(8,128)(2,1)S(1)}, bf16[256,128]{1,0:T(8,128)(2,1)S(1)}, bf16[256,128]{1,0:T(8,128)(2,1)S(1)}) custom-call(s32[2,4]{1,0:T(2,128)S(1)} %get-tuple-element.41.near0, ...), custom_call_target="tpu_custom_call", output_to_operand_aliasing={{0}: (2, {})} | custom-call | flops 100663296 | tf_op jit(solution)/shard_map/pallas_call | solution.py:503
  9.0 2.5 %collective-permute-start.4 = (bf16[256,128]{1,0:T(8,128)(2,1)S(1)}, bf16[256,128]{1,0:T(8,128)(2,1)S(1)}, u32[]{:S(2)}, u32[]{:S(2)}) collective-permute-start(bf16[256,128]{1,0:T(8,128)(2,1)S(1)} %get-tuple-element.57), channel_id=1, source_target_pairs={{4,8},{5,9},{6,10},{7,11},{12,16},{13,17},{14,18},{15,19},{20,24},... | collective-permute-start | bytes 196616 | tf_op jit(solution)/shard_map/ppermute | solution.py:54
  11.5 0.0 collective-permute-start.5
  11.5 0.3 %collective-permute-start.6 = (bf16[256,128]{1,0:T(8,128)(2,1)S(1)}, bf16[256,128]{1,0:T(8,128)(2,1)S(1)}, u32[]{:S(2)}, u32[]{:S(2)}) collective-permute-start(bf16[256,128]{1,0:T(8,128)(2,1)S(1)} %get-tuple-element.59), channel_id=1, source_target_pairs={{0,1},{2,3},{4,5},{6,7},{8,9},{10,11},{12,13},{14,15},{16,17},{18,... | collective-permute-start | bytes 196616 | tf_op jit(solution)/shard_map/ppermute | solution.py:54
  11.8 1.3 %collective-permute-start.7 = (bf16[256,128]{1,0:T(8,128)(2,1)S(1)}, bf16[256,128]{1,0:T(8,128)(2,1)S(1)}, u32[]{:S(2)}, u32[]{:S(2)}) collective-permute-start(bf16[256,128]{1,0:T(8,128)(2,1)S(1)} %get-tuple-element.60), channel_id=1, source_target_pairs={{1,2},{5,6},{9,10},{13,14},{17,18},{21,22},{25,26},{29,30},{0,3},{... | collective-permute-start | bytes 196616 | tf_op jit(solution)/shard_map/ppermute | solution.py:54
  13.1 0.0 copy-done
  13.1 0.9 %shard_map.152 = (bf16[24,128,128]{2,1,0:T(8,128)(2,1)S(1)}, f32[96,128]{1,0:T(8,128)S(1)}) custom-call(s32[2,16]{1,0:T(2,128)S(1)} %get-tuple-element.40.links, bf16[24,128,128]{2,1,0:T(8,128)(2,1)S(1)} %get-tuple-element.51.extended, bf16[16,2,128,128]{3,2,1,0:T(8,128)(2,1)S(1)} %get-tuple-element.52.couple, ...), custom_call_target="tpu_custom_call" | custom-call | flops 201326592 | tf_op jit(solution)/shard_map/pallas_call | solution.py:514
  14.0 0.0 collective-permute-done.4.in1
  14.0 1.5 %collective-permute-done.5.in0 = bf16[256,128]{1,0:T(8,128)(2,1)S(1)} collective-permute-done((bf16[256,128]{1,0:T(8,128)(2,1)S(1)}, bf16[256,128]{1,0:T(8,128)(2,1)S(1)}, u32[]{:S(2)}, u32[]{:S(2)}) %collective-permute-start.5) | collective-permute-done | bytes 65568 | tf_op jit(solution)/shard_map/ppermute | solution.py:54
  15.5 0.0 collective-permute-done.6.in2
  15.5 0.4 %collective-permute-done.7.in3 = bf16[256,128]{1,0:T(8,128)(2,1)S(1)} collective-permute-done((bf16[256,128]{1,0:T(8,128)(2,1)S(1)}, bf16[256,128]{1,0:T(8,128)(2,1)S(1)}, u32[]{:S(2)}, u32[]{:S(2)}) %collective-permute-start.7) | collective-permute-done | bytes 65568 | tf_op jit(solution)/shard_map/ppermute | solution.py:54
  15.9 0.4 %shard_map.153 = (bf16[24,128,128]{2,1,0:T(8,128)(2,1)S(1)}, bf16[16,128]{1,0:T(8,128)(2,1)S(1)}, bf16[16,128]{1,0:T(8,128)(2,1)S(1)}, bf16[16,128]{1,0:T(8,128)(2,1)S(1)}, bf16[16,128]{1,0:T(8,128)(2,1)S(1)}) custom-call(s32[2,4]{1,0:T(2,128)S(1)} %get-tuple-element.41.near0, s32[2,4]{1,0:T(2,128)S(1)} %get-tuple-element.42.near1, ...), custom_call_target="tpu_custom_call", output_to_operand_aliasing={{0}: (2, {})} | custom-call | flops 12582912 | tf_op jit(solution)/shard_map/pallas_call | solution.py:522
  16.3 1.4 %collective-permute-start.10 = (bf16[16,128]{1,0:T(8,128)(2,1)S(1)}, bf16[16,128]{1,0:T(8,128)(2,1)S(1)}, u32[]{:S(2)}, u32[]{:S(2)}) collective-permute-start(bf16[16,128]{1,0:T(8,128)(2,1)S(1)} %get-tuple-element.67), channel_id=1, source_target_pairs={{0,4},{1,5},{2,6},{3,7},{8,12},{9,13},{10,14},{11,15},{16,20},{17,... | collective-permute-start | bytes 12296 | tf_op jit(solution)/shard_map/ppermute | solution.py:54
  17.7 0.3 %collective-permute-start.11 = (bf16[16,128]{1,0:T(8,128)(2,1)S(1)}, bf16[16,128]{1,0:T(8,128)(2,1)S(1)}, u32[]{:S(2)}, u32[]{:S(2)}) collective-permute-start(bf16[16,128]{1,0:T(8,128)(2,1)S(1)} %get-tuple-element.68), channel_id=1, source_target_pairs={{0,1},{2,3},{4,5},{6,7},{8,9},{10,11},{12,13},{14,15},{16,17},{18,... | collective-permute-start | bytes 12296 | tf_op jit(solution)/shard_map/ppermute | solution.py:54
  18.1 1.5 %collective-permute-start.8 = (bf16[16,128]{1,0:T(8,128)(2,1)S(1)}, bf16[16,128]{1,0:T(8,128)(2,1)S(1)}, u32[]{:S(2)}, u32[]{:S(2)}) collective-permute-start(bf16[16,128]{1,0:T(8,128)(2,1)S(1)} %get-tuple-element.65), channel_id=1, source_target_pairs={{4,8},{5,9},{6,10},{7,11},{12,16},{13,17},{14,18},{15,19},{20,24},... | collective-permute-start | bytes 12296 | tf_op jit(solution)/shard_map/ppermute | solution.py:54
  19.6 1.4 %collective-permute-start.9 = (bf16[16,128]{1,0:T(8,128)(2,1)S(1)}, bf16[16,128]{1,0:T(8,128)(2,1)S(1)}, u32[]{:S(2)}, u32[]{:S(2)}) collective-permute-start(bf16[16,128]{1,0:T(8,128)(2,1)S(1)} %get-tuple-element.66), channel_id=1, source_target_pairs={{1,2},{5,6},{9,10},{13,14},{17,18},{21,22},{25,26},{29,30},{0,3},{... | collective-permute-start | bytes 12296 | tf_op jit(solution)/shard_map/ppermute | solution.py:54
  20.9 1.6 %shard_map.154 = (f32[16,128,128]{2,1,0:T(8,128)}, f32[96,128]{1,0:T(8,128)S(1)}, bf16[24,128,128]{2,1,0:T(8,128)(2,1)S(1)}) custom-call(s32[2,16]{1,0:T(2,128)S(1)} %get-tuple-element.40.links, bf16[24,128,128]{2,1,0:T(8,128)(2,1)S(1)} %get-tuple-element.61._, bf16[256,128]{1,0:T(8,128)(2,1)S(1)} %collective-permute-done.5.in0, ...), custom_call_target="tpu_custom_call", output_to_operand_aliasing={{2}: (1, {})} | custom-call | flops 201326592 | tf_op jit(solution)/shard_map/pallas_call | solution.py:531
  22.6 0.0 collective-permute-done.10.in0
  22.6 0.0 collective-permute-done.11.in2
  22.6 0.0 collective-permute-done.8.in1
  22.6 0.0 collective-permute-done.9.in3
  22.6 0.9 %shard_map.155 = f32[64,128]{1,0:T(8,128)} custom-call(f32[96,128]{1,0:T(8,128)S(1)} %get-tuple-element.64.partial, bf16[16,128]{1,0:T(8,128)(2,1)S(1)} %collective-permute-done.8.in1, bf16[16,128]{1,0:T(8,128)(2,1)S(1)} %collective-permute-done.9.in3, bf16[16,128]{1,0:T(8,128)(2,1)S(1)} %collective-permute-done.10.in0, ...), custom_call_target="tpu_custom_call" | custom-call | tf_op jit(solution)/shard_map/pallas_call | solution.py:549
  (5 shorter events, 0.0 us)
Async XLA Ops:
  2.1 5.3 %collective-permute-start = (bf16[272,128]{1,0:T(8,128)(2,1)S(1)}, bf16[272,128]{1,0:T(8,128)(2,1)S(1)}, u32[]{:S(2)}, u32[]{:S(2)}) collective-permute-start(bf16[272,128]{1,0:T(8,128)(2,1)S(1)} %get-tuple-element.44), channel_id=1, source_target_pairs={{4,8},{5,9},{6,10},{7,11},{12,16},{13,17},{14,18},{15,19},{20,24},... | collective-permute-start | bytes 208904 | tf_op jit(solution)/shard_map/ppermute | solution.py:54
  3.4 4.9 %collective-permute-start.1 = (bf16[272,128]{1,0:T(8,128)(2,1)S(1)}, bf16[272,128]{1,0:T(8,128)(2,1)S(1)}, u32[]{:S(2)}, u32[]{:S(2)}) collective-permute-start(bf16[272,128]{1,0:T(8,128)(2,1)S(1)} %get-tuple-element.45), channel_id=1, source_target_pairs={{0,4},{1,5},{2,6},{3,7},{8,12},{9,13},{10,14},{11,15},{16,20},{17,... | collective-permute-start | bytes 208904 | tf_op jit(solution)/shard_map/ppermute | solution.py:54
  3.4 4.9 %collective-permute-start.2 = (bf16[272,128]{1,0:T(8,128)(2,1)S(1)}, bf16[272,128]{1,0:T(8,128)(2,1)S(1)}, u32[]{:S(2)}, u32[]{:S(2)}) collective-permute-start(bf16[272,128]{1,0:T(8,128)(2,1)S(1)} %get-tuple-element.46), channel_id=1, source_target_pairs={{0,1},{2,3},{4,5},{6,7},{8,9},{10,11},{12,13},{14,15},{16,17},{18,... | collective-permute-start | bytes 208904 | tf_op jit(solution)/shard_map/ppermute | solution.py:54
  4.4 4.1 %collective-permute-start.3 = (bf16[272,128]{1,0:T(8,128)(2,1)S(1)}, bf16[272,128]{1,0:T(8,128)(2,1)S(1)}, u32[]{:S(2)}, u32[]{:S(2)}) collective-permute-start(bf16[272,128]{1,0:T(8,128)(2,1)S(1)} %get-tuple-element.47), channel_id=1, source_target_pairs={{1,2},{5,6},{9,10},{13,14},{17,18},{21,22},{25,26},{29,30},{0,3},{... | collective-permute-start | bytes 208904 | tf_op jit(solution)/shard_map/ppermute | solution.py:54
  8.5 4.7 %copy-start = (f32[1,1,16,128,128]{4,3,2,1,0:T(8,128)S(1)}, f32[1,1,16,128,128]{4,3,2,1,0:T(8,128)}, u32[]{:S(2)}) copy-start(f32[1,1,16,128,128]{4,3,2,1,0:T(8,128)} %param.15) | copy-start | bytes 3145732
  9.0 5.0 %collective-permute-start.4 = (bf16[256,128]{1,0:T(8,128)(2,1)S(1)}, bf16[256,128]{1,0:T(8,128)(2,1)S(1)}, u32[]{:S(2)}, u32[]{:S(2)}) collective-permute-start(bf16[256,128]{1,0:T(8,128)(2,1)S(1)} %get-tuple-element.57), channel_id=1, source_target_pairs={{4,8},{5,9},{6,10},{7,11},{12,16},{13,17},{14,18},{15,19},{20,24},... | collective-permute-start | bytes 196616 | tf_op jit(solution)/shard_map/ppermute | solution.py:54
  11.5 4.0 %collective-permute-start.5 = (bf16[256,128]{1,0:T(8,128)(2,1)S(1)}, bf16[256,128]{1,0:T(8,128)(2,1)S(1)}, u32[]{:S(2)}, u32[]{:S(2)}) collective-permute-start(bf16[256,128]{1,0:T(8,128)(2,1)S(1)} %get-tuple-element.58), channel_id=1, source_target_pairs={{0,4},{1,5},{2,6},{3,7},{8,12},{9,13},{10,14},{11,15},{16,20},{17,... | collective-permute-start | bytes 196616 | tf_op jit(solution)/shard_map/ppermute | solution.py:54
  11.5 4.0 %collective-permute-start.6 = (bf16[256,128]{1,0:T(8,128)(2,1)S(1)}, bf16[256,128]{1,0:T(8,128)(2,1)S(1)}, u32[]{:S(2)}, u32[]{:S(2)}) collective-permute-start(bf16[256,128]{1,0:T(8,128)(2,1)S(1)} %get-tuple-element.59), channel_id=1, source_target_pairs={{0,1},{2,3},{4,5},{6,7},{8,9},{10,11},{12,13},{14,15},{16,17},{18,... | collective-permute-start | bytes 196616 | tf_op jit(solution)/shard_map/ppermute | solution.py:54
  11.8 4.1 %collective-permute-start.7 = (bf16[256,128]{1,0:T(8,128)(2,1)S(1)}, bf16[256,128]{1,0:T(8,128)(2,1)S(1)}, u32[]{:S(2)}, u32[]{:S(2)}) collective-permute-start(bf16[256,128]{1,0:T(8,128)(2,1)S(1)} %get-tuple-element.60), channel_id=1, source_target_pairs={{1,2},{5,6},{9,10},{13,14},{17,18},{21,22},{25,26},{29,30},{0,3},{... | collective-permute-start | bytes 196616 | tf_op jit(solution)/shard_map/ppermute | solution.py:54
  16.3 6.3 %collective-permute-start.10 = (bf16[16,128]{1,0:T(8,128)(2,1)S(1)}, bf16[16,128]{1,0:T(8,128)(2,1)S(1)}, u32[]{:S(2)}, u32[]{:S(2)}) collective-permute-start(bf16[16,128]{1,0:T(8,128)(2,1)S(1)} %get-tuple-element.67), channel_id=1, source_target_pairs={{0,4},{1,5},{2,6},{3,7},{8,12},{9,13},{10,14},{11,15},{16,20},{17,... | collective-permute-start | bytes 12296 | tf_op jit(solution)/shard_map/ppermute | solution.py:54
  17.7 4.9 %collective-permute-start.11 = (bf16[16,128]{1,0:T(8,128)(2,1)S(1)}, bf16[16,128]{1,0:T(8,128)(2,1)S(1)}, u32[]{:S(2)}, u32[]{:S(2)}) collective-permute-start(bf16[16,128]{1,0:T(8,128)(2,1)S(1)} %get-tuple-element.68), channel_id=1, source_target_pairs={{0,1},{2,3},{4,5},{6,7},{8,9},{10,11},{12,13},{14,15},{16,17},{18,... | collective-permute-start | bytes 12296 | tf_op jit(solution)/shard_map/ppermute | solution.py:54
  18.1 4.5 %collective-permute-start.8 = (bf16[16,128]{1,0:T(8,128)(2,1)S(1)}, bf16[16,128]{1,0:T(8,128)(2,1)S(1)}, u32[]{:S(2)}, u32[]{:S(2)}) collective-permute-start(bf16[16,128]{1,0:T(8,128)(2,1)S(1)} %get-tuple-element.65), channel_id=1, source_target_pairs={{4,8},{5,9},{6,10},{7,11},{12,16},{13,17},{14,18},{15,19},{20,24},... | collective-permute-start | bytes 12296 | tf_op jit(solution)/shard_map/ppermute | solution.py:54
  19.6 3.1 %collective-permute-start.9 = (bf16[16,128]{1,0:T(8,128)(2,1)S(1)}, bf16[16,128]{1,0:T(8,128)(2,1)S(1)}, u32[]{:S(2)}, u32[]{:S(2)}) collective-permute-start(bf16[16,128]{1,0:T(8,128)(2,1)S(1)} %get-tuple-element.66), channel_id=1, source_target_pairs={{1,2},{5,6},{9,10},{13,14},{17,18},{21,22},{25,26},{29,30},{0,3},{... | collective-permute-start | bytes 12296 | tf_op jit(solution)/shard_map/ppermute | solution.py:54
